TPU v7x, 256 devices: a whole 4x4x8 slice. The times are simulated.
256 devices in a mesh: dp: 16 (over y_lo, x, core), task: 16 (over z, y_hi).
Axes of the slice: x: 4, y: 4 (y_hi: 2, y_lo: 2; y = y_hi * 2 + y_lo), z: 8, core: 2. Of those that a mesh axis runs over, the one named last changes fastest.
Arguments:
- features: bfloat16 [4096, 8, 512], P(('dp', 'task')), may hold values from -6 to 6
- task_embed: bfloat16 [8192, 512], P('task'), may hold values from -0.25 to 0.25
- bin_bias: float32 [8192, 8], P('task'), may hold values from -2 to 0.5
- bin_bounds: int32 [9], replicated, may hold values from 0 to 640, as said below
- event_time: int32 [4096, 8192], P('dp', 'task'), may hold values from 1 to 639
- censored: int32 [4096, 8192], P('dp', 'task'), may hold values 0 or 1
- at_risk: int32 [32, 64], P('dp', 'task'), may hold values from 0 to 1
Outputs:
- grad_features: bfloat16 [4096, 8, 512], P(('dp', 'task'))
- grad_embed: float32 [8192, 512], P(('task', 'dp'))
- grad_bias: float32 [8192, 8], P(('task', 'dp'))
Inputs may be any that keep to these rules, and one draw needn't show every extreme that they name: bin_bounds[0] is 0, bin_bounds[8] is 640, and the bounds rise strictly.
All inputs are finite; a program needn't handle non-finite values. No bound on the sum of `censored` on one device may be relied on, other than what follows from the above.
Results may differ from a plain program's by a relative error of at most 0.0045.
Values may be sent and summed in bfloat16 or wider, within the bound.
No kernel may reach another device: no remote copies, remote signals or barrier semaphores. Data moves between devices by JAX's collectives and lax.ppermute only.
A program may use at most 64 MiB of HBM per device.

v0:
```python
import jax
import jax.numpy as jnp
from jax import lax
from jax.sharding import PartitionSpec as P

time_unit = 0.015625


def per_device(features, task_embed, bin_bias, bin_bounds, event_time, censored, at_risk):
    gathered = lax.all_gather(features, "task", axis=0, tiled=True)
    tok_count, bins, width_e = gathered.shape
    tile = tok_count // at_risk.shape[0]
    local_tasks = task_embed.shape[0]
    blocks = local_tasks // tile
    lower = bin_bounds[:-1]
    spans = bin_bounds[1:] - lower
    risk_rows = jnp.repeat(at_risk, tile, axis=0)
    tokens_all = tok_count * lax.axis_size("dp")

    def block_terms(index):
        start = index * tile
        emb = lax.dynamic_slice_in_dim(task_embed, start, tile, 0)
        bias = lax.dynamic_slice_in_dim(bin_bias, start, tile, 0)
        times = lax.dynamic_slice_in_dim(event_time, start, tile, 1)
        cens = lax.dynamic_slice_in_dim(censored, start, tile, 1)
        risk = lax.dynamic_slice_in_dim(risk_rows, index, 1, 1)
        logit = (
            jnp.einsum("tbd,kd->tbk", gathered, emb, preferred_element_type=jnp.float32)
            + bias.T[None, :, :]
        )
        moment = times[:, None, :]
        exposure = (
            jnp.clip(moment - lower[None, :, None], 0, spans[None, :, None]).astype(jnp.float32)
            * time_unit
        )
        inside = (
            (moment > lower[None, :, None])
            & (moment <= (lower + spans)[None, :, None])
            & (cens[:, None, :] == 0)
        )
        dlogit = risk[:, :, None].astype(jnp.float32) * (
            exposure * jnp.exp(logit) - inside.astype(jnp.float32)
        )
        return (start, emb, dlogit)

    def common_parts(start, dlogit, low, grad_emb, grad_bin):
        part_emb = jnp.einsum("tbk,tbd->kd", low, gathered, preferred_element_type=jnp.float32)
        grad_emb = lax.dynamic_update_slice_in_dim(grad_emb, part_emb, start, 0)
        grad_bin = lax.dynamic_update_slice_in_dim(grad_bin, jnp.sum(dlogit, axis=0).T, start, 0)
        return (grad_emb, grad_bin)

    empty_emb = jnp.zeros((local_tasks, width_e), jnp.float32)
    empty_bin = jnp.zeros((local_tasks, bins), jnp.float32)

    def step(index, carry):
        grad_rows, grad_emb, grad_bin = carry
        start, emb, dlogit = block_terms(index)
        low = dlogit.astype(jnp.bfloat16)
        grad_rows = grad_rows + jnp.einsum(
            "tbk,kd->tbd", low, emb, preferred_element_type=jnp.float32
        )
        grad_emb, grad_bin = common_parts(start, dlogit, low, grad_emb, grad_bin)
        return (grad_rows, grad_emb, grad_bin)

    init = (jnp.zeros((tok_count, bins, width_e), jnp.float32), empty_emb, empty_bin)
    grad_rows, grad_emb, grad_bin = lax.fori_loop(0, blocks, step, init)
    summed_emb, summed_bin = (
        lax.psum_scatter(grad_emb, "dp", scatter_dimension=0, tiled=True),
        lax.psum_scatter(grad_bin, "dp", scatter_dimension=0, tiled=True),
    )
    feature_part = lax.psum_scatter(grad_rows, "task", scatter_dimension=0, tiled=True)
    emb_scale = (tokens_all * bins) ** (-0.5)
    return (
        feature_part.astype(jnp.bfloat16),
        summed_emb * emb_scale,
        summed_bin * (1.0 / tokens_all),
    )


def solution(mesh):
    return jax.shard_map(
        per_device,
        mesh=mesh,
        in_specs=(
            P(("dp", "task"), None, None),
            P("task", None),
            P("task", None),
            P(),
            P("dp", "task"),
            P("dp", "task"),
            P("dp", "task"),
        ),
        out_specs=(P(("dp", "task"), None, None), P(("task", "dp"), None), P(("task", "dp"), None)),
        check_vma=False,
    )
```

profile of v0, /device:TPU:32, one launch (start us, length us, event | category | flops | bytes accessed | tf_op | source)
XLA Modules:
  0.0 491.1 jit_solution(7995530972654144729)
XLA Ops:
  7.2 0.0 all-gather.2.cloned.1.call-start
  7.2 1.6 copy.18
  8.8 0.0 all-gather.2.cloned.1.call-update
  8.8 0.0 reduce-scatter.10.cloned.1.call-start
  8.9 0.8 copy.17
  9.7 0.1 broadcast_bitcast_fusion
  9.7 1.4 slice_bitcast_fusion
  11.1 87.7 %all-gather.2.cloned.1.call-done = bf16[256,8,512]{2,0,1:T(8,128)(2,1)} async-done(((bf16[16,8,512]{2,0,1:T(8,128)(2,1)}), bf16[256,8,512]{2,0,1:T(8,128)(2,1)}) %all-gather.2.cloned.1.call-update) | async-done | bytes 2097168 | tf_op jit(solution)/shard_map/all_gather | solution.py:10
  98.8 0.6 broadcast_in_dim.36
  99.4 0.1 broadcast_in_dim.35
  99.5 42.8 %while.19 = (s32[]{:T(128)}, f32[256,8,512]{2,0,1:T(8,128)}, f32[512,512]{1,0:T(8,128)S(1)}, f32[512,8]{0,1:T(8,128)}, s32[256,4]{0,1:T(4,128)S(1)}, /*index=5*/...) while((s32[]{:T(128)}, f32[256,8,512]{2,0,1:T(8,128)}, ...), condition=%wide.region_2.3_spmd.clone, body=%wide.region_0.2_spmd.clone.sunk | while | flops 811629824 | bytes 58028392 | solution.py:66
  99.6 0.8 dynamic-slice_bitcast_fusion.2
  100.4 1.0 constant_dynamic-slice_fusion.4
  101.4 0.1 copy.32
  101.5 0.6 broadcast_compare_fusion.2
  102.2 0.1 copy.33
  102.3 2.9 fusion.34
  105.1 0.6 bitcast_dynamic-update-slice_fusion.2
  105.7 0.4 fusion.35
  106.2 2.1 select_add_fusion.2
  108.3 2.0 copy-done.1
  110.3 0.8 dynamic-slice_bitcast_fusion.2
  111.1 1.0 constant_dynamic-slice_fusion.4
  112.1 0.1 copy.32
  112.2 0.6 broadcast_compare_fusion.2
  112.8 0.1 copy.33
  113.0 2.9 fusion.34
  115.8 0.6 bitcast_dynamic-update-slice_fusion.2
  116.4 0.4 fusion.35
  116.9 2.1 select_add_fusion.2
  119.0 2.0 copy-done.1
  121.0 0.8 dynamic-slice_bitcast_fusion.2
  121.8 1.0 constant_dynamic-slice_fusion.4
  122.8 0.1 copy.32
  122.9 0.6 broadcast_compare_fusion.2
  123.5 0.1 copy.33
  123.6 2.9 fusion.34
  126.5 0.6 bitcast_dynamic-update-slice_fusion.2
  127.1 0.4 fusion.35
  127.6 2.1 select_add_fusion.2
  129.7 2.0 copy-done.1
  131.6 0.8 dynamic-slice_bitcast_fusion.2
  132.5 1.0 constant_dynamic-slice_fusion.4
  133.5 0.1 copy.32
  133.6 0.6 broadcast_compare_fusion.2
  134.2 0.1 copy.33
  134.3 2.9 fusion.34
  137.2 0.6 bitcast_dynamic-update-slice_fusion.2
  137.8 0.4 fusion.35
  138.2 2.1 select_add_fusion.2
  140.4 2.0 copy-done.1
  142.3 1.5 copy.23
  143.9 0.0 reduce-scatter.10.cloned.1.call-update
  143.9 0.0 reduce-scatter.8.cloned.1.call-start
  144.0 0.7 reduce-scatter.8.cloned.1.call-update
  144.6 0.0 reduce-scatter.6.cloned.1.call-start
  144.7 6.6 %copy.21 = f32[256,8,512]{2,1,0:T(8,128)} copy(f32[256,8,512]{2,0,1:T(8,128)} %get-tuple-element.258) | data formatting | bytes 8388608 | tf_op jit(solution)/shard_map/while | solution.py:66
  151.3 52.7 %reduce-scatter.10.cloned.1.call-done = f32[32,8]{1,0:T(8,128)} async-done(((f32[512,8]{1,0:T(8,128)}), f32[32,8]{1,0:T(8,128)}) %reduce-scatter.10.cloned.1.call-update) | async-done | bytes 1040
  203.9 0.8 copy.24
  204.7 0.6 broadcast_multiply_fusion.1
  205.3 63.7 %reduce-scatter.8.cloned.1.call-done = f32[32,512]{1,0:T(8,128)} async-done(((f32[512,512]{1,0:T(8,128)}), f32[32,512]{1,0:T(8,128)}) %reduce-scatter.8.cloned.1.call-update) | async-done | bytes 65552 | tf_op jit(solution)/shard_map/reduce_scatter | solution.py:68
  269.0 1.5 broadcast_multiply_fusion
  270.5 212.4 %reduce-scatter.6.cloned.1.call-done = f32[16,8,512]{2,1,0:T(8,128)} async-done(((f32[256,8,512]{2,1,0:T(8,128)}), f32[16,8,512]{2,1,0:T(8,128)}) %reduce-scatter.6.cloned.1.call-update) | async-done | bytes 262160 | tf_op jit(solution)/shard_map/reduce_scatter | solution.py:71
  482.9 1.6 convert_element_type.43
  (29 shorter events, 0.1 us)
Async XLA Ops:
  7.2 91.6 %all-gather.2.cloned.1.call-start = ((), (), s32[]{:S(2)}) async-start(), calls=%async_computation.3 | async-start | bytes 2228224 | tf_op jit(solution)/shard_map/all_gather | solution.py:10
  8.8 195.1 %reduce-scatter.10.cloned.1.call-start = ((), (), s32[]{:S(2)}) async-start(), calls=%async_computation.6 | async-start | bytes 278528
  99.5 6.2 %copy-start.2 = (bf16[256,8,512]{2,0,1:T(8,128)(2,1)S(1)}, bf16[256,8,512]{2,0,1:T(8,128)(2,1)}, u32[]{:S(2)}) copy-start(bf16[256,8,512]{2,0,1:T(8,128)(2,1)} %get-tuple-element.494) | copy-start | bytes 6291460 | tf_op jit(solution)/shard_map/while
  102.3 3.9 copy-start
  108.3 2.0 copy-start.1
  110.3 6.2 %copy-start.2 = (bf16[256,8,512]{2,0,1:T(8,128)(2,1)S(1)}, bf16[256,8,512]{2,0,1:T(8,128)(2,1)}, u32[]{:S(2)}) copy-start(bf16[256,8,512]{2,0,1:T(8,128)(2,1)} %get-tuple-element.494) | copy-start | bytes 6291460 | tf_op jit(solution)/shard_map/while
  112.9 3.9 copy-start
  119.0 2.0 copy-start.1
  121.0 6.2 %copy-start.2 = (bf16[256,8,512]{2,0,1:T(8,128)(2,1)S(1)}, bf16[256,8,512]{2,0,1:T(8,128)(2,1)}, u32[]{:S(2)}) copy-start(bf16[256,8,512]{2,0,1:T(8,128)(2,1)} %get-tuple-element.494) | copy-start | bytes 6291460 | tf_op jit(solution)/shard_map/while
  123.6 3.9 copy-start
  129.7 2.0 copy-start.1
  131.6 6.2 %copy-start.2 = (bf16[256,8,512]{2,0,1:T(8,128)(2,1)S(1)}, bf16[256,8,512]{2,0,1:T(8,128)(2,1)}, u32[]{:S(2)}) copy-start(bf16[256,8,512]{2,0,1:T(8,128)(2,1)} %get-tuple-element.494) | copy-start | bytes 6291460 | tf_op jit(solution)/shard_map/while
  134.3 3.9 copy-start
  140.3 2.0 copy-start.1
  142.3 1.6 copy-start.3
  143.9 125.1 %reduce-scatter.8.cloned.1.call-start = ((), (), s32[]{:S(2)}) async-start(), calls=%async_computation.5 | async-start | bytes 1114112 | tf_op jit(solution)/shard_map/reduce_scatter | solution.py:68
  144.6 338.3 %reduce-scatter.6.cloned.1.call-start = ((), (), s32[]{:S(2)}) async-start(), calls=%async_computation.4 | async-start | bytes 4456448 | tf_op jit(solution)/shard_map/reduce_scatter | solution.py:71
Sparse Core Ops, SparseCore 0:
  11.2 87.5 all-gather.1
  144.0 59.8 reduce-scatter.9
  206.6 62.3 reduce-scatter.7
  272.9 210.0 reduce-scatter.5
where the time goes:
time: 493 us; the launch traced here: 491 us
  waiting for transfers between devices  417 us (85%)
  local copies, waits for them, and re-layouts  30.4 us (6%)
  matrix products  21.5 us (4%)
  between operations  13.8 us (3%)
  other arithmetic  7.64 us (2%)
    reduce_scatter x1, waiting for transfers between devices, per_device(): lax.psum_scatter(grad_rows, 'task', scatter_dimension=0, tiled=True)  212 us
    all_gather x1, waiting for transfers between devices, per_device(): gathered = lax.all_gather(features, 'task', axis=0, tiled=True)  87.7 us
    reduce_scatter x1, waiting for transfers between devices, per_device(): lax.psum_scatter(grad_emb, 'dp', scatter_dimension=0, tiled=True)  63.7 us
    unnamed x5, waiting for transfers between devices  53.4 us
    dot_general x4, matrix products, block_terms(): jnp.einsum('tbd,kd->tbk', gathered, emb, preferred_element_type=jnp.float32)  11.4 us
  transfers between devices with their start and end apart: 4, of which 4 were waited for; matrix products, arithmetic and copies ran while one was open for 2% of the time, Pallas kernels for 0%

commit v1 on v0

v1 whole, which is shorter than its diff:
```python
import functools

import jax
import jax.numpy as jnp
from jax import lax
from jax.experimental import pallas as pl
from jax.experimental.pallas import tpu as pltpu
from jax.sharding import PartitionSpec as P

time_unit = 0.015625

NZ = 8
NDP = 16
BLOCK = 256


def z_shift(step):
    return [(z * 2 + h, ((z + step) % NZ) * 2 + h) for z in range(NZ) for h in range(2)]


def swap_low_bit(count):
    return [(i, i ^ 1) for i in range(count)]


def plane_groups():
    return [
        [
            ((low * 4 + x) * 2 + core) * 16 + z * 2 + h
            for h in range(2)
            for low in range(2)
            for x in range(4)
        ]
        for core in range(2)
        for z in range(NZ)
    ]


def pack_kernel(where_ref, risk_ref, time_ref, cens_ref, own_ref, other_ref):
    h = where_ref[2]
    for z in range(NZ):
        row = z // (NZ // 2)
        for side, out in ((h, own_ref), (1 - h, other_ref)):
            start = pl.multiple_of(z * 32 + side * 16, 16)
            times = time_ref[pl.ds(start, 16), :]
            signed = jnp.where(cens_ref[pl.ds(start, 16), :] == 0, times, -times)
            for k in range(4):
                cols = slice(k * 128, (k + 1) * 128)
                out[z * 16 : (z + 1) * 16, cols] = signed[:, cols] * risk_ref[row, k]


def pack_events(where, at_risk, event_time, censored):
    smem = pl.BlockSpec(memory_space=pltpu.SMEM)
    vmem = pl.BlockSpec(memory_space=pltpu.VMEM)
    half = jax.ShapeDtypeStruct((128, 512), jnp.int32)
    return pl.pallas_call(
        pack_kernel,
        out_shape=(half, half),
        in_specs=[smem, smem, vmem, vmem],
        out_specs=(vmem, vmem),
        name="pack_events",
    )(where, at_risk, event_time, censored)


SLOTS = (0, 1, -1, 2, -2, 3, -3, 4)


def main_kernel(
    where_ref,
    bounds_ref,
    f0, f1, f2, f3, f4, f5, f6, f7a, f7b,
    e0_ref, e1_ref, b0_ref, b1_ref, p0_ref, p1_ref,
    own_ref, r1, r2, r3, r4, r5, r6, r7,
    keep_ref, send_ref,
    feats, acc,
):
    step = pl.program_id(0)
    z, core, h = where_ref[0], where_ref[1], where_ref[2]

    @pl.when(step == 0)
    def _():
        for slot, ref in enumerate((f0, f1, f2, f3, f4, f5, f6)):
            feats[slot * 128 : (slot + 1) * 128, :] = ref[...]
        feats[896:960, :] = f7a[...]
        feats[960:1024, :] = f7b[...]
        acc[...] = jnp.zeros_like(acc)

    first = step < 2
    emb = jnp.where(first, e0_ref[...], e1_ref[...])
    bias = jnp.where(first, b0_ref[...], b1_ref[...])
    bins = lax.broadcasted_iota(jnp.int32, (8, BLOCK), 0)
    lower = jnp.zeros((8, BLOCK), jnp.float32)
    upper = jnp.zeros((8, BLOCK), jnp.float32)
    for b in range(8):
        lower = jnp.where(bins == b, bounds_ref[b].astype(jnp.float32) * time_unit, lower)
        upper = jnp.where(bins == b, bounds_ref[b + 1].astype(jnp.float32) * time_unit, upper)
    span = upper - lower

    g_emb = jnp.zeros((BLOCK, 512), jnp.float32)
    g_bin = jnp.zeros((8, BLOCK), jnp.float32)
    for part in range(4):
        rows = slice(part * 256, (part + 1) * 256)
        block = feats[rows, :]
        logit = lax.dot_general(
            block, emb, (((1,), (1,)), ((), ())), preferred_element_type=jnp.float32
        )
        lows = []
        for slot in (2 * part, 2 * part + 1):
            owner = lax.rem(z + (NZ - SLOTS[slot]), NZ)
            tok = pl.ds(pl.multiple_of(owner * 16, 16), 16)
            signed = jnp.where(first, p0_ref[tok, :], p1_ref[tok, :])
            signed = signed.astype(jnp.float32) * time_unit
            moment = jnp.abs(signed)
            at = (slot % 2) * 128
            piece = logit[at : at + 128].reshape(16, 8, BLOCK) + bias[None]
            exposure = jnp.clip(moment[:, None, :] - lower[None], 0.0, span[None])
            inside = (signed[:, None, :] > lower[None]) & (signed[:, None, :] <= upper[None])
            dlogit = exposure * jnp.exp(piece) - inside.astype(jnp.float32)
            g_bin = g_bin + jnp.sum(dlogit, axis=0)
            lows.append(dlogit.reshape(128, BLOCK).astype(jnp.bfloat16))
        low = jnp.concatenate(lows, axis=0)
        acc[rows, :] += jnp.dot(low, emb, preferred_element_type=jnp.float32)
        g_emb = g_emb + lax.dot_general(
            low, block, (((0,), (0,)), ((), ())), preferred_element_type=jnp.float32
        )

    h_abs = jnp.where(first, h, 1 - h)
    half = lax.rem(step, 2)
    split = g_emb.reshape(4, 2, 32, 512)
    zero, one = split[:, 0].reshape(128, 512), split[:, 1].reshape(128, 512)
    spot = pl.ds(pl.multiple_of((h_abs * 2 + half) * 128, 128), 128)
    keep_ref[spot, :] = jnp.where(core == 0, zero, one)
    send_ref[spot, :] = jnp.where(core == 0, one, zero)
    brow = pl.ds(pl.multiple_of(512 + h_abs * 8, 8), 8)
    bcol = pl.ds(pl.multiple_of(half * BLOCK, BLOCK), BLOCK)
    keep_ref[brow, bcol] = g_bin
    send_ref[brow, bcol] = g_bin

    @pl.when(step == 3)
    def _():
        own_ref[...] = acc[0:128, :]
        for slot, ref in enumerate((r1, r2, r3, r4, r5, r6, r7), 1):
            ref[...] = acc[slot * 128 : (slot + 1) * 128, :].astype(jnp.bfloat16)


def main_call(where, bounds, feats, embs, biases, events):
    def whole(rows):
        return pl.BlockSpec((rows, 512), lambda i, w, b: (0, 0))

    def early(i):
        return jnp.minimum(i, 1)

    def late(i):
        return jnp.maximum(i - 2, 0)

    in_specs = [whole(128)] * 7 + [whole(64)] * 2
    in_specs += [
        pl.BlockSpec((BLOCK, 512), lambda i, w, b: (early(i), 0)),
        pl.BlockSpec((BLOCK, 512), lambda i, w, b: (late(i), 0)),
        pl.BlockSpec((8, BLOCK), lambda i, w, b: (0, early(i))),
        pl.BlockSpec((8, BLOCK), lambda i, w, b: (0, late(i))),
        pl.BlockSpec((128, BLOCK), lambda i, w, b: (0, early(i))),
        pl.BlockSpec((128, BLOCK), lambda i, w, b: (0, late(i))),
    ]
    back = jax.ShapeDtypeStruct((128, 512), jnp.bfloat16)
    wide = jax.ShapeDtypeStruct((528, 512), jnp.float32)
    return pl.pallas_call(
        main_kernel,
        out_shape=(jax.ShapeDtypeStruct((128, 512), jnp.float32),) + (back,) * 7 + (wide, wide),
        grid_spec=pltpu.PrefetchScalarGridSpec(
            num_scalar_prefetch=2,
            grid=(4,),
            in_specs=in_specs,
            out_specs=[whole(128)] * 8 + [whole(528)] * 2,
            scratch_shapes=[
                pltpu.VMEM((1024, 512), jnp.bfloat16),
                pltpu.VMEM((1024, 512), jnp.float32),
            ],
        ),
        compiler_params=pltpu.CompilerParams(vmem_limit_bytes=40 * 1024 * 1024),
        cost_estimate=pl.CostEstimate(
            flops=3_300_000_000, bytes_accessed=8_000_000, transcendentals=1_048_576
        ),
        name="terms",
    )(where, bounds, *feats, *embs, *biases, *events)


def per_device(features, task_embed, bin_bias, bin_bounds, event_time, censored, at_risk):
    tokens_all = features.shape[0] * lax.axis_size("dp") * lax.axis_size("task")
    bins = features.shape[1]
    task, dp = lax.axis_index("task"), lax.axis_index("dp")
    z, h, core = task // 2, task % 2, dp % 2
    where = jnp.stack([z, core, h]).astype(jnp.int32)

    mine = features.reshape(128, 512)
    chunk = {0: mine}
    for step in (1, -1, 2, -2):
        chunk[step] = lax.ppermute(mine, "task", z_shift(step))
    own_p, other_p = pack_events(where, at_risk, event_time, censored)
    swap = swap_low_bit(16)
    far_p = lax.ppermute(other_p, "task", swap)
    far_emb = lax.ppermute(task_embed, "task", swap)
    bias = bin_bias.T
    far_bias = lax.ppermute(bias, "task", swap)
    chunk[3] = lax.ppermute(chunk[1], "task", z_shift(2))
    chunk[-3] = lax.ppermute(chunk[-1], "task", z_shift(-2))
    upper = lax.ppermute(chunk[2][:64], "task", z_shift(2))
    lower = lax.ppermute(chunk[-2][64:], "task", z_shift(-2))

    feats = [chunk[step] for step in SLOTS[:-1]] + [upper, lower]
    outs = main_call(
        where, bin_bounds, feats, (task_embed, far_emb), (bias, far_bias), (own_p, far_p)
    )
    own, backs, keep, send = outs[0], outs[1:8], outs[8], outs[9]

    other = lax.ppermute(send, "dp", swap)
    returned = [
        lax.ppermute(part, "task", z_shift(-step)) for part, step in zip(backs, SLOTS[1:])
    ]
    both = keep + other
    pieces = jnp.concatenate(
        [
            both[:512].reshape(2, 8, 32, 512),
            jnp.broadcast_to(both[512:].reshape(2, 1, 8, 512), (2, 8, 8, 512)),
        ],
        axis=2,
    ).astype(jnp.bfloat16)
    swapped = lax.all_to_all(
        pieces.reshape(640, 512),
        ("dp", "task"),
        0,
        0,
        tiled=True,
        axis_index_groups=plane_groups(),
    )
    total = jnp.sum(swapped.reshape(16, 40, 512).astype(jnp.float32), axis=0)
    emb_scale = (tokens_all * bins) ** (-0.5)
    grad_embed = total[:32] * emb_scale
    grad_bias = lax.dynamic_slice_in_dim(total[32:], dp * 32, 32, 1).T * (1.0 / tokens_all)

    grad = own
    for part in returned:
        grad = grad + part.astype(jnp.float32)
    return (grad.astype(jnp.bfloat16).reshape(features.shape), grad_embed, grad_bias)


def solution(mesh):
    return jax.shard_map(
        per_device,
        mesh=mesh,
        in_specs=(
            P(("dp", "task"), None, None),
            P("task", None),
            P("task", None),
            P(),
            P("dp", "task"),
            P("dp", "task"),
            P("dp", "task"),
        ),
        out_specs=(P(("dp", "task"), None, None), P(("task", "dp"), None), P(("task", "dp"), None)),
        check_vma=False,
    )
```

time: 493 us -> 87.3 us (0.18)
  waiting for transfers between devices: 417 us -> 27 us
  starting transfers between devices: 0.16 us -> 43.5 us
  local copies, waits for them, and re-layouts: 30.4 us -> 1.03 us
  matrix products: 21.5 us -> 0 us
  between operations: 13.8 us -> 0.8 us
  Pallas kernels: 0 us -> 10.5 us
    reduce_scatter x2 -> x0, waiting for transfers between devices: 276 us -> none  [the longest x1 212 us: per_device(): lax.psum_scatter(grad_rows, 'task', scatter_dimension=0, tiled=True)]
    all_gather x1 -> x0, waiting for transfers between devices: 87.7 us -> none  [per_device(): gathered = lax.all_gather(features, 'task', axis=0, tiled=True)]
    unnamed x5 -> x0, waiting for transfers between devices: 53.4 us -> none
    ppermute x0 -> x19, starting transfers between devices: none -> 38.7 us  [the longest x7 13.8 us: per_device(): lax.ppermute(part, 'task', z_shift(-step))]
    ppermute x0 -> x19, waiting for transfers between devices: none -> 27 us  [the longest x7 14.1 us: per_device(): lax.ppermute(part, 'task', z_shift(-step))]
    dot_general x12 -> x0, matrix products: 21.5 us -> none  [the longest x4 11.4 us: block_terms(): jnp.einsum('tbd,kd->tbk', gathered, emb, preferred_element_type=jnp.float32)]
    while x25 -> x0, local copies, waits for them, and re-layouts: 14.5 us -> none
    pallas_call x0 -> x2, Pallas kernels: none -> 10.5 us  [the longest x1 8.37 us: main_call(): pl.pallas_call(main_kernel, out_shape=(jax.ShapeDtypeStruct((128, 512), j...]
  transfers between devices with their start and end apart: 4 -> 20, of which waited for: 4 -> 8; matrix products, arithmetic and copies ran while one was open for 2% -> 2% of each run, Pallas kernels for 0% -> 2%
where the time goes in v1:
time: 87.3 us; the launch traced here: 86.7 us
  starting transfers between devices  43.5 us (50%)
  waiting for transfers between devices  27 us (31%)
  Pallas kernels  10.5 us (12%)
  other arithmetic  3.98 us (5%)
  local copies, waits for them, and re-layouts  1.03 us (1%)
    ppermute x7, waiting for transfers between devices, per_device(): lax.ppermute(part, 'task', z_shift(-step))  14.1 us
    ppermute x7, starting transfers between devices, per_device(): lax.ppermute(part, 'task', z_shift(-step))  13.8 us
    pallas_call x1, Pallas kernels, main_call(): pl.pallas_call(main_kernel, out_shape=(jax.ShapeDtypeStruct((128, 512), j...  8.37 us
    ppermute x4, starting transfers between devices, per_device(): chunk[step] = lax.ppermute(mine, 'task', z_shift(step))  8.33 us
    all_to_all x1, starting transfers between devices, per_device(): lax.all_to_all(pieces.reshape(640, 512), ('dp', 'task'), 0, 0, tiled=True...  4.72 us
    ppermute x1, starting transfers between devices, per_device(): lower = lax.ppermute(chunk[-2][64:], 'task', z_shift(-2))  3.65 us
    ppermute x1, waiting for transfers between devices, per_device(): lower = lax.ppermute(chunk[-2][64:], 'task', z_shift(-2))  3.61 us
    ppermute x1, waiting for transfers between devices, per_device(): upper = lax.ppermute(chunk[2][:64], 'task', z_shift(2))  3.48 us
  transfers between devices with their start and end apart: 20, of which 8 were waited for; matrix products, arithmetic and copies ran while one was open for 2% of the time, Pallas kernels for 2%

profile of v1, /device:TPU:32, one launch (start us, length us, event | category | flops | bytes accessed | tf_op | source)
XLA Modules:
  0.0 86.7 jit_solution(14992280427995778824)
XLA Ops:
  0.6 0.0 copy-start.1
  0.6 0.0 copy-start.3
  0.7 0.0 copy-start.4
  0.7 0.0 copy-start.5
  0.7 3.3 %collective-permute-start.8 = (bf16[512,512]{1,0:T(8,128)(2,1)}, bf16[512,512]{1,0:T(8,128)(2,1)S(1)}, u32[]{:S(2)}, u32[]{:S(2)}) collective-permute-start(bf16[512,512]{1,0:T(8,128)(2,1)} %e0_ref.1), channel_id=1, source_target_pairs={{0,1},{1,0},{2,3},{3,2},{4,5},{5,4},{6,7},{7,6},{8,9},{9,8},{10,11... | collective-permute-start | bytes 1572872 | tf_op jit(solution)/shard_map/ppermute | solution.py:201
  4.0 5.4 %collective-permute-start.3 = (bf16[128,512]{1,0:T(8,128)(2,1)}, bf16[128,512]{1,0:T(8,128)(2,1)S(1)}, u32[]{:S(2)}, u32[]{:S(2)}) collective-permute-start(bf16[128,512]{1,0:T(8,128)(2,1)} %bitcast.13), channel_id=1, source_target_pairs={{0,12},{1,13},{2,14},{3,15},{4,0},{5,1},{6,2},{7,3},{8,4},{9,5},{1... | collective-permute-start | bytes 393224 | tf_op jit(solution)/shard_map/ppermute | solution.py:197
  9.4 0.0 collective-permute-start.2
  9.4 1.0 %collective-permute-start.1 = (bf16[128,512]{1,0:T(8,128)(2,1)}, bf16[128,512]{1,0:T(8,128)(2,1)S(1)}, u32[]{:S(2)}, u32[]{:S(2)}) collective-permute-start(bf16[128,512]{1,0:T(8,128)(2,1)} %bitcast.15), channel_id=1, source_target_pairs={{0,14},{1,15},{2,0},{3,1},{4,2},{5,3},{6,4},{7,5},{8,6},{9,7},{10,... | collective-permute-start | bytes 393224 | tf_op jit(solution)/shard_map/ppermute | solution.py:197
  10.4 0.3 collective-permute-start.9
  10.7 0.6 pad_add_fusion.where_ref
  11.3 0.0 copy-start
  11.3 2.1 %pack_events.1 = (s32[128,512]{1,0:T(8,128)}, s32[128,512]{1,0:T(8,128)}) custom-call(s32[3]{0:T(128)} %pad_add_fusion.where_ref, s32[2,4]{1,0:T(2,128)} %risk_ref.1, s32[256,512]{1,0:T(8,128)} %time_ref.1, s32[256,512]{1,0:T(8,128)} %cens_ref.1), custom_call_target="tpu_custom_call" | custom-call | tf_op jit(solution)/shard_map/pack_events/pallas_call | solution.py:55
  13.4 3.1 %collective-permute-done.9.b1_ref = f32[8,512]{1,0:T(8,128)S(1)} collective-permute-done((f32[8,512]{1,0:T(8,128)}, f32[8,512]{1,0:T(8,128)S(1)}, u32[]{:S(2)}, u32[]{:S(2)}) %collective-permute-start.9) | collective-permute-done | bytes 16416 | tf_op jit(solution)/shard_map/ppermute | solution.py:203
  16.5 0.0 copy-done.3
  16.5 1.9 %collective-permute-start = (bf16[128,512]{1,0:T(8,128)(2,1)S(1)}, bf16[128,512]{1,0:T(8,128)(2,1)S(1)}, u32[]{:S(2)}, u32[]{:S(2)}) collective-permute-start(bf16[128,512]{1,0:T(8,128)(2,1)S(1)} %bitcast.16), channel_id=1, source_target_pairs={{0,2},{1,3},{2,4},{3,5},{4,6},{5,7},{6,8},{7,9},{8,10},{9,11},{10,... | collective-permute-start | bytes 393224 | tf_op jit(solution)/shard_map/ppermute | solution.py:197
  18.4 0.0 collective-permute-done.3.f4
  18.4 3.2 %collective-permute-start.10 = (s32[128,512]{1,0:T(8,128)}, s32[128,512]{1,0:T(8,128)S(1)}, u32[]{:S(2)}, u32[]{:S(2)}) collective-permute-start(s32[128,512]{1,0:T(8,128)} %get-tuple-element.16), channel_id=1, source_target_pairs={{0,1},{1,0},{2,3},{3,2},{4,5},{5,4},{6,7},{7,6},{8,9},{9,8},{10,11... | collective-permute-start | bytes 786440 | tf_op jit(solution)/shard_map/ppermute | solution.py:200
  21.6 0.0 collective-permute-done.2.f3
  21.6 3.7 %collective-permute-start.7 = (bf16[64,512]{1,0:T(8,128)(2,1)S(1)}, bf16[64,512]{1,0:T(8,128)(2,1)S(1)}, u32[]{:S(2)}, u32[]{:S(2)}) collective-permute-start(bf16[64,512]{1,0:T(8,128)(2,1)S(1)} %slice.26), channel_id=1, source_target_pairs={{0,12},{1,13},{2,14},{3,15},{4,0},{5,1},{6,2},{7,3},{8,4},{9,5},{1... | collective-permute-start | bytes 196616 | tf_op jit(solution)/shard_map/ppermute | solution.py:207
  25.3 0.0 collective-permute-done.1.f2
  25.3 2.4 %collective-permute-start.5 = (bf16[128,512]{1,0:T(8,128)(2,1)S(1)}, bf16[128,512]{1,0:T(8,128)(2,1)S(1)}, u32[]{:S(2)}, u32[]{:S(2)}) collective-permute-start(bf16[128,512]{1,0:T(8,128)(2,1)S(1)} %collective-permute-done.1.f2), channel_id=1, source_target_pairs={{0,12},{1,13},{2,14},{3,15},{4,0},{5,1},{6,2},{7,3},{8,4},{9,5},{1... | collective-permute-start | bytes 393224 | tf_op jit(solution)/shard_map/ppermute | solution.py:205
  27.7 0.0 collective-permute-done.f1
  27.7 0.5 collective-permute-start.4
  28.2 3.6 %collective-permute-done.7.f7b = bf16[64,512]{1,0:T(8,128)(2,1)S(1)} collective-permute-done((bf16[64,512]{1,0:T(8,128)(2,1)S(1)}, bf16[64,512]{1,0:T(8,128)(2,1)S(1)}, u32[]{:S(2)}, u32[]{:S(2)}) %collective-permute-start.7) | collective-permute-done | bytes 65568 | tf_op jit(solution)/shard_map/ppermute | solution.py:207
  31.8 3.1 %collective-permute-start.6 = (bf16[64,512]{1,0:T(8,128)(2,1)S(1)}, bf16[64,512]{1,0:T(8,128)(2,1)S(1)}, u32[]{:S(2)}, u32[]{:S(2)}) collective-permute-start(bf16[64,512]{1,0:T(8,128)(2,1)S(1)} %slice.25), channel_id=1, source_target_pairs={{0,4},{1,5},{2,6},{3,7},{4,8},{5,9},{6,10},{7,11},{8,12},{9,13},{1... | collective-permute-start | bytes 196616 | tf_op jit(solution)/shard_map/ppermute | solution.py:206
  35.0 3.5 %collective-permute-done.6.f7a = bf16[64,512]{1,0:T(8,128)(2,1)S(1)} collective-permute-done((bf16[64,512]{1,0:T(8,128)(2,1)S(1)}, bf16[64,512]{1,0:T(8,128)(2,1)S(1)}, u32[]{:S(2)}, u32[]{:S(2)}) %collective-permute-start.6) | collective-permute-done | bytes 65568 | tf_op jit(solution)/shard_map/ppermute | solution.py:206
  38.4 0.0 collective-permute-done.5.f6
  38.4 0.0 collective-permute-done.4.f5
  38.5 0.0 collective-permute-done.10.p1_ref
  38.5 0.0 collective-permute-done.8.e1_ref
  38.5 0.0 copy-done.1
  38.5 0.0 copy-done.4
  38.5 0.0 copy-done.5
  38.5 0.0 copy-done
  38.5 0.0 copy-start.2
  38.5 0.9 %copy-done.2 = s32[128,512]{1,0:T(8,128)S(1)} copy-done((s32[128,512]{1,0:T(8,128)S(1)}, s32[128,512]{1,0:T(8,128)}, u32[]{:S(2)}) %copy-start.2) | copy-done | bytes 262168
  39.5 8.4 %terms.1 = (f32[128,512]{1,0:T(8,128)S(1)}, bf16[128,512]{1,0:T(8,128)(2,1)S(1)}, bf16[128,512]{1,0:T(8,128)(2,1)S(1)}, bf16[128,512]{1,0:T(8,128)(2,1)S(1)}, bf...) custom-call(s32[3]{0:T(128)S(1)} %copy-done, ...), custom_call_target="tpu_custom_call" | custom-call | flops 3300000000 | bytes 8000000 | tf_op jit(solution)/shard_map/terms/pallas_call | solution.py:166
  47.8 0.1 collective-permute-start.18
  47.9 2.7 %collective-permute-done.18 = f32[528,512]{1,0:T(8,128)S(1)} collective-permute-done((f32[528,512]{1,0:T(8,128)S(1)}, f32[528,512]{1,0:T(8,128)S(1)}, u32[]{:S(2)}, u32[]{:S(2)}) %collective-permute-start.18) | collective-permute-done | bytes 1081376 | tf_op jit(solution)/shard_map/ppermute | solution.py:215
  50.6 0.3 add.44
  51.0 0.9 %pad_maximum_fusion = bf16[16,40,512]{2,1,0:T(8,128)(2,1)} fusion(bf16[16,8,512]{2,1,0:T(8,128)(2,1)S(1)} %bitcast.21, bf16[16,32,512]{2,1,0:T(8,128)(2,1)S(1)} %bitcast.20), kind=kLoop, calls=%fused_computation.2 | loop fusion | flops 1310720 | bytes 1310720 | tf_op jit(solution)/shard_map/concatenate | solution.py:220
  51.9 4.7 %all-to-all-start = ((bf16[16,40,512]{2,1,0:T(8,128)(2,1)}), bf16[16,40,512]{2,1,0:T(8,128)(2,1)S(1)}, u32[]{:S(2)}, u32[]{:S(2)}) async-start(bf16[16,40,512]{2,1,0:T(8,128)(2,1)} %pad_maximum_fusion), calls=%async_computation | async-start | bytes 1310720 | tf_op jit(solution)/shard_map/all_to_all | solution.py:227
  56.6 1.5 %collective-permute-start.11 = (bf16[128,512]{1,0:T(8,128)(2,1)S(1)}, bf16[128,512]{1,0:T(8,128)(2,1)S(1)}, u32[]{:S(2)}, u32[]{:S(2)}) collective-permute-start(bf16[128,512]{1,0:T(8,128)(2,1)S(1)} %get-tuple-element.18), channel_id=1, source_target_pairs={{0,14},{1,15},{2,0},{3,1},{4,2},{5,3},{6,4},{7,5},{8,6},{9,7},{10,... | collective-permute-start | bytes 393224 | tf_op jit(solution)/shard_map/ppermute | solution.py:217
  58.1 0.6 collective-permute-start.12
  58.7 3.1 %collective-permute-start.13 = (bf16[128,512]{1,0:T(8,128)(2,1)S(1)}, bf16[128,512]{1,0:T(8,128)(2,1)S(1)}, u32[]{:S(2)}, u32[]{:S(2)}) collective-permute-start(bf16[128,512]{1,0:T(8,128)(2,1)S(1)} %get-tuple-element.20), channel_id=1, source_target_pairs={{0,12},{1,13},{2,14},{3,15},{4,0},{5,1},{6,2},{7,3},{8,4},{9,5},{1... | collective-permute-start | bytes 393224 | tf_op jit(solution)/shard_map/ppermute | solution.py:217
  61.8 0.0 collective-permute-start.14
  61.8 3.1 %collective-permute-start.15 = (bf16[128,512]{1,0:T(8,128)(2,1)S(1)}, bf16[128,512]{1,0:T(8,128)(2,1)S(1)}, u32[]{:S(2)}, u32[]{:S(2)}) collective-permute-start(bf16[128,512]{1,0:T(8,128)(2,1)S(1)} %get-tuple-element.22), channel_id=1, source_target_pairs={{0,10},{1,11},{2,12},{3,13},{4,14},{5,15},{6,0},{7,1},{8,2},{9,3},... | collective-permute-start | bytes 393224 | tf_op jit(solution)/shard_map/ppermute | solution.py:217
  64.9 0.0 collective-permute-done.11
  64.9 2.0 %collective-permute-start.16 = (bf16[128,512]{1,0:T(8,128)(2,1)S(1)}, bf16[128,512]{1,0:T(8,128)(2,1)S(1)}, u32[]{:S(2)}, u32[]{:S(2)}) collective-permute-start(bf16[128,512]{1,0:T(8,128)(2,1)S(1)} %get-tuple-element.23), channel_id=1, source_target_pairs={{0,6},{1,7},{2,8},{3,9},{4,10},{5,11},{6,12},{7,13},{8,14},{9,15},... | collective-permute-start | bytes 393224 | tf_op jit(solution)/shard_map/ppermute | solution.py:217
  66.9 0.0 collective-permute-done.12
  66.9 3.6 %collective-permute-start.17 = (bf16[128,512]{1,0:T(8,128)(2,1)S(1)}, bf16[128,512]{1,0:T(8,128)(2,1)S(1)}, u32[]{:S(2)}, u32[]{:S(2)}) collective-permute-start(bf16[128,512]{1,0:T(8,128)(2,1)S(1)} %get-tuple-element.24), channel_id=1, source_target_pairs={{0,8},{1,9},{2,10},{3,11},{4,12},{5,13},{6,14},{7,15},{8,0},{9,1},... | collective-permute-start | bytes 393224 | tf_op jit(solution)/shard_map/ppermute | solution.py:217
  70.4 0.0 collective-permute-done.13
  70.4 0.5 collective-permute-done.14
  70.9 7.7 %collective-permute-done.15 = bf16[128,512]{1,0:T(8,128)(2,1)S(1)} collective-permute-done((bf16[128,512]{1,0:T(8,128)(2,1)S(1)}, bf16[128,512]{1,0:T(8,128)(2,1)S(1)}, u32[]{:S(2)}, u32[]{:S(2)}) %collective-permute-start.15) | collective-permute-done | bytes 131104 | tf_op jit(solution)/shard_map/ppermute | solution.py:217
  78.6 3.5 %collective-permute-done.16 = bf16[128,512]{1,0:T(8,128)(2,1)S(1)} collective-permute-done((bf16[128,512]{1,0:T(8,128)(2,1)S(1)}, bf16[128,512]{1,0:T(8,128)(2,1)S(1)}, u32[]{:S(2)}, u32[]{:S(2)}) %collective-permute-start.16) | collective-permute-done | bytes 131104 | tf_op jit(solution)/shard_map/ppermute | solution.py:217
  82.1 2.4 %collective-permute-done.17 = bf16[128,512]{1,0:T(8,128)(2,1)S(1)} collective-permute-done((bf16[128,512]{1,0:T(8,128)(2,1)S(1)}, bf16[128,512]{1,0:T(8,128)(2,1)S(1)}, u32[]{:S(2)}, u32[]{:S(2)}) %collective-permute-start.17) | collective-permute-done | bytes 131104 | tf_op jit(solution)/shard_map/ppermute | solution.py:217
  84.5 0.8 fusion
  85.3 0.0 all-to-all-done
  85.3 0.1 convert_reduce_fusion
  85.4 0.6 slice_multiply_fusion
  86.0 0.7 multiply_bitcast_fusion
  (6 shorter events, 0.1 us)
Async XLA Ops:
  0.6 37.8 %copy-start.1 = (bf16[512,512]{1,0:T(8,128)(2,1)S(1)}, bf16[512,512]{1,0:T(8,128)(2,1)}, u32[]{:S(2)}) copy-start(bf16[512,512]{1,0:T(8,128)(2,1)} %e0_ref.1) | copy-start | bytes 1572868
  0.6 15.8 %copy-start.3 = (bf16[16,8,512]{2,1,0:T(8,128)(2,1)S(1)}, bf16[16,8,512]{2,1,0:T(8,128)(2,1)}, u32[]{:S(2)}) copy-start(bf16[16,8,512]{2,1,0:T(8,128)(2,1)} %param.7) | copy-start | bytes 393220
  0.7 37.8 %copy-start.4 = (f32[512,8]{0,1:T(8,128)S(1)}, f32[512,8]{0,1:T(8,128)}, u32[]{:S(2)}) copy-start(f32[512,8]{0,1:T(8,128)} %param.9) | copy-start | bytes 49156
  0.7 37.8 %copy-start.5 = (s32[9]{0:T(128)S(1)}, s32[9]{0:T(128)}, u32[]{:S(2)}) copy-start(s32[9]{0:T(128)} %bounds_ref.1) | copy-start | bytes 112
  0.7 37.8 %collective-permute-start.8 = (bf16[512,512]{1,0:T(8,128)(2,1)}, bf16[512,512]{1,0:T(8,128)(2,1)S(1)}, u32[]{:S(2)}, u32[]{:S(2)}) collective-permute-start(bf16[512,512]{1,0:T(8,128)(2,1)} %e0_ref.1), channel_id=1, source_target_pairs={{0,1},{1,0},{2,3},{3,2},{4,5},{5,4},{6,7},{7,6},{8,9},{9,8},{10,11... | collective-permute-start | bytes 1572872 | tf_op jit(solution)/shard_map/ppermute | solution.py:201
  4.0 14.5 %collective-permute-start.3 = (bf16[128,512]{1,0:T(8,128)(2,1)}, bf16[128,512]{1,0:T(8,128)(2,1)S(1)}, u32[]{:S(2)}, u32[]{:S(2)}) collective-permute-start(bf16[128,512]{1,0:T(8,128)(2,1)} %bitcast.13), channel_id=1, source_target_pairs={{0,12},{1,13},{2,14},{3,15},{4,0},{5,1},{6,2},{7,3},{8,4},{9,5},{1... | collective-permute-start | bytes 393224 | tf_op jit(solution)/shard_map/ppermute | solution.py:197
  9.4 12.3 %collective-permute-start.2 = (bf16[128,512]{1,0:T(8,128)(2,1)}, bf16[128,512]{1,0:T(8,128)(2,1)S(1)}, u32[]{:S(2)}, u32[]{:S(2)}) collective-permute-start(bf16[128,512]{1,0:T(8,128)(2,1)} %bitcast.14), channel_id=1, source_target_pairs={{0,4},{1,5},{2,6},{3,7},{4,8},{5,9},{6,10},{7,11},{8,12},{9,13},{1... | collective-permute-start | bytes 393224 | tf_op jit(solution)/shard_map/ppermute | solution.py:197
  9.4 15.9 %collective-permute-start.1 = (bf16[128,512]{1,0:T(8,128)(2,1)}, bf16[128,512]{1,0:T(8,128)(2,1)S(1)}, u32[]{:S(2)}, u32[]{:S(2)}) collective-permute-start(bf16[128,512]{1,0:T(8,128)(2,1)} %bitcast.15), channel_id=1, source_target_pairs={{0,14},{1,15},{2,0},{3,1},{4,2},{5,3},{6,4},{7,5},{8,6},{9,7},{10,... | collective-permute-start | bytes 393224 | tf_op jit(solution)/shard_map/ppermute | solution.py:197
  10.4 6.1 %collective-permute-start.9 = (f32[8,512]{1,0:T(8,128)}, f32[8,512]{1,0:T(8,128)S(1)}, u32[]{:S(2)}, u32[]{:S(2)}) collective-permute-start(f32[8,512]{1,0:T(8,128)} %bitcast.18), channel_id=1, source_target_pairs={{0,1},{1,0},{2,3},{3,2},{4,5},{5,4},{6,7},{7,6},{8,9},{9,8},{10,11... | collective-permute-start | bytes 49160 | tf_op jit(solution)/shard_map/ppermute | solution.py:203
  11.3 27.2 %copy-start = (s32[3]{0:T(128)S(1)}, s32[3]{0:T(128)}, u32[]{:S(2)}) copy-start(s32[3]{0:T(128)} %pad_add_fusion.where_ref) | copy-start | bytes 40
  16.5 11.2 %collective-permute-start = (bf16[128,512]{1,0:T(8,128)(2,1)S(1)}, bf16[128,512]{1,0:T(8,128)(2,1)S(1)}, u32[]{:S(2)}, u32[]{:S(2)}) collective-permute-start(bf16[128,512]{1,0:T(8,128)(2,1)S(1)} %bitcast.16), channel_id=1, source_target_pairs={{0,2},{1,3},{2,4},{3,5},{4,6},{5,7},{6,8},{7,9},{8,10},{9,11},{10,... | collective-permute-start | bytes 393224 | tf_op jit(solution)/shard_map/ppermute | solution.py:197
  18.4 20.0 %collective-permute-start.10 = (s32[128,512]{1,0:T(8,128)}, s32[128,512]{1,0:T(8,128)S(1)}, u32[]{:S(2)}, u32[]{:S(2)}) collective-permute-start(s32[128,512]{1,0:T(8,128)} %get-tuple-element.16), channel_id=1, source_target_pairs={{0,1},{1,0},{2,3},{3,2},{4,5},{5,4},{6,7},{7,6},{8,9},{9,8},{10,11... | collective-permute-start | bytes 786440 | tf_op jit(solution)/shard_map/ppermute | solution.py:200
  21.6 10.2 %collective-permute-start.7 = (bf16[64,512]{1,0:T(8,128)(2,1)S(1)}, bf16[64,512]{1,0:T(8,128)(2,1)S(1)}, u32[]{:S(2)}, u32[]{:S(2)}) collective-permute-start(bf16[64,512]{1,0:T(8,128)(2,1)S(1)} %slice.26), channel_id=1, source_target_pairs={{0,12},{1,13},{2,14},{3,15},{4,0},{5,1},{6,2},{7,3},{8,4},{9,5},{1... | collective-permute-start | bytes 196616 | tf_op jit(solution)/shard_map/ppermute | solution.py:207
  25.3 13.2 %collective-permute-start.5 = (bf16[128,512]{1,0:T(8,128)(2,1)S(1)}, bf16[128,512]{1,0:T(8,128)(2,1)S(1)}, u32[]{:S(2)}, u32[]{:S(2)}) collective-permute-start(bf16[128,512]{1,0:T(8,128)(2,1)S(1)} %collective-permute-done.1.f2), channel_id=1, source_target_pairs={{0,12},{1,13},{2,14},{3,15},{4,0},{5,1},{6,2},{7,3},{8,4},{9,5},{1... | collective-permute-start | bytes 393224 | tf_op jit(solution)/shard_map/ppermute | solution.py:205
  27.7 10.8 %collective-permute-start.4 = (bf16[128,512]{1,0:T(8,128)(2,1)S(1)}, bf16[128,512]{1,0:T(8,128)(2,1)S(1)}, u32[]{:S(2)}, u32[]{:S(2)}) collective-permute-start(bf16[128,512]{1,0:T(8,128)(2,1)S(1)} %collective-permute-done.f1), channel_id=1, source_target_pairs={{0,4},{1,5},{2,6},{3,7},{4,8},{5,9},{6,10},{7,11},{8,12},{9,13},{1... | collective-permute-start | bytes 393224 | tf_op jit(solution)/shard_map/ppermute | solution.py:204
  31.8 6.6 %collective-permute-start.6 = (bf16[64,512]{1,0:T(8,128)(2,1)S(1)}, bf16[64,512]{1,0:T(8,128)(2,1)S(1)}, u32[]{:S(2)}, u32[]{:S(2)}) collective-permute-start(bf16[64,512]{1,0:T(8,128)(2,1)S(1)} %slice.25), channel_id=1, source_target_pairs={{0,4},{1,5},{2,6},{3,7},{4,8},{5,9},{6,10},{7,11},{8,12},{9,13},{1... | collective-permute-start | bytes 196616 | tf_op jit(solution)/shard_map/ppermute | solution.py:206
  38.5 1.0 %copy-start.2 = (s32[128,512]{1,0:T(8,128)S(1)}, s32[128,512]{1,0:T(8,128)}, u32[]{:S(2)}) copy-start(s32[128,512]{1,0:T(8,128)} %get-tuple-element.15.p0_ref) | copy-start | bytes 786436
  47.8 2.8 %collective-permute-start.18 = (f32[528,512]{1,0:T(8,128)S(1)}, f32[528,512]{1,0:T(8,128)S(1)}, u32[]{:S(2)}, u32[]{:S(2)}) collective-permute-start(f32[528,512]{1,0:T(8,128)S(1)} %get-tuple-element.26), channel_id=1, source_target_pairs={{0,16},{16,0},{32,48},{48,32},{64,80},{80,64},{96,112},{112,96},{1... | collective-permute-start | bytes 3244040 | tf_op jit(solution)/shard_map/ppermute | solution.py:215
  51.9 33.4 %all-to-all-start = ((bf16[16,40,512]{2,1,0:T(8,128)(2,1)}), bf16[16,40,512]{2,1,0:T(8,128)(2,1)S(1)}, u32[]{:S(2)}, u32[]{:S(2)}) async-start(bf16[16,40,512]{2,1,0:T(8,128)(2,1)} %pad_maximum_fusion), calls=%async_computation | async-start | bytes 1310720 | tf_op jit(solution)/shard_map/all_to_all | solution.py:227
  56.6 8.3 %collective-permute-start.11 = (bf16[128,512]{1,0:T(8,128)(2,1)S(1)}, bf16[128,512]{1,0:T(8,128)(2,1)S(1)}, u32[]{:S(2)}, u32[]{:S(2)}) collective-permute-start(bf16[128,512]{1,0:T(8,128)(2,1)S(1)} %get-tuple-element.18), channel_id=1, source_target_pairs={{0,14},{1,15},{2,0},{3,1},{4,2},{5,3},{6,4},{7,5},{8,6},{9,7},{10,... | collective-permute-start | bytes 393224 | tf_op jit(solution)/shard_map/ppermute | solution.py:217
  58.1 8.7 %collective-permute-start.12 = (bf16[128,512]{1,0:T(8,128)(2,1)S(1)}, bf16[128,512]{1,0:T(8,128)(2,1)S(1)}, u32[]{:S(2)}, u32[]{:S(2)}) collective-permute-start(bf16[128,512]{1,0:T(8,128)(2,1)S(1)} %get-tuple-element.19), channel_id=1, source_target_pairs={{0,2},{1,3},{2,4},{3,5},{4,6},{5,7},{6,8},{7,9},{8,10},{9,11},{10,... | collective-permute-start | bytes 393224 | tf_op jit(solution)/shard_map/ppermute | solution.py:217
  58.7 11.7 %collective-permute-start.13 = (bf16[128,512]{1,0:T(8,128)(2,1)S(1)}, bf16[128,512]{1,0:T(8,128)(2,1)S(1)}, u32[]{:S(2)}, u32[]{:S(2)}) collective-permute-start(bf16[128,512]{1,0:T(8,128)(2,1)S(1)} %get-tuple-element.20), channel_id=1, source_target_pairs={{0,12},{1,13},{2,14},{3,15},{4,0},{5,1},{6,2},{7,3},{8,4},{9,5},{1... | collective-permute-start | bytes 393224 | tf_op jit(solution)/shard_map/ppermute | solution.py:217
  61.8 9.1 %collective-permute-start.14 = (bf16[128,512]{1,0:T(8,128)(2,1)S(1)}, bf16[128,512]{1,0:T(8,128)(2,1)S(1)}, u32[]{:S(2)}, u32[]{:S(2)}) collective-permute-start(bf16[128,512]{1,0:T(8,128)(2,1)S(1)} %get-tuple-element.21), channel_id=1, source_target_pairs={{0,4},{1,5},{2,6},{3,7},{4,8},{5,9},{6,10},{7,11},{8,12},{9,13},{1... | collective-permute-start | bytes 393224 | tf_op jit(solution)/shard_map/ppermute | solution.py:217
  61.8 16.8 %collective-permute-start.15 = (bf16[128,512]{1,0:T(8,128)(2,1)S(1)}, bf16[128,512]{1,0:T(8,128)(2,1)S(1)}, u32[]{:S(2)}, u32[]{:S(2)}) collective-permute-start(bf16[128,512]{1,0:T(8,128)(2,1)S(1)} %get-tuple-element.22), channel_id=1, source_target_pairs={{0,10},{1,11},{2,12},{3,13},{4,14},{5,15},{6,0},{7,1},{8,2},{9,3},... | collective-permute-start | bytes 393224 | tf_op jit(solution)/shard_map/ppermute | solution.py:217
  64.9 17.2 %collective-permute-start.16 = (bf16[128,512]{1,0:T(8,128)(2,1)S(1)}, bf16[128,512]{1,0:T(8,128)(2,1)S(1)}, u32[]{:S(2)}, u32[]{:S(2)}) collective-permute-start(bf16[128,512]{1,0:T(8,128)(2,1)S(1)} %get-tuple-element.23), channel_id=1, source_target_pairs={{0,6},{1,7},{2,8},{3,9},{4,10},{5,11},{6,12},{7,13},{8,14},{9,15},... | collective-permute-start | bytes 393224 | tf_op jit(solution)/shard_map/ppermute | solution.py:217
  66.9 17.6 %collective-permute-start.17 = (bf16[128,512]{1,0:T(8,128)(2,1)S(1)}, bf16[128,512]{1,0:T(8,128)(2,1)S(1)}, u32[]{:S(2)}, u32[]{:S(2)}) collective-permute-start(bf16[128,512]{1,0:T(8,128)(2,1)S(1)} %get-tuple-element.24), channel_id=1, source_target_pairs={{0,8},{1,9},{2,10},{3,11},{4,12},{5,13},{6,14},{7,15},{8,0},{9,1},... | collective-permute-start | bytes 393224 | tf_op jit(solution)/shard_map/ppermute | solution.py:217

commit v2 on v0

v2 whole, which is shorter than its diff:
```python
import jax
import jax.numpy as jnp
from jax import lax
from jax.experimental import pallas as pl
from jax.experimental.pallas import tpu as pltpu
from jax.sharding import PartitionSpec as P

time_unit = 0.015625

NZ = 8
ROWS = 128
WIDE = 512
LIMIT = 40 * 1024 * 1024
BOTH = ("dp", "task")


def z_shift(step):
    return [(z * 2 + h, ((z + step) % NZ) * 2 + h) for z in range(NZ) for h in range(2)]


def z_apart(step):
    pairs = []
    for dp in range(16):
        way = step if dp % 2 == 0 else -step
        for z in range(NZ):
            for h in range(2):
                pairs.append((dp * 16 + z * 2 + h, dp * 16 + ((z + way) % NZ) * 2 + h))
    return pairs


def y_shift(step):
    pairs = []
    for y in range(4):
        there = (y + step) % 4
        for inner in range(8):
            for z in range(NZ):
                source = ((y % 2) * 8 + inner) * 16 + z * 2 + y // 2
                target = ((there % 2) * 8 + inner) * 16 + z * 2 + there // 2
                pairs.append((source, target))
    return pairs


def x_shift(step):
    return [
        ((low * 4 + x) * 2 + core, (low * 4 + (x + step) % 4) * 2 + core)
        for low in range(2)
        for x in range(4)
        for core in range(2)
    ]


def swap_low_bit():
    return [(i, i ^ 1) for i in range(16)]


def column_groups():
    return [[z * 2 + h for z in range(NZ)] for h in range(2)]


def place():
    task, dp = lax.axis_index("task"), lax.axis_index("dp")
    return task // 2, lax.rem(dp, 2), lax.rem(task, 2)


def call(kernel, name, outs, args, spaces="", to="", scratch=(), limit=LIMIT):
    kinds = {"s": pltpu.SMEM, "v": pltpu.VMEM, "a": pl.ANY, "h": pltpu.HBM}
    spaces = spaces + "v" * (len(args) - len(spaces))
    to = to + "v" * (len(outs) - len(to))
    return pl.pallas_call(
        kernel,
        out_shape=[jax.ShapeDtypeStruct(shape, kind) for shape, kind in outs],
        in_specs=[pl.BlockSpec(memory_space=kinds[space]) for space in spaces],
        out_specs=[pl.BlockSpec(memory_space=kinds[space]) for space in to],
        scratch_shapes=scratch,
        compiler_params=pltpu.CompilerParams(vmem_limit_bytes=limit),
        name=name,
    )(*args)


def pack_kernel(risk_ref, bounds_ref, time_ref, cens_ref, bias_ref, own_ref, other_ref):
    _, _, h = place()
    for z in range(NZ):
        row = z // (NZ // 2)
        for side, out in ((h, own_ref), (1 - h, other_ref)):
            start = pl.multiple_of(z * 32 + side * 16, 16)
            times = time_ref[pl.ds(start, 16), :]
            signed = jnp.where(cens_ref[pl.ds(start, 16), :] == 0, times, -times)
            for k in range(4):
                cols = slice(k * 128, (k + 1) * 128)
                live = signed[:, cols] * risk_ref[row, k]
                out[z * 16 : (z + 1) * 16, cols] = live.astype(jnp.float32) * time_unit
    own_ref[128:136, :] = bias_ref[...]
    other_ref[128:136, :] = bias_ref[...]
    bins = lax.broadcasted_iota(jnp.int32, (8, WIDE), 0)
    for k in range(2):
        edge = jnp.zeros((8, WIDE), jnp.int32)
        for b in range(8):
            edge = jnp.where(bins == b, bounds_ref[b + k], edge)
        own_ref[136 + k * 8 : 144 + k * 8, :] = edge.astype(jnp.float32) * time_unit


def grad_kernel(*refs):
    chunks, refs = refs[:8], refs[8:]
    e0, e1, p0, p1, back_ref, low_out, bin_ref, feats, embs, events, backs, low_ref, sems = refs
    z, core, _ = place()

    def fetch(source, target, slot):
        copy = pltpu.make_async_copy(source, target, sems.at[slot])
        copy.start()
        return copy

    copies = [
        fetch(chunk, feats.at[pl.ds(slot * ROWS, ROWS)], slot)
        for slot, chunk in enumerate(chunks)
    ]
    copies.append(fetch(e0, embs.at[pl.ds(0, 512)], 8))
    copies.append(fetch(p0, events.at[pl.ds(0, 152)], 9))
    copies.append(fetch(e1, embs.at[pl.ds(512, 512)], 10))
    copies.append(fetch(p1, events.at[pl.ds(152, 136)], 11))

    way = 1 - 2 * core
    shifts = (0, 1, -1, 2 * way, -2 * way, 3 * way, -3 * way, 4)
    owners = [lax.rem(z + (NZ - shift), NZ) for shift in shifts]
    for copy in copies:
        copy.wait()
    lower, upper = events[136:144, :], events[144:152, :]
    span = upper - lower

    def step(i, carry):
        out = pl.ds(pl.multiple_of(i * WIDE, WIDE), WIDE)
        emb = embs[out, :]
        base = i * 152
        bias = events[pl.ds(pl.multiple_of(base + 128, 8), 8), :]
        g_bin = jnp.zeros((8, WIDE), jnp.float32)
        for part in range(4):
            logit = lax.dot_general(
                feats[part * 256 : (part + 1) * 256, :],
                emb,
                (((1,), (1,)), ((), ())),
                preferred_element_type=jnp.float32,
            )
            for slot in (2 * part, 2 * part + 1):
                signed = events[pl.ds(pl.multiple_of(base + owners[slot] * 16, 8), 16), :]
                moment = jnp.abs(signed)[:, None, :]
                signed = signed[:, None, :]
                at = (slot % 2) * ROWS
                piece = logit[at : at + ROWS].reshape(16, 8, WIDE) + bias[None]
                exposure = jnp.clip(moment - lower[None], 0.0, span[None])
                inside = (signed > lower[None]) & (signed <= upper[None])
                dlogit = exposure * jnp.exp(piece) - inside.astype(jnp.float32)
                g_bin = g_bin + jnp.sum(dlogit, axis=0)
                low_ref[slot * ROWS : (slot + 1) * ROWS, out] = dlogit.reshape(ROWS, WIDE).astype(
                    jnp.bfloat16
                )
        bin_ref[:, out] = g_bin
        return carry

    lax.fori_loop(0, 2, step, 0)
    sent = [fetch(low_ref, low_out, 8)]
    for slot in range(0, 8, 2):
        both = jnp.dot(
            low_ref[slot * ROWS : (slot + 2) * ROWS, :],
            embs[...],
            preferred_element_type=jnp.float32,
        ).astype(jnp.bfloat16)
        backs[slot * ROWS : (slot + 2) * ROWS, :] = both
        for one in (slot, slot + 1):
            source = backs.at[pl.ds(one * ROWS, ROWS)]
            target = back_ref.at[pl.ds(pl.multiple_of(owners[one] * ROWS, ROWS), ROWS)]
            sent.append(fetch(source, target, one))
    for copy in sent:
        copy.wait()


def split_sums(sums):
    high = sums.astype(jnp.bfloat16)
    rest = (sums - high.astype(jnp.float32)).astype(jnp.bfloat16)
    return jnp.concatenate([high, rest], axis=0)


def emb_kernel(*refs):
    chunks, refs = refs[:8], refs[8:]
    low_in, bin_ref, keep_ref, send_ref, feats, low_ref, sems = refs
    copies = []
    for slot, chunk in enumerate(chunks):
        copy = pltpu.make_async_copy(
            chunk, feats.at[pl.ds(slot * ROWS, ROWS)], sems.at[slot]
        )
        copy.start()
        copies.append(copy)
    blocks = []
    for i in range(4):
        part = pl.ds(i * 256, 256)
        blocks.append(
            pltpu.make_async_copy(low_in.at[:, part], low_ref.at[:, part], sems.at[8 + i])
        )
        blocks[i].start()
    for copy in copies:
        copy.wait()
    _, core, h = place()

    for i in range(4):
        blocks[i].wait()
        g_emb = lax.dot_general(
            low_ref[:, i * 256 : (i + 1) * 256],
            feats[...],
            (((0,), (0,)), ((), ())),
            preferred_element_type=jnp.float32,
        )
        there = (h if i < 2 else 1 - h) * 2 + i % 2
        split = g_emb.reshape(4, 2, 32, 512)
        zero, one = split[:, 0].reshape(128, 512), split[:, 1].reshape(128, 512)
        spot = pl.ds(pl.multiple_of(there * 128, 128), 128)
        keep_ref[spot, :] = jnp.where(core == 0, zero, one)
        send_ref[spot, :] = jnp.where(core == 0, one, zero).astype(jnp.bfloat16)

    for side in range(2):
        sums = bin_ref[:, side * 512 : (side + 1) * 512]
        there = h if side == 0 else 1 - h
        keep_ref[pl.ds(pl.multiple_of(512 + there * 8, 8), 8), :] = sums
        send_ref[pl.ds(pl.multiple_of(512 + there * 16, 16), 16), :] = split_sums(sums)


def join_kernel(keep_ref, got_ref, own_ref, *outs):
    h, low_y = lax.rem(lax.axis_index("task"), 2), lax.axis_index("dp") // 8
    for shift in range(4):
        there = lax.rem(h * 2 + low_y + shift, 4)
        spot = pl.ds(pl.multiple_of(there * 128, 128), 128)
        rows = keep_ref[spot, :] + got_ref[spot, :].astype(jnp.float32)
        side = there // 2
        tail = got_ref[pl.ds(pl.multiple_of(512 + side * 16, 16), 16), :].astype(jnp.float32)
        sums = keep_ref[pl.ds(pl.multiple_of(512 + side * 8, 8), 8), :] + tail[0:8] + tail[8:16]
        if shift == 0:
            own_ref[0:128, :] = rows
            own_ref[128:136, :] = sums
        else:
            outs[shift - 1][0:128, :] = rows.astype(jnp.bfloat16)
            outs[shift - 1][128:144, :] = split_sums(sums)


def add_parts(own_ref, parts, rows):
    total = own_ref[0:rows, :]
    sums = own_ref[rows : rows + 8, :]
    for part in parts:
        total = total + part[0:rows, :].astype(jnp.float32)
        tail = part[rows : rows + 16, :].astype(jnp.float32)
        sums = sums + tail[0:8] + tail[8:16]
    return total, sums


def sum_y_kernel(*refs):
    own_ref, parts, mine_ref, outs, total = refs[0], refs[1:4], refs[4], refs[5:8], refs[8]
    rows, sums = add_parts(own_ref, parts, 128)
    total[...] = rows
    x = lax.rem(lax.axis_index("dp") // 2, 4)
    for shift in range(4):
        there = lax.rem(x + shift, 4)
        piece = total[pl.ds(pl.multiple_of(there * 32, 32), 32), :]
        if shift == 0:
            mine_ref[0:32, :] = piece
            mine_ref[32:40, :] = sums
        else:
            outs[shift - 1][0:32, :] = piece.astype(jnp.bfloat16)
            outs[shift - 1][32:48, :] = split_sums(sums)


def sum_x_kernel(emb_scale, bin_scale, *refs):
    own_ref, parts, emb_ref, bin_ref = refs[0], refs[1:4], refs[4], refs[5]
    rows, sums = add_parts(own_ref, parts, 32)
    emb_ref[...] = rows * emb_scale
    dp = lax.axis_index("dp")
    turned = pltpu.roll(sums, lax.rem(512 - dp * 32, 512), 1)
    bin_ref[...] = turned[:, 0:32] * bin_scale


def sum_kernel(parts_ref, out_ref):
    total = parts_ref[0:ROWS, :].astype(jnp.float32)
    for k in range(1, NZ):
        total = total + parts_ref[k * ROWS : (k + 1) * ROWS, :].astype(jnp.float32)
    out_ref[...] = total.astype(jnp.bfloat16)


def per_device(features, task_embed, bin_bias, bin_bounds, event_time, censored, at_risk):
    tokens_all = features.shape[0] * lax.axis_size("dp") * lax.axis_size("task")
    bins = features.shape[1]
    swap = swap_low_bit()
    low, wide = jnp.bfloat16, jnp.float32

    mine = features.reshape(ROWS, 512)
    far_emb = lax.ppermute(task_embed, "task", swap)
    two = lax.ppermute(mine, BOTH, z_apart(2))
    two_back = lax.ppermute(mine, BOTH, z_apart(-2))
    p0, out_p = call(
        pack_kernel,
        "pack_events",
        [((152, 512), wide), ((136, 512), wide)],
        (at_risk, bin_bounds, event_time, censored, bin_bias.T),
        "ss",
        limit=None,
    )
    p1 = lax.ppermute(out_p, "task", swap)
    three = lax.ppermute(two, BOTH, z_apart(1))
    three_back = lax.ppermute(two_back, BOTH, z_apart(-1))
    four = lax.ppermute(two, BOTH, z_apart(2))
    one = lax.ppermute(mine, "task", z_shift(1))
    one_back = lax.ppermute(mine, "task", z_shift(-1))
    chunks = (mine, one, one_back, two, two_back, three, three_back, four)

    back, lows, g_bin = call(
        grad_kernel,
        "terms",
        [((1024, 512), low), ((1024, 1024), low), ((8, 1024), wide)],
        (*chunks, task_embed, far_emb, p0, p1),
        "h" * 12,
        "hh",
        limit=None,
        scratch=[
            pltpu.VMEM((1024, 512), low),
            pltpu.VMEM((1024, 512), low),
            pltpu.VMEM((288, 512), wide),
            pltpu.VMEM((1024, 512), low),
            pltpu.VMEM((1024, 1024), low),
            pltpu.SemaphoreType.DMA((12,)),
        ],
    )
    returned = lax.all_to_all(back, "task", 0, 0, tiled=True, axis_index_groups=column_groups())

    keep, send = call(
        emb_kernel,
        "emb_terms",
        [((528, 512), wide), ((544, 512), low)],
        (*chunks, lows, g_bin),
        "h" * 9,
        limit=None,
        scratch=[
            pltpu.VMEM((1024, 512), low),
            pltpu.VMEM((1024, 1024), low),
            pltpu.SemaphoreType.DMA((12,)),
        ],
    )
    got = lax.ppermute(send, "dp", swap)
    own, *parts = call(
        join_kernel, "join_cores", [((136, 512), wide)] + [((144, 512), low)] * 3, (keep, got)
    )
    parts = [lax.ppermute(part, BOTH, y_shift(d)) for d, part in enumerate(parts, 1)]
    own, *parts = call(
        sum_y_kernel,
        "sum_y",
        [((40, 512), wide)] + [((48, 512), low)] * 3,
        (own, *parts),
        scratch=[pltpu.VMEM((128, 512), wide)],
    )
    parts = [lax.ppermute(part, "dp", x_shift(d)) for d, part in enumerate(parts, 1)]

    def sum_x(*refs):
        sum_x_kernel((tokens_all * bins) ** (-0.5), 1.0 / tokens_all, *refs)

    grad_embed, grad_bias = call(
        sum_x, "sum_x", [((32, 512), wide), ((8, 32), wide)], (own, *parts)
    )
    (grad,) = call(sum_kernel, "sum_returned", [((ROWS, 512), low)], (returned,))
    return (grad.reshape(features.shape), grad_embed, grad_bias.T)


def solution(mesh):
    return jax.shard_map(
        per_device,
        mesh=mesh,
        in_specs=(
            P(("dp", "task"), None, None),
            P("task", None),
            P("task", None),
            P(),
            P("dp", "task"),
            P("dp", "task"),
            P("dp", "task"),
        ),
        out_specs=(P(("dp", "task"), None, None), P(("task", "dp"), None), P(("task", "dp"), None)),
        check_vma=False,
    )
```

time: 493 us -> 75 us (0.15)
  waiting for transfers between devices: 417 us -> 24.1 us
  starting transfers between devices: 0.16 us -> 31 us
  local copies, waits for them, and re-layouts: 30.4 us -> 2.16 us
  matrix products: 21.5 us -> 0 us
  Pallas kernels: 0 us -> 16.7 us
  between operations: 13.8 us -> 0.76 us
  other arithmetic: 7.64 us -> 0 us
    reduce_scatter x2 -> x0, waiting for transfers between devices: 276 us -> none  [the longest x1 212 us: per_device(): lax.psum_scatter(grad_rows, 'task', scatter_dimension=0, tiled=True)]
    all_gather x1 -> x0, waiting for transfers between devices: 87.7 us -> none  [per_device(): gathered = lax.all_gather(features, 'task', axis=0, tiled=True)]
    unnamed x5 -> x0, waiting for transfers between devices: 53.4 us -> none
    ppermute x0 -> x16, starting transfers between devices: none -> 25.6 us  [the longest x3 5.74 us: per_device(): lax.ppermute(part, 'dp', x_shift(d))]
    ppermute x0 -> x16, waiting for transfers between devices: none -> 24.1 us  [the longest x1 6.4 us: per_device(): two = lax.ppermute(mine, BOTH, z_apart(2))]
    dot_general x12 -> x0, matrix products: 21.5 us -> none  [the longest x4 11.4 us: block_terms(): jnp.einsum('tbd,kd->tbk', gathered, emb, preferred_element_type=jnp.float32)]
    pallas_call x0 -> x7, Pallas kernels: none -> 16.7 us  [call(): pl.pallas_call(kernel, out_shape=[jax.ShapeDtypeStruct(shape, kind) for s...]
    while x25 -> x0, local copies, waits for them, and re-layouts: 14.5 us -> none
  transfers between devices with their start and end apart: 4 -> 17, of which waited for: 4 -> 10; matrix products, arithmetic and copies ran while one was open for 2% -> 0% of each run, Pallas kernels for 0% -> 11%
where the time goes in v2:
time: 75 us; the launch traced here: 74.7 us
  starting transfers between devices  31 us (41%)
  waiting for transfers between devices  24.1 us (32%)
  Pallas kernels  16.7 us (22%)
  local copies, waits for them, and re-layouts  2.16 us (3%)
  between operations  0.76 us (1%)
    pallas_call x7, Pallas kernels, call(): pl.pallas_call(kernel, out_shape=[jax.ShapeDtypeStruct(shape, kind) for s...  16.7 us
    ppermute x1, waiting for transfers between devices, per_device(): two = lax.ppermute(mine, BOTH, z_apart(2))  6.4 us
    ppermute x3, starting transfers between devices, per_device(): lax.ppermute(part, 'dp', x_shift(d))  5.74 us
    ppermute x3, starting transfers between devices, per_device(): lax.ppermute(part, BOTH, y_shift(d))  5.65 us
    ppermute x3, waiting for transfers between devices, per_device(): lax.ppermute(part, BOTH, y_shift(d))  5.52 us
    ppermute x1, starting transfers between devices, per_device(): two_back = lax.ppermute(mine, BOTH, z_apart(-2))  5.4 us
    all_to_all x1, starting transfers between devices, per_device(): lax.all_to_all(back, 'task', 0, 0, tiled=True, axis_index_groups=column_g...  5.4 us
    ppermute x1, waiting for transfers between devices, per_device(): three_back = lax.ppermute(two_back, BOTH, z_apart(-1))  4.35 us
  transfers between devices with their start and end apart: 17, of which 10 were waited for; matrix products, arithmetic and copies ran while one was open for 0% of the time, Pallas kernels for 11%

profile of v2, /device:TPU:32, one launch (start us, length us, event | category | flops | bytes accessed | tf_op | source)
XLA Modules:
  0.0 74.7 jit_solution(10370982693346586030)
XLA Ops:
  0.6 3.3 %collective-permute-start.7 = (bf16[512,512]{1,0:T(8,128)(2,1)}, bf16[512,512]{1,0:T(8,128)(2,1)S(1)}, u32[]{:S(2)}, u32[]{:S(2)}) collective-permute-start(bf16[512,512]{1,0:T(8,128)(2,1)} %refs_8_.1), channel_id=1, source_target_pairs={{0,1},{1,0},{2,3},{3,2},{4,5},{5,4},{6,7},{7,6},{8,9},{9,8},{10,11... | collective-permute-start | bytes 1572872 | tf_op jit(solution)/shard_map/ppermute | solution.py:290
  3.9 5.4 %collective-permute-start.3 = (bf16[128,512]{1,0:T(8,128)(2,1)}, bf16[128,512]{1,0:T(8,128)(2,1)S(1)}, u32[]{:S(2)}, u32[]{:S(2)}) collective-permute-start(bf16[128,512]{1,0:T(8,128)(2,1)} %bitcast.8), channel_id=1, source_target_pairs={{0,12},{1,13},{2,14},{3,15},{4,0},{5,1},{6,2},{7,3},{8,4},{9,5},{1... | collective-permute-start | bytes 393224 | tf_op jit(solution)/shard_map/ppermute | solution.py:292
  9.3 2.1 %pack_events.1 = (f32[152,512]{1,0:T(8,128)}, f32[136,512]{1,0:T(8,128)}) custom-call(s32[2,4]{1,0:T(2,128)} %risk_ref.1, s32[9]{0:T(128)} %bounds_ref.1, s32[256,512]{1,0:T(8,128)} %time_ref.1, s32[256,512]{1,0:T(8,128)} %cens_ref.1, f32[8,512]{1,0:T(8,128)} %bitcast.15), custom_call_target="tpu_custom_call" | custom-call | tf_op jit(solution)/shard_map/pack_events/pallas_call | solution.py:69
  11.5 0.3 collective-permute-start.8
  11.8 0.0 collective-permute-start.2
  11.8 1.0 %collective-permute-start.1 = (bf16[128,512]{1,0:T(8,128)(2,1)}, bf16[128,512]{1,0:T(8,128)(2,1)S(1)}, u32[]{:S(2)}, u32[]{:S(2)}) collective-permute-start(bf16[128,512]{1,0:T(8,128)(2,1)} %bitcast.10), channel_id=1, source_target_pairs={{0,14},{1,15},{2,0},{3,1},{4,2},{5,3},{6,4},{7,5},{8,6},{9,7},{10,... | collective-permute-start | bytes 393224 | tf_op jit(solution)/shard_map/ppermute | solution.py:306
  12.8 0.4 collective-permute-done.3.refs_4_
  13.2 0.0 copy-start.2
  13.2 1.8 %collective-permute-start = (bf16[128,512]{1,0:T(8,128)(2,1)}, bf16[128,512]{1,0:T(8,128)(2,1)S(1)}, u32[]{:S(2)}, u32[]{:S(2)}) collective-permute-start(bf16[128,512]{1,0:T(8,128)(2,1)} %bitcast.11), channel_id=1, source_target_pairs={{0,2},{1,3},{2,4},{3,5},{4,6},{5,7},{6,8},{7,9},{8,10},{9,11},{10,... | collective-permute-start | bytes 393224 | tf_op jit(solution)/shard_map/ppermute | solution.py:305
  15.0 6.4 %collective-permute-done.2.refs_3_ = bf16[128,512]{1,0:T(8,128)(2,1)S(1)} collective-permute-done((bf16[128,512]{1,0:T(8,128)(2,1)}, bf16[128,512]{1,0:T(8,128)(2,1)S(1)}, u32[]{:S(2)}, u32[]{:S(2)}) %collective-permute-start.2) | collective-permute-done | bytes 131104 | tf_op jit(solution)/shard_map/ppermute | solution.py:291
  21.4 0.0 copy-start.3
  21.4 0.9 %collective-permute-start.5 = (bf16[128,512]{1,0:T(8,128)(2,1)S(1)}, bf16[128,512]{1,0:T(8,128)(2,1)S(1)}, u32[]{:S(2)}, u32[]{:S(2)}) collective-permute-start(bf16[128,512]{1,0:T(8,128)(2,1)S(1)} %collective-permute-done.3.refs_4_), channel_id=1, source_target_pairs={{0,14},{1,15},{2,0},{3,1},{4,2},{5,3},{6,4},{7,5},{8,6},{9,7},{10,... | collective-permute-start | bytes 393224 | tf_op jit(solution)/shard_map/ppermute | solution.py:303
  22.2 0.0 collective-permute-done.1.refs_2_
  22.2 0.0 copy-start.4
  22.2 0.0 collective-permute-start.6
  22.3 0.0 collective-permute-done.refs_1_
  22.3 0.0 copy-start.5
  22.3 1.4 %collective-permute-start.4 = (bf16[128,512]{1,0:T(8,128)(2,1)S(1)}, bf16[128,512]{1,0:T(8,128)(2,1)S(1)}, u32[]{:S(2)}, u32[]{:S(2)}) collective-permute-start(bf16[128,512]{1,0:T(8,128)(2,1)S(1)} %collective-permute-done.2.refs_3_), channel_id=1, source_target_pairs={{0,2},{1,3},{2,4},{3,5},{4,6},{5,7},{6,8},{7,9},{8,10},{9,11},{10,... | collective-permute-start | bytes 393224 | tf_op jit(solution)/shard_map/ppermute | solution.py:302
  23.7 4.3 %collective-permute-done.5.refs_6_ = bf16[128,512]{1,0:T(8,128)(2,1)S(1)} collective-permute-done((bf16[128,512]{1,0:T(8,128)(2,1)S(1)}, bf16[128,512]{1,0:T(8,128)(2,1)S(1)}, u32[]{:S(2)}, u32[]{:S(2)}) %collective-permute-start.5) | collective-permute-done | bytes 131104 | tf_op jit(solution)/shard_map/ppermute | solution.py:303
  28.0 0.0 copy-start.6
  28.0 1.8 %collective-permute-done.6.refs_7_ = bf16[128,512]{1,0:T(8,128)(2,1)S(1)} collective-permute-done((bf16[128,512]{1,0:T(8,128)(2,1)S(1)}, bf16[128,512]{1,0:T(8,128)(2,1)S(1)}, u32[]{:S(2)}, u32[]{:S(2)}) %collective-permute-start.6) | collective-permute-done | bytes 131104 | tf_op jit(solution)/shard_map/ppermute | solution.py:304
  29.8 0.0 copy-start.7
  29.8 0.9 %collective-permute-done.4.refs_5_ = bf16[128,512]{1,0:T(8,128)(2,1)S(1)} collective-permute-done((bf16[128,512]{1,0:T(8,128)(2,1)S(1)}, bf16[128,512]{1,0:T(8,128)(2,1)S(1)}, u32[]{:S(2)}, u32[]{:S(2)}) %collective-permute-start.4) | collective-permute-done | bytes 131104 | tf_op jit(solution)/shard_map/ppermute | solution.py:302
  30.7 0.0 copy-start.8
  30.7 0.0 collective-permute-done.8.refs_11_
  30.7 0.0 copy-start.9
  30.7 0.0 collective-permute-done.7.refs_9_
  30.7 0.0 copy-start.1
  30.7 0.0 copy-done.2
  30.7 0.0 copy-done.3
  30.7 0.0 copy-done.4
  30.7 0.0 copy-done.5
  30.7 0.0 copy-done.6
  30.7 0.0 copy-done.7
  30.8 0.6 copy-done.8
  31.3 0.1 copy-done.9
  31.5 0.2 copy-done.1
  31.7 7.5 %terms.1 = (bf16[1024,512]{1,0:T(8,128)(2,1)}, bf16[1024,1024]{1,0:T(8,128)(2,1)}, f32[8,1024]{1,0:T(8,128)}) custom-call(bf16[128,512]{1,0:T(8,128)(2,1)} %bitcast.12, bf16[128,512]{1,0:T(8,128)(2,1)} %copy-done.5, bf16[128,512]{1,0:T(8,128)(2,1)} %copy-done.4, bf16[128,512]{1,0:T(8,128)(2,1)} %copy-done.3, bf16[128,512]{1,0:T(8,128)(2,1)} %copy-done.2, ...), custom_call_target="tpu_custom_call" | custom-call | tf_op jit(solution)/shard_map/terms/pallas_call | solution.py:69
  39.1 5.4 %all-to-all-start = ((bf16[8,128,512]{2,1,0:T(8,128)(2,1)}), bf16[8,128,512]{2,1,0:T(8,128)(2,1)S(1)}, u32[]{:S(2)}, u32[]{:S(2)}) async-start(bf16[8,128,512]{2,1,0:T(8,128)(2,1)} %bitcast.7), calls=%async_computation | async-start | bytes 2097152 | tf_op jit(solution)/shard_map/all_to_all | solution.py:326
  44.5 5.4 %emb_terms.1 = (f32[528,512]{1,0:T(8,128)}, bf16[544,512]{1,0:T(8,128)(2,1)}) custom-call(bf16[128,512]{1,0:T(8,128)(2,1)} %bitcast.13, bf16[128,512]{1,0:T(8,128)(2,1)} %copy-done.5, bf16[128,512]{1,0:T(8,128)(2,1)} %copy-done.4, bf16[128,512]{1,0:T(8,128)(2,1)} %copy-done.3, bf16[128,512]{1,0:T(8,128)(2,1)} %copy-done.2, bf16[128,512]{1,0:T(8,128)(2,1)} %copy-done.8, ...), custom_call_target="tpu_custom_call" | custom-call | tf_op jit(solution)/shard_map/emb_terms/pallas_call | solution.py:69
  50.0 0.1 collective-permute-start.9
  50.0 2.2 %collective-permute-done.9.got_ref = bf16[544,512]{1,0:T(8,128)(2,1)S(1)} collective-permute-done((bf16[544,512]{1,0:T(8,128)(2,1)}, bf16[544,512]{1,0:T(8,128)(2,1)S(1)}, u32[]{:S(2)}, u32[]{:S(2)}) %collective-permute-start.9) | collective-permute-done | bytes 557088 | tf_op jit(solution)/shard_map/ppermute | solution.py:341
  52.2 0.0 copy-start
  52.2 1.2 %copy-done = f32[528,512]{1,0:T(8,128)S(1)} copy-done((f32[528,512]{1,0:T(8,128)S(1)}, f32[528,512]{1,0:T(8,128)}, u32[]{:S(2)}) %copy-start) | copy-done | bytes 1081368
  53.4 0.1 join_cores.1
  53.6 1.1 %collective-permute-start.10 = (bf16[144,512]{1,0:T(8,128)(2,1)S(1)}, bf16[144,512]{1,0:T(8,128)(2,1)S(1)}, u32[]{:S(2)}, u32[]{:S(2)}) collective-permute-start(bf16[144,512]{1,0:T(8,128)(2,1)S(1)} %get-tuple-element.28), channel_id=1, source_target_pairs={{0,128},{2,130},{4,132},{6,134},{8,136},{10,138},{12,140},{14,142}... | collective-permute-start | bytes 442376 | tf_op jit(solution)/shard_map/ppermute | solution.py:345
  54.7 3.0 %collective-permute-start.11 = (bf16[144,512]{1,0:T(8,128)(2,1)S(1)}, bf16[144,512]{1,0:T(8,128)(2,1)S(1)}, u32[]{:S(2)}, u32[]{:S(2)}) collective-permute-start(bf16[144,512]{1,0:T(8,128)(2,1)S(1)} %get-tuple-element.29), channel_id=1, source_target_pairs={{0,1},{2,3},{4,5},{6,7},{8,9},{10,11},{12,13},{14,15},{16,17},{18,... | collective-permute-start | bytes 442376 | tf_op jit(solution)/shard_map/ppermute | solution.py:345
  57.7 1.5 %collective-permute-start.12 = (bf16[144,512]{1,0:T(8,128)(2,1)S(1)}, bf16[144,512]{1,0:T(8,128)(2,1)S(1)}, u32[]{:S(2)}, u32[]{:S(2)}) collective-permute-start(bf16[144,512]{1,0:T(8,128)(2,1)S(1)} %get-tuple-element.30), channel_id=1, source_target_pairs={{0,129},{2,131},{4,133},{6,135},{8,137},{10,139},{12,141},{14,143}... | collective-permute-start | bytes 442376 | tf_op jit(solution)/shard_map/ppermute | solution.py:345
  59.2 1.5 %collective-permute-done.10.refs_1_ = bf16[144,512]{1,0:T(8,128)(2,1)S(1)} collective-permute-done((bf16[144,512]{1,0:T(8,128)(2,1)S(1)}, bf16[144,512]{1,0:T(8,128)(2,1)S(1)}, u32[]{:S(2)}, u32[]{:S(2)}) %collective-permute-start.10) | collective-permute-done | bytes 147488 | tf_op jit(solution)/shard_map/ppermute | solution.py:345
  60.7 4.0 %collective-permute-done.11.refs_2_ = bf16[144,512]{1,0:T(8,128)(2,1)S(1)} collective-permute-done((bf16[144,512]{1,0:T(8,128)(2,1)S(1)}, bf16[144,512]{1,0:T(8,128)(2,1)S(1)}, u32[]{:S(2)}, u32[]{:S(2)}) %collective-permute-start.11) | collective-permute-done | bytes 147488 | tf_op jit(solution)/shard_map/ppermute | solution.py:345
  64.7 0.0 collective-permute-done.12.refs_3_
  64.7 0.1 sum_y.1
  64.8 1.6 %collective-permute-start.13 = (bf16[48,512]{1,0:T(8,128)(2,1)S(1)}, bf16[48,512]{1,0:T(8,128)(2,1)S(1)}, u32[]{:S(2)}, u32[]{:S(2)}) collective-permute-start(bf16[48,512]{1,0:T(8,128)(2,1)S(1)} %get-tuple-element.32), channel_id=1, source_target_pairs={{0,32},{16,48},{32,64},{48,80},{64,96},{80,112},{96,0},{112,16},{1... | collective-permute-start | bytes 147464 | tf_op jit(solution)/shard_map/ppermute | solution.py:353
  66.4 2.7 %collective-permute-start.14 = (bf16[48,512]{1,0:T(8,128)(2,1)S(1)}, bf16[48,512]{1,0:T(8,128)(2,1)S(1)}, u32[]{:S(2)}, u32[]{:S(2)}) collective-permute-start(bf16[48,512]{1,0:T(8,128)(2,1)S(1)} %get-tuple-element.33), channel_id=1, source_target_pairs={{0,64},{16,80},{32,96},{48,112},{64,0},{80,16},{96,32},{112,48},{1... | collective-permute-start | bytes 147464 | tf_op jit(solution)/shard_map/ppermute | solution.py:353
  69.1 1.4 %collective-permute-start.15 = (bf16[48,512]{1,0:T(8,128)(2,1)S(1)}, bf16[48,512]{1,0:T(8,128)(2,1)S(1)}, u32[]{:S(2)}, u32[]{:S(2)}) collective-permute-start(bf16[48,512]{1,0:T(8,128)(2,1)S(1)} %get-tuple-element.34), channel_id=1, source_target_pairs={{0,96},{16,112},{32,0},{48,16},{64,32},{80,48},{96,64},{112,80},{1... | collective-permute-start | bytes 147464 | tf_op jit(solution)/shard_map/ppermute | solution.py:353
  70.6 0.0 collective-permute-done.13.refs_1_
  70.6 1.4 %collective-permute-done.14.refs_2_ = bf16[48,512]{1,0:T(8,128)(2,1)S(1)} collective-permute-done((bf16[48,512]{1,0:T(8,128)(2,1)S(1)}, bf16[48,512]{1,0:T(8,128)(2,1)S(1)}, u32[]{:S(2)}, u32[]{:S(2)}) %collective-permute-start.14) | collective-permute-done | bytes 49184 | tf_op jit(solution)/shard_map/ppermute | solution.py:353
  72.0 1.2 %collective-permute-done.15.refs_3_ = bf16[48,512]{1,0:T(8,128)(2,1)S(1)} collective-permute-done((bf16[48,512]{1,0:T(8,128)(2,1)S(1)}, bf16[48,512]{1,0:T(8,128)(2,1)S(1)}, u32[]{:S(2)}, u32[]{:S(2)}) %collective-permute-start.15) | collective-permute-done | bytes 49184 | tf_op jit(solution)/shard_map/ppermute | solution.py:353
  73.2 0.7 sum_x.1
  73.9 0.0 all-to-all-done
  73.9 0.8 %sum_returned.1 = bf16[128,512]{1,0:T(8,128)(2,1)} custom-call(bf16[1024,512]{1,0:T(8,128)(2,1)S(1)} %bitcast.6), custom_call_target="tpu_custom_call" | custom-call | tf_op jit(solution)/shard_map/sum_returned/pallas_call | solution.py:69
Async XLA Ops:
  0.6 30.1 %collective-permute-start.7 = (bf16[512,512]{1,0:T(8,128)(2,1)}, bf16[512,512]{1,0:T(8,128)(2,1)S(1)}, u32[]{:S(2)}, u32[]{:S(2)}) collective-permute-start(bf16[512,512]{1,0:T(8,128)(2,1)} %refs_8_.1), channel_id=1, source_target_pairs={{0,1},{1,0},{2,3},{3,2},{4,5},{5,4},{6,7},{7,6},{8,9},{9,8},{10,11... | collective-permute-start | bytes 1572872 | tf_op jit(solution)/shard_map/ppermute | solution.py:290
  3.9 9.2 %collective-permute-start.3 = (bf16[128,512]{1,0:T(8,128)(2,1)}, bf16[128,512]{1,0:T(8,128)(2,1)S(1)}, u32[]{:S(2)}, u32[]{:S(2)}) collective-permute-start(bf16[128,512]{1,0:T(8,128)(2,1)} %bitcast.8), channel_id=1, source_target_pairs={{0,12},{1,13},{2,14},{3,15},{4,0},{5,1},{6,2},{7,3},{8,4},{9,5},{1... | collective-permute-start | bytes 393224 | tf_op jit(solution)/shard_map/ppermute | solution.py:292
  11.5 19.2 %collective-permute-start.8 = (f32[136,512]{1,0:T(8,128)}, f32[136,512]{1,0:T(8,128)S(1)}, u32[]{:S(2)}, u32[]{:S(2)}) collective-permute-start(f32[136,512]{1,0:T(8,128)} %get-tuple-element.21), channel_id=1, source_target_pairs={{0,1},{1,0},{2,3},{3,2},{4,5},{5,4},{6,7},{7,6},{8,9},{9,8},{10,11... | collective-permute-start | bytes 835592 | tf_op jit(solution)/shard_map/ppermute | solution.py:301
  11.8 9.6 %collective-permute-start.2 = (bf16[128,512]{1,0:T(8,128)(2,1)}, bf16[128,512]{1,0:T(8,128)(2,1)S(1)}, u32[]{:S(2)}, u32[]{:S(2)}) collective-permute-start(bf16[128,512]{1,0:T(8,128)(2,1)} %bitcast.9), channel_id=1, source_target_pairs={{0,4},{1,5},{2,6},{3,7},{4,8},{5,9},{6,10},{7,11},{8,12},{9,13},{1... | collective-permute-start | bytes 393224 | tf_op jit(solution)/shard_map/ppermute | solution.py:291
  11.8 10.4 %collective-permute-start.1 = (bf16[128,512]{1,0:T(8,128)(2,1)}, bf16[128,512]{1,0:T(8,128)(2,1)S(1)}, u32[]{:S(2)}, u32[]{:S(2)}) collective-permute-start(bf16[128,512]{1,0:T(8,128)(2,1)} %bitcast.10), channel_id=1, source_target_pairs={{0,14},{1,15},{2,0},{3,1},{4,2},{5,3},{6,4},{7,5},{8,6},{9,7},{10,... | collective-permute-start | bytes 393224 | tf_op jit(solution)/shard_map/ppermute | solution.py:306
  13.2 17.5 %copy-start.2 = (bf16[128,512]{1,0:T(8,128)(2,1)}, bf16[128,512]{1,0:T(8,128)(2,1)S(1)}, u32[]{:S(2)}) copy-start(bf16[128,512]{1,0:T(8,128)(2,1)S(1)} %collective-permute-done.3.refs_4_) | copy-start | bytes 393220
  13.2 9.1 %collective-permute-start = (bf16[128,512]{1,0:T(8,128)(2,1)}, bf16[128,512]{1,0:T(8,128)(2,1)S(1)}, u32[]{:S(2)}, u32[]{:S(2)}) collective-permute-start(bf16[128,512]{1,0:T(8,128)(2,1)} %bitcast.11), channel_id=1, source_target_pairs={{0,2},{1,3},{2,4},{3,5},{4,6},{5,7},{6,8},{7,9},{8,10},{9,11},{10,... | collective-permute-start | bytes 393224 | tf_op jit(solution)/shard_map/ppermute | solution.py:305
  21.4 9.3 %copy-start.3 = (bf16[128,512]{1,0:T(8,128)(2,1)}, bf16[128,512]{1,0:T(8,128)(2,1)S(1)}, u32[]{:S(2)}) copy-start(bf16[128,512]{1,0:T(8,128)(2,1)S(1)} %collective-permute-done.2.refs_3_) | copy-start | bytes 393220
  21.4 6.6 %collective-permute-start.5 = (bf16[128,512]{1,0:T(8,128)(2,1)S(1)}, bf16[128,512]{1,0:T(8,128)(2,1)S(1)}, u32[]{:S(2)}, u32[]{:S(2)}) collective-permute-start(bf16[128,512]{1,0:T(8,128)(2,1)S(1)} %collective-permute-done.3.refs_4_), channel_id=1, source_target_pairs={{0,14},{1,15},{2,0},{3,1},{4,2},{5,3},{6,4},{7,5},{8,6},{9,7},{10,... | collective-permute-start | bytes 393224 | tf_op jit(solution)/shard_map/ppermute | solution.py:303
  22.2 8.5 %copy-start.4 = (bf16[128,512]{1,0:T(8,128)(2,1)}, bf16[128,512]{1,0:T(8,128)(2,1)S(1)}, u32[]{:S(2)}) copy-start(bf16[128,512]{1,0:T(8,128)(2,1)S(1)} %collective-permute-done.1.refs_2_) | copy-start | bytes 393220
  22.2 7.6 %collective-permute-start.6 = (bf16[128,512]{1,0:T(8,128)(2,1)S(1)}, bf16[128,512]{1,0:T(8,128)(2,1)S(1)}, u32[]{:S(2)}, u32[]{:S(2)}) collective-permute-start(bf16[128,512]{1,0:T(8,128)(2,1)S(1)} %collective-permute-done.2.refs_3_), channel_id=1, source_target_pairs={{0,4},{1,5},{2,6},{3,7},{4,8},{5,9},{6,10},{7,11},{8,12},{9,13},{1... | collective-permute-start | bytes 393224 | tf_op jit(solution)/shard_map/ppermute | solution.py:304
  22.3 8.5 %copy-start.5 = (bf16[128,512]{1,0:T(8,128)(2,1)}, bf16[128,512]{1,0:T(8,128)(2,1)S(1)}, u32[]{:S(2)}) copy-start(bf16[128,512]{1,0:T(8,128)(2,1)S(1)} %collective-permute-done.refs_1_) | copy-start | bytes 393220
  22.3 8.4 %collective-permute-start.4 = (bf16[128,512]{1,0:T(8,128)(2,1)S(1)}, bf16[128,512]{1,0:T(8,128)(2,1)S(1)}, u32[]{:S(2)}, u32[]{:S(2)}) collective-permute-start(bf16[128,512]{1,0:T(8,128)(2,1)S(1)} %collective-permute-done.2.refs_3_), channel_id=1, source_target_pairs={{0,2},{1,3},{2,4},{3,5},{4,6},{5,7},{6,8},{7,9},{8,10},{9,11},{10,... | collective-permute-start | bytes 393224 | tf_op jit(solution)/shard_map/ppermute | solution.py:302
  28.0 2.7 %copy-start.6 = (bf16[128,512]{1,0:T(8,128)(2,1)}, bf16[128,512]{1,0:T(8,128)(2,1)S(1)}, u32[]{:S(2)}) copy-start(bf16[128,512]{1,0:T(8,128)(2,1)S(1)} %collective-permute-done.5.refs_6_) | copy-start | bytes 393220
  29.8 0.9 %copy-start.7 = (bf16[128,512]{1,0:T(8,128)(2,1)}, bf16[128,512]{1,0:T(8,128)(2,1)S(1)}, u32[]{:S(2)}) copy-start(bf16[128,512]{1,0:T(8,128)(2,1)S(1)} %collective-permute-done.6.refs_7_) | copy-start | bytes 393220
  30.7 0.7 copy-start.8
  30.7 0.8 %copy-start.9 = (f32[136,512]{1,0:T(8,128)}, f32[136,512]{1,0:T(8,128)S(1)}, u32[]{:S(2)}) copy-start(f32[136,512]{1,0:T(8,128)S(1)} %collective-permute-done.8.refs_11_) | copy-start | bytes 835588
  30.7 1.0 %copy-start.1 = (bf16[512,512]{1,0:T(8,128)(2,1)}, bf16[512,512]{1,0:T(8,128)(2,1)S(1)}, u32[]{:S(2)}) copy-start(bf16[512,512]{1,0:T(8,128)(2,1)S(1)} %collective-permute-done.7.refs_9_) | copy-start | bytes 1572868
  39.1 34.8 %all-to-all-start = ((bf16[8,128,512]{2,1,0:T(8,128)(2,1)}), bf16[8,128,512]{2,1,0:T(8,128)(2,1)S(1)}, u32[]{:S(2)}, u32[]{:S(2)}) async-start(bf16[8,128,512]{2,1,0:T(8,128)(2,1)} %bitcast.7), calls=%async_computation | async-start | bytes 2097152 | tf_op jit(solution)/shard_map/all_to_all | solution.py:326
  50.0 2.3 %collective-permute-start.9 = (bf16[544,512]{1,0:T(8,128)(2,1)}, bf16[544,512]{1,0:T(8,128)(2,1)S(1)}, u32[]{:S(2)}, u32[]{:S(2)}) collective-permute-start(bf16[544,512]{1,0:T(8,128)(2,1)} %get-tuple-element.26), channel_id=1, source_target_pairs={{0,16},{16,0},{32,48},{48,32},{64,80},{80,64},{96,112},{112,96},{1... | collective-permute-start | bytes 1671176 | tf_op jit(solution)/shard_map/ppermute | solution.py:341
  52.2 1.2 %copy-start = (f32[528,512]{1,0:T(8,128)S(1)}, f32[528,512]{1,0:T(8,128)}, u32[]{:S(2)}) copy-start(f32[528,512]{1,0:T(8,128)} %get-tuple-element.25.keep_ref) | copy-start | bytes 3244036
  53.6 7.2 %collective-permute-start.10 = (bf16[144,512]{1,0:T(8,128)(2,1)S(1)}, bf16[144,512]{1,0:T(8,128)(2,1)S(1)}, u32[]{:S(2)}, u32[]{:S(2)}) collective-permute-start(bf16[144,512]{1,0:T(8,128)(2,1)S(1)} %get-tuple-element.28), channel_id=1, source_target_pairs={{0,128},{2,130},{4,132},{6,134},{8,136},{10,138},{12,140},{14,142}... | collective-permute-start | bytes 442376 | tf_op jit(solution)/shard_map/ppermute | solution.py:345
  54.7 10.0 %collective-permute-start.11 = (bf16[144,512]{1,0:T(8,128)(2,1)S(1)}, bf16[144,512]{1,0:T(8,128)(2,1)S(1)}, u32[]{:S(2)}, u32[]{:S(2)}) collective-permute-start(bf16[144,512]{1,0:T(8,128)(2,1)S(1)} %get-tuple-element.29), channel_id=1, source_target_pairs={{0,1},{2,3},{4,5},{6,7},{8,9},{10,11},{12,13},{14,15},{16,17},{18,... | collective-permute-start | bytes 442376 | tf_op jit(solution)/shard_map/ppermute | solution.py:345
  57.7 7.0 %collective-permute-start.12 = (bf16[144,512]{1,0:T(8,128)(2,1)S(1)}, bf16[144,512]{1,0:T(8,128)(2,1)S(1)}, u32[]{:S(2)}, u32[]{:S(2)}) collective-permute-start(bf16[144,512]{1,0:T(8,128)(2,1)S(1)} %get-tuple-element.30), channel_id=1, source_target_pairs={{0,129},{2,131},{4,133},{6,135},{8,137},{10,139},{12,141},{14,143}... | collective-permute-start | bytes 442376 | tf_op jit(solution)/shard_map/ppermute | solution.py:345
  64.8 5.8 %collective-permute-start.13 = (bf16[48,512]{1,0:T(8,128)(2,1)S(1)}, bf16[48,512]{1,0:T(8,128)(2,1)S(1)}, u32[]{:S(2)}, u32[]{:S(2)}) collective-permute-start(bf16[48,512]{1,0:T(8,128)(2,1)S(1)} %get-tuple-element.32), channel_id=1, source_target_pairs={{0,32},{16,48},{32,64},{48,80},{64,96},{80,112},{96,0},{112,16},{1... | collective-permute-start | bytes 147464 | tf_op jit(solution)/shard_map/ppermute | solution.py:353
  66.4 5.6 %collective-permute-start.14 = (bf16[48,512]{1,0:T(8,128)(2,1)S(1)}, bf16[48,512]{1,0:T(8,128)(2,1)S(1)}, u32[]{:S(2)}, u32[]{:S(2)}) collective-permute-start(bf16[48,512]{1,0:T(8,128)(2,1)S(1)} %get-tuple-element.33), channel_id=1, source_target_pairs={{0,64},{16,80},{32,96},{48,112},{64,0},{80,16},{96,32},{112,48},{1... | collective-permute-start | bytes 147464 | tf_op jit(solution)/shard_map/ppermute | solution.py:353
  69.1 4.1 %collective-permute-start.15 = (bf16[48,512]{1,0:T(8,128)(2,1)S(1)}, bf16[48,512]{1,0:T(8,128)(2,1)S(1)}, u32[]{:S(2)}, u32[]{:S(2)}) collective-permute-start(bf16[48,512]{1,0:T(8,128)(2,1)S(1)} %get-tuple-element.34), channel_id=1, source_target_pairs={{0,96},{16,112},{32,0},{48,16},{64,32},{80,48},{96,64},{112,80},{1... | collective-permute-start | bytes 147464 | tf_op jit(solution)/shard_map/ppermute | solution.py:353

commit v3 on v2

--- a/solution.py
+++ b/solution.py
@@ -99,9 +99,16 @@
         own_ref[136 + k * 8 : 144 + k * 8, :] = edge.astype(jnp.float32) * time_unit
 
 
+def split_sums(sums):
+    high = sums.astype(jnp.bfloat16)
+    rest = (sums - high.astype(jnp.float32)).astype(jnp.bfloat16)
+    return jnp.concatenate([high, rest], axis=0)
+
+
 def grad_kernel(*refs):
     chunks, refs = refs[:8], refs[8:]
-    e0, e1, p0, p1, back_ref, low_out, bin_ref, feats, embs, events, backs, low_ref, sems = refs
+    e0, e1, p0, p1, back_out, low_out, feat_out, bin_ref = refs[:8]
+    feats, embs, events, lows, backs, sems = refs[8:]
     z, core, _ = place()
 
     def fetch(source, target, slot):
@@ -109,30 +116,40 @@
         copy.start()
         return copy
 
+    first = [
+        fetch(e0, embs.at[pl.ds(0, 512)], 8),
+        fetch(p0, events.at[pl.ds(0, 152)], 9),
+    ]
     copies = [
         fetch(chunk, feats.at[pl.ds(slot * ROWS, ROWS)], slot)
         for slot, chunk in enumerate(chunks)
     ]
-    copies.append(fetch(e0, embs.at[pl.ds(0, 512)], 8))
-    copies.append(fetch(p0, events.at[pl.ds(0, 152)], 9))
-    copies.append(fetch(e1, embs.at[pl.ds(512, 512)], 10))
-    copies.append(fetch(p1, events.at[pl.ds(152, 136)], 11))
-
+    second = [
+        fetch(e1, embs.at[pl.ds(512, 512)], 10),
+        fetch(p1, events.at[pl.ds(152, 136)], 11),
+    ]
     way = 1 - 2 * core
     shifts = (0, 1, -1, 2 * way, -2 * way, 3 * way, -3 * way, 4)
     owners = [lax.rem(z + (NZ - shift), NZ) for shift in shifts]
-    for copy in copies:
+    for copy in first:
         copy.wait()
     lower, upper = events[136:144, :], events[144:152, :]
     span = upper - lower
 
     def step(i, carry):
-        out = pl.ds(pl.multiple_of(i * WIDE, WIDE), WIDE)
+        out = pl.ds(i * WIDE, WIDE)
+        if i == 1:
+            for copy in second:
+                copy.wait()
+
         emb = embs[out, :]
         base = i * 152
-        bias = events[pl.ds(pl.multiple_of(base + 128, 8), 8), :]
+        bias = events[base + 128 : base + 136, :]
         g_bin = jnp.zeros((8, WIDE), jnp.float32)
         for part in range(4):
+            if i == 0:
+                copies[2 * part].wait()
+                copies[2 * part + 1].wait()
             logit = lax.dot_general(
                 feats[part * 256 : (part + 1) * 256, :],
                 emb,
@@ -149,58 +166,37 @@
                 inside = (signed > lower[None]) & (signed <= upper[None])
                 dlogit = exposure * jnp.exp(piece) - inside.astype(jnp.float32)
                 g_bin = g_bin + jnp.sum(dlogit, axis=0)
-                low_ref[slot * ROWS : (slot + 1) * ROWS, out] = dlogit.reshape(ROWS, WIDE).astype(
+                lows[slot * ROWS : (slot + 1) * ROWS, out] = dlogit.reshape(ROWS, WIDE).astype(
                     jnp.bfloat16
                 )
         bin_ref[:, out] = g_bin
         return carry
 
-    lax.fori_loop(0, 2, step, 0)
-    sent = [fetch(low_ref, low_out, 8)]
+    stored = []
+    for i in range(2):
+        step(i, 0)
+        if i == 0:
+            stored.append(fetch(feats, feat_out, 14))
+        half = pl.ds(i * WIDE, WIDE)
+        stored.append(fetch(lows.at[:, half], low_out.at[:, half], 12 + i))
+    sent = []
     for slot in range(0, 8, 2):
-        both = jnp.dot(
-            low_ref[slot * ROWS : (slot + 2) * ROWS, :],
+        backs[slot * ROWS : (slot + 2) * ROWS, :] = jnp.dot(
+            lows[slot * ROWS : (slot + 2) * ROWS, :],
             embs[...],
             preferred_element_type=jnp.float32,
         ).astype(jnp.bfloat16)
-        backs[slot * ROWS : (slot + 2) * ROWS, :] = both
         for one in (slot, slot + 1):
             source = backs.at[pl.ds(one * ROWS, ROWS)]
-            target = back_ref.at[pl.ds(pl.multiple_of(owners[one] * ROWS, ROWS), ROWS)]
+            target = back_out.at[pl.ds(pl.multiple_of(owners[one] * ROWS, ROWS), ROWS)]
             sent.append(fetch(source, target, one))
-    for copy in sent:
+    for copy in stored + sent:
         copy.wait()
 
 
-def split_sums(sums):
-    high = sums.astype(jnp.bfloat16)
-    rest = (sums - high.astype(jnp.float32)).astype(jnp.bfloat16)
-    return jnp.concatenate([high, rest], axis=0)
-
-
-def emb_kernel(*refs):
-    chunks, refs = refs[:8], refs[8:]
-    low_in, bin_ref, keep_ref, send_ref, feats, low_ref, sems = refs
-    copies = []
-    for slot, chunk in enumerate(chunks):
-        copy = pltpu.make_async_copy(
-            chunk, feats.at[pl.ds(slot * ROWS, ROWS)], sems.at[slot]
-        )
-        copy.start()
-        copies.append(copy)
-    blocks = []
+def emb_kernel(low_ref, feats, bin_ref, keep_ref, send_ref):
+    _, core, h = place()
     for i in range(4):
-        part = pl.ds(i * 256, 256)
-        blocks.append(
-            pltpu.make_async_copy(low_in.at[:, part], low_ref.at[:, part], sems.at[8 + i])
-        )
-        blocks[i].start()
-    for copy in copies:
-        copy.wait()
-    _, core, h = place()
-
-    for i in range(4):
-        blocks[i].wait()
         g_emb = lax.dot_general(
             low_ref[:, i * 256 : (i + 1) * 256],
             feats[...],
@@ -213,7 +209,6 @@
         spot = pl.ds(pl.multiple_of(there * 128, 128), 128)
         keep_ref[spot, :] = jnp.where(core == 0, zero, one)
         send_ref[spot, :] = jnp.where(core == 0, one, zero).astype(jnp.bfloat16)
-
     for side in range(2):
         sums = bin_ref[:, side * 512 : (side + 1) * 512]
         there = h if side == 0 else 1 - h
@@ -306,37 +301,27 @@
     one_back = lax.ppermute(mine, "task", z_shift(-1))
     chunks = (mine, one, one_back, two, two_back, three, three_back, four)
 
-    back, lows, g_bin = call(
+    back, lows, gathered, g_bin = call(
         grad_kernel,
         "terms",
-        [((1024, 512), low), ((1024, 1024), low), ((8, 1024), wide)],
+        [((1024, 512), low), ((1024, 1024), low), ((1024, 512), low), ((8, 1024), wide)],
         (*chunks, task_embed, far_emb, p0, p1),
         "h" * 12,
-        "hh",
+        "hhh",
         limit=None,
         scratch=[
             pltpu.VMEM((1024, 512), low),
             pltpu.VMEM((1024, 512), low),
             pltpu.VMEM((288, 512), wide),
+            pltpu.VMEM((1024, 1024), low),
             pltpu.VMEM((1024, 512), low),
-            pltpu.VMEM((1024, 1024), low),
-            pltpu.SemaphoreType.DMA((12,)),
+            pltpu.SemaphoreType.DMA((15,)),
         ],
     )
     returned = lax.all_to_all(back, "task", 0, 0, tiled=True, axis_index_groups=column_groups())
 
     keep, send = call(
-        emb_kernel,
-        "emb_terms",
-        [((528, 512), wide), ((544, 512), low)],
-        (*chunks, lows, g_bin),
-        "h" * 9,
-        limit=None,
-        scratch=[
-            pltpu.VMEM((1024, 512), low),
-            pltpu.VMEM((1024, 1024), low),
-            pltpu.SemaphoreType.DMA((12,)),
-        ],
+        emb_kernel, "emb_terms", [((528, 512), wide), ((544, 512), low)], (lows, gathered, g_bin)
     )
     got = lax.ppermute(send, "dp", swap)
     own, *parts = call(

time: 75 us -> 72.4 us (0.965); the launches traced: 74.7 us -> 71.2 us
  Pallas kernels: 16.7 us -> 12.4 us
    pallas_call x7, Pallas kernels: 16.7 us -> 12.4 us  [call(): pl.pallas_call(kernel, out_shape=[jax.ShapeDtypeStruct(shape, kind) for s...]
    unnamed x20 -> x24, local copies, waits for them, and re-layouts: 2.16 us -> 2.9 us
  transfers between devices with their start and end apart: 17 -> 17, of which waited for: 10 -> 10; matrix products, arithmetic and copies ran while one was open for 0% -> 0% of each run, Pallas kernels for 11% -> 6%
where the time goes in v3:
time: 72.4 us; the launch traced here: 71.2 us
  starting transfers between devices  31.3 us (43%)
  waiting for transfers between devices  23.9 us (33%)
  Pallas kernels  12.4 us (17%)
  local copies, waits for them, and re-layouts  2.9 us (4%)
  between operations  0.77 us (1%)
    pallas_call x7, Pallas kernels, call(): pl.pallas_call(kernel, out_shape=[jax.ShapeDtypeStruct(shape, kind) for s...  12.4 us
    ppermute x1, waiting for transfers between devices, per_device(): two = lax.ppermute(mine, BOTH, z_apart(2))  6.39 us
    ppermute x3, starting transfers between devices, per_device(): lax.ppermute(part, 'dp', x_shift(d))  5.7 us
    ppermute x3, starting transfers between devices, per_device(): lax.ppermute(part, BOTH, y_shift(d))  5.69 us
    all_to_all x1, starting transfers between devices, per_device(): lax.all_to_all(back, 'task', 0, 0, tiled=True, axis_index_groups=column_g...  5.55 us
    ppermute x3, waiting for transfers between devices, per_device(): lax.ppermute(part, BOTH, y_shift(d))  5.52 us
    ppermute x1, starting transfers between devices, per_device(): two_back = lax.ppermute(mine, BOTH, z_apart(-2))  5.4 us
    ppermute x1, waiting for transfers between devices, per_device(): three_back = lax.ppermute(two_back, BOTH, z_apart(-1))  4.34 us
  transfers between devices with their start and end apart: 17, of which 10 were waited for; matrix products, arithmetic and copies ran while one was open for 0% of the time, Pallas kernels for 6%

profile of v3, /device:TPU:32, one launch (start us, length us, event | category | flops | bytes accessed | tf_op | source)
XLA Modules:
  0.0 71.2 jit_solution(4713029651210567768)
XLA Ops:
  0.6 3.3 %collective-permute-start.7 = (bf16[512,512]{1,0:T(8,128)(2,1)}, bf16[512,512]{1,0:T(8,128)(2,1)S(1)}, u32[]{:S(2)}, u32[]{:S(2)}) collective-permute-start(bf16[512,512]{1,0:T(8,128)(2,1)} %refs_8_.1), channel_id=1, source_target_pairs={{0,1},{1,0},{2,3},{3,2},{4,5},{5,4},{6,7},{7,6},{8,9},{9,8},{10,11... | collective-permute-start | bytes 1572872 | tf_op jit(solution)/shard_map/ppermute | solution.py:285
  3.9 5.4 %collective-permute-start.3 = (bf16[128,512]{1,0:T(8,128)(2,1)}, bf16[128,512]{1,0:T(8,128)(2,1)S(1)}, u32[]{:S(2)}, u32[]{:S(2)}) collective-permute-start(bf16[128,512]{1,0:T(8,128)(2,1)} %bitcast.9), channel_id=1, source_target_pairs={{0,12},{1,13},{2,14},{3,15},{4,0},{5,1},{6,2},{7,3},{8,4},{9,5},{1... | collective-permute-start | bytes 393224 | tf_op jit(solution)/shard_map/ppermute | solution.py:287
  9.3 2.1 %pack_events.1 = (f32[152,512]{1,0:T(8,128)}, f32[136,512]{1,0:T(8,128)}) custom-call(s32[2,4]{1,0:T(2,128)} %risk_ref.1, s32[9]{0:T(128)} %bounds_ref.1, s32[256,512]{1,0:T(8,128)} %time_ref.1, s32[256,512]{1,0:T(8,128)} %cens_ref.1, f32[8,512]{1,0:T(8,128)} %bitcast.14), custom_call_target="tpu_custom_call" | custom-call | tf_op jit(solution)/shard_map/pack_events/pallas_call | solution.py:69
  11.5 0.3 collective-permute-start.8
  11.8 0.0 collective-permute-start.2
  11.8 1.0 %collective-permute-start.1 = (bf16[128,512]{1,0:T(8,128)(2,1)}, bf16[128,512]{1,0:T(8,128)(2,1)S(1)}, u32[]{:S(2)}, u32[]{:S(2)}) collective-permute-start(bf16[128,512]{1,0:T(8,128)(2,1)} %bitcast.11), channel_id=1, source_target_pairs={{0,14},{1,15},{2,0},{3,1},{4,2},{5,3},{6,4},{7,5},{8,6},{9,7},{10,... | collective-permute-start | bytes 393224 | tf_op jit(solution)/shard_map/ppermute | solution.py:301
  12.8 0.4 collective-permute-done.3.refs_4_
  13.2 0.0 copy-start.5
  13.2 1.8 %collective-permute-start = (bf16[128,512]{1,0:T(8,128)(2,1)}, bf16[128,512]{1,0:T(8,128)(2,1)S(1)}, u32[]{:S(2)}, u32[]{:S(2)}) collective-permute-start(bf16[128,512]{1,0:T(8,128)(2,1)} %bitcast.12), channel_id=1, source_target_pairs={{0,2},{1,3},{2,4},{3,5},{4,6},{5,7},{6,8},{7,9},{8,10},{9,11},{10,... | collective-permute-start | bytes 393224 | tf_op jit(solution)/shard_map/ppermute | solution.py:300
  15.0 6.4 %collective-permute-done.2.refs_3_ = bf16[128,512]{1,0:T(8,128)(2,1)S(1)} collective-permute-done((bf16[128,512]{1,0:T(8,128)(2,1)}, bf16[128,512]{1,0:T(8,128)(2,1)S(1)}, u32[]{:S(2)}, u32[]{:S(2)}) %collective-permute-start.2) | collective-permute-done | bytes 131104 | tf_op jit(solution)/shard_map/ppermute | solution.py:286
  21.4 0.0 copy-start.6
  21.4 0.9 %collective-permute-start.5 = (bf16[128,512]{1,0:T(8,128)(2,1)S(1)}, bf16[128,512]{1,0:T(8,128)(2,1)S(1)}, u32[]{:S(2)}, u32[]{:S(2)}) collective-permute-start(bf16[128,512]{1,0:T(8,128)(2,1)S(1)} %collective-permute-done.3.refs_4_), channel_id=1, source_target_pairs={{0,14},{1,15},{2,0},{3,1},{4,2},{5,3},{6,4},{7,5},{8,6},{9,7},{10,... | collective-permute-start | bytes 393224 | tf_op jit(solution)/shard_map/ppermute | solution.py:298
  22.2 0.0 collective-permute-done.1.refs_2_
  22.2 0.0 copy-start.7
  22.2 0.0 collective-permute-start.6
  22.2 0.0 collective-permute-done.refs_1_
  22.3 0.0 copy-start.8
  22.3 1.4 %collective-permute-start.4 = (bf16[128,512]{1,0:T(8,128)(2,1)S(1)}, bf16[128,512]{1,0:T(8,128)(2,1)S(1)}, u32[]{:S(2)}, u32[]{:S(2)}) collective-permute-start(bf16[128,512]{1,0:T(8,128)(2,1)S(1)} %collective-permute-done.2.refs_3_), channel_id=1, source_target_pairs={{0,2},{1,3},{2,4},{3,5},{4,6},{5,7},{6,8},{7,9},{8,10},{9,11},{10,... | collective-permute-start | bytes 393224 | tf_op jit(solution)/shard_map/ppermute | solution.py:297
  23.6 4.3 %collective-permute-done.5.refs_6_ = bf16[128,512]{1,0:T(8,128)(2,1)S(1)} collective-permute-done((bf16[128,512]{1,0:T(8,128)(2,1)S(1)}, bf16[128,512]{1,0:T(8,128)(2,1)S(1)}, u32[]{:S(2)}, u32[]{:S(2)}) %collective-permute-start.5) | collective-permute-done | bytes 131104 | tf_op jit(solution)/shard_map/ppermute | solution.py:298
  28.0 0.0 copy-start.9
  28.0 1.8 %collective-permute-done.6.refs_7_ = bf16[128,512]{1,0:T(8,128)(2,1)S(1)} collective-permute-done((bf16[128,512]{1,0:T(8,128)(2,1)S(1)}, bf16[128,512]{1,0:T(8,128)(2,1)S(1)}, u32[]{:S(2)}, u32[]{:S(2)}) %collective-permute-start.6) | collective-permute-done | bytes 131104 | tf_op jit(solution)/shard_map/ppermute | solution.py:299
  29.8 0.0 copy-start.10
  29.8 0.8 %collective-permute-done.4.refs_5_ = bf16[128,512]{1,0:T(8,128)(2,1)S(1)} collective-permute-done((bf16[128,512]{1,0:T(8,128)(2,1)S(1)}, bf16[128,512]{1,0:T(8,128)(2,1)S(1)}, u32[]{:S(2)}, u32[]{:S(2)}) %collective-permute-start.4) | collective-permute-done | bytes 131104 | tf_op jit(solution)/shard_map/ppermute | solution.py:297
  30.7 0.0 copy-start.11
  30.7 0.0 collective-permute-done.8.refs_11_
  30.7 0.0 copy-start.4
  30.7 0.0 collective-permute-done.7.refs_9_
  30.7 0.0 copy-start.3
  30.7 0.0 copy-done.5
  30.7 0.0 copy-done.6
  30.7 0.0 copy-done.7
  30.7 0.0 copy-done.8
  30.7 0.0 copy-done.9
  30.7 0.0 copy-done.10
  30.7 0.6 copy-done.11
  31.3 0.1 copy-done.4
  31.4 0.2 copy-done.3
  31.6 7.3 %terms.1 = (bf16[1024,512]{1,0:T(8,128)(2,1)}, bf16[1024,1024]{1,0:T(8,128)(2,1)}, bf16[1024,512]{1,0:T(8,128)(2,1)}, f32[8,1024]{1,0:T(8,128)}) custom-call(bf16[128,512]{1,0:T(8,128)(2,1)} %bitcast.13, bf16[128,512]{1,0:T(8,128)(2,1)} %copy-done.8, bf16[128,512]{1,0:T(8,128)(2,1)} %copy-done.7, bf16[128,512]{1,0:T(8,128)(2,1)} %copy-done.6, ...), custom_call_target="tpu_custom_call" | custom-call | tf_op jit(solution)/shard_map/terms/pallas_call | solution.py:69
  38.9 0.0 copy-start
  38.9 5.5 %all-to-all-start = ((bf16[8,128,512]{2,1,0:T(8,128)(2,1)}), bf16[8,128,512]{2,1,0:T(8,128)(2,1)S(1)}, u32[]{:S(2)}, u32[]{:S(2)}) async-start(bf16[8,128,512]{2,1,0:T(8,128)(2,1)} %bitcast.7), calls=%async_computation | async-start | bytes 2097152 | tf_op jit(solution)/shard_map/all_to_all | solution.py:321
  44.4 0.0 copy-done
  44.5 1.2 %copy-done.1 = bf16[1024,512]{1,0:T(8,128)(2,1)S(1)} copy-done((bf16[1024,512]{1,0:T(8,128)(2,1)S(1)}, bf16[1024,512]{1,0:T(8,128)(2,1)}, u32[]{:S(2)}) %copy-start.1) | copy-done | bytes 1048600
  45.7 0.0 copy-start.2
  45.7 0.8 %copy-done.2 = f32[8,1024]{1,0:T(8,128)S(1)} copy-done((f32[8,1024]{1,0:T(8,128)S(1)}, f32[8,1024]{1,0:T(8,128)}, u32[]{:S(2)}) %copy-start.2) | copy-done | bytes 32792
  46.4 1.3 %emb_terms.1 = (f32[528,512]{1,0:T(8,128)S(1)}, bf16[544,512]{1,0:T(8,128)(2,1)S(1)}) custom-call(bf16[1024,1024]{1,0:T(8,128)(2,1)S(1)} %copy-done, bf16[1024,512]{1,0:T(8,128)(2,1)S(1)} %copy-done.1, f32[8,1024]{1,0:T(8,128)S(1)} %copy-done.2), custom_call_target="tpu_custom_call" | custom-call | tf_op jit(solution)/shard_map/emb_terms/pallas_call | solution.py:69
  47.7 0.3 collective-permute-start.9
  48.0 1.9 %collective-permute-done.9.got_ref = bf16[544,512]{1,0:T(8,128)(2,1)S(1)} collective-permute-done((bf16[544,512]{1,0:T(8,128)(2,1)S(1)}, bf16[544,512]{1,0:T(8,128)(2,1)S(1)}, u32[]{:S(2)}, u32[]{:S(2)}) %collective-permute-start.9) | collective-permute-done | bytes 557088 | tf_op jit(solution)/shard_map/ppermute | solution.py:326
  50.0 0.1 join_cores.1
  50.1 1.2 %collective-permute-start.10 = (bf16[144,512]{1,0:T(8,128)(2,1)S(1)}, bf16[144,512]{1,0:T(8,128)(2,1)S(1)}, u32[]{:S(2)}, u32[]{:S(2)}) collective-permute-start(bf16[144,512]{1,0:T(8,128)(2,1)S(1)} %get-tuple-element.30), channel_id=1, source_target_pairs={{0,128},{2,130},{4,132},{6,134},{8,136},{10,138},{12,140},{14,142}... | collective-permute-start | bytes 442376 | tf_op jit(solution)/shard_map/ppermute | solution.py:330
  51.2 3.0 %collective-permute-start.11 = (bf16[144,512]{1,0:T(8,128)(2,1)S(1)}, bf16[144,512]{1,0:T(8,128)(2,1)S(1)}, u32[]{:S(2)}, u32[]{:S(2)}) collective-permute-start(bf16[144,512]{1,0:T(8,128)(2,1)S(1)} %get-tuple-element.31), channel_id=1, source_target_pairs={{0,1},{2,3},{4,5},{6,7},{8,9},{10,11},{12,13},{14,15},{16,17},{18,... | collective-permute-start | bytes 442376 | tf_op jit(solution)/shard_map/ppermute | solution.py:330
  54.3 1.5 %collective-permute-start.12 = (bf16[144,512]{1,0:T(8,128)(2,1)S(1)}, bf16[144,512]{1,0:T(8,128)(2,1)S(1)}, u32[]{:S(2)}, u32[]{:S(2)}) collective-permute-start(bf16[144,512]{1,0:T(8,128)(2,1)S(1)} %get-tuple-element.32), channel_id=1, source_target_pairs={{0,129},{2,131},{4,133},{6,135},{8,137},{10,139},{12,141},{14,143}... | collective-permute-start | bytes 442376 | tf_op jit(solution)/shard_map/ppermute | solution.py:330
  55.8 1.5 %collective-permute-done.10.refs_1_ = bf16[144,512]{1,0:T(8,128)(2,1)S(1)} collective-permute-done((bf16[144,512]{1,0:T(8,128)(2,1)S(1)}, bf16[144,512]{1,0:T(8,128)(2,1)S(1)}, u32[]{:S(2)}, u32[]{:S(2)}) %collective-permute-start.10) | collective-permute-done | bytes 147488 | tf_op jit(solution)/shard_map/ppermute | solution.py:330
  57.3 4.0 %collective-permute-done.11.refs_2_ = bf16[144,512]{1,0:T(8,128)(2,1)S(1)} collective-permute-done((bf16[144,512]{1,0:T(8,128)(2,1)S(1)}, bf16[144,512]{1,0:T(8,128)(2,1)S(1)}, u32[]{:S(2)}, u32[]{:S(2)}) %collective-permute-start.11) | collective-permute-done | bytes 147488 | tf_op jit(solution)/shard_map/ppermute | solution.py:330
  61.3 0.0 collective-permute-done.12.refs_3_
  61.3 0.1 sum_y.1
  61.4 1.5 %collective-permute-start.13 = (bf16[48,512]{1,0:T(8,128)(2,1)S(1)}, bf16[48,512]{1,0:T(8,128)(2,1)S(1)}, u32[]{:S(2)}, u32[]{:S(2)}) collective-permute-start(bf16[48,512]{1,0:T(8,128)(2,1)S(1)} %get-tuple-element.34), channel_id=1, source_target_pairs={{0,32},{16,48},{32,64},{48,80},{64,96},{80,112},{96,0},{112,16},{1... | collective-permute-start | bytes 147464 | tf_op jit(solution)/shard_map/ppermute | solution.py:338
  62.9 2.7 %collective-permute-start.14 = (bf16[48,512]{1,0:T(8,128)(2,1)S(1)}, bf16[48,512]{1,0:T(8,128)(2,1)S(1)}, u32[]{:S(2)}, u32[]{:S(2)}) collective-permute-start(bf16[48,512]{1,0:T(8,128)(2,1)S(1)} %get-tuple-element.35), channel_id=1, source_target_pairs={{0,64},{16,80},{32,96},{48,112},{64,0},{80,16},{96,32},{112,48},{1... | collective-permute-start | bytes 147464 | tf_op jit(solution)/shard_map/ppermute | solution.py:338
  65.7 1.4 %collective-permute-start.15 = (bf16[48,512]{1,0:T(8,128)(2,1)S(1)}, bf16[48,512]{1,0:T(8,128)(2,1)S(1)}, u32[]{:S(2)}, u32[]{:S(2)}) collective-permute-start(bf16[48,512]{1,0:T(8,128)(2,1)S(1)} %get-tuple-element.36), channel_id=1, source_target_pairs={{0,96},{16,112},{32,0},{48,16},{64,32},{80,48},{96,64},{112,80},{1... | collective-permute-start | bytes 147464 | tf_op jit(solution)/shard_map/ppermute | solution.py:338
  67.1 0.0 collective-permute-done.13.refs_1_
  67.1 1.4 %collective-permute-done.14.refs_2_ = bf16[48,512]{1,0:T(8,128)(2,1)S(1)} collective-permute-done((bf16[48,512]{1,0:T(8,128)(2,1)S(1)}, bf16[48,512]{1,0:T(8,128)(2,1)S(1)}, u32[]{:S(2)}, u32[]{:S(2)}) %collective-permute-start.14) | collective-permute-done | bytes 49184 | tf_op jit(solution)/shard_map/ppermute | solution.py:338
  68.5 1.2 %collective-permute-done.15.refs_3_ = bf16[48,512]{1,0:T(8,128)(2,1)S(1)} collective-permute-done((bf16[48,512]{1,0:T(8,128)(2,1)S(1)}, bf16[48,512]{1,0:T(8,128)(2,1)S(1)}, u32[]{:S(2)}, u32[]{:S(2)}) %collective-permute-start.15) | collective-permute-done | bytes 49184 | tf_op jit(solution)/shard_map/ppermute | solution.py:338
  69.8 0.7 sum_x.1
  70.4 0.0 all-to-all-done
  70.4 0.8 %sum_returned.1 = bf16[128,512]{1,0:T(8,128)(2,1)} custom-call(bf16[1024,512]{1,0:T(8,128)(2,1)S(1)} %bitcast.6), custom_call_target="tpu_custom_call" | custom-call | tf_op jit(solution)/shard_map/sum_returned/pallas_call | solution.py:69
  (1 shorter events, 0.0 us)
Async XLA Ops:
  0.6 30.0 %collective-permute-start.7 = (bf16[512,512]{1,0:T(8,128)(2,1)}, bf16[512,512]{1,0:T(8,128)(2,1)S(1)}, u32[]{:S(2)}, u32[]{:S(2)}) collective-permute-start(bf16[512,512]{1,0:T(8,128)(2,1)} %refs_8_.1), channel_id=1, source_target_pairs={{0,1},{1,0},{2,3},{3,2},{4,5},{5,4},{6,7},{7,6},{8,9},{9,8},{10,11... | collective-permute-start | bytes 1572872 | tf_op jit(solution)/shard_map/ppermute | solution.py:285
  3.9 9.3 %collective-permute-start.3 = (bf16[128,512]{1,0:T(8,128)(2,1)}, bf16[128,512]{1,0:T(8,128)(2,1)S(1)}, u32[]{:S(2)}, u32[]{:S(2)}) collective-permute-start(bf16[128,512]{1,0:T(8,128)(2,1)} %bitcast.9), channel_id=1, source_target_pairs={{0,12},{1,13},{2,14},{3,15},{4,0},{5,1},{6,2},{7,3},{8,4},{9,5},{1... | collective-permute-start | bytes 393224 | tf_op jit(solution)/shard_map/ppermute | solution.py:287
  11.5 19.2 %collective-permute-start.8 = (f32[136,512]{1,0:T(8,128)}, f32[136,512]{1,0:T(8,128)S(1)}, u32[]{:S(2)}, u32[]{:S(2)}) collective-permute-start(f32[136,512]{1,0:T(8,128)} %get-tuple-element.22), channel_id=1, source_target_pairs={{0,1},{1,0},{2,3},{3,2},{4,5},{5,4},{6,7},{7,6},{8,9},{9,8},{10,11... | collective-permute-start | bytes 835592 | tf_op jit(solution)/shard_map/ppermute | solution.py:296
  11.8 9.6 %collective-permute-start.2 = (bf16[128,512]{1,0:T(8,128)(2,1)}, bf16[128,512]{1,0:T(8,128)(2,1)S(1)}, u32[]{:S(2)}, u32[]{:S(2)}) collective-permute-start(bf16[128,512]{1,0:T(8,128)(2,1)} %bitcast.10), channel_id=1, source_target_pairs={{0,4},{1,5},{2,6},{3,7},{4,8},{5,9},{6,10},{7,11},{8,12},{9,13},{1... | collective-permute-start | bytes 393224 | tf_op jit(solution)/shard_map/ppermute | solution.py:286
  11.8 10.4 %collective-permute-start.1 = (bf16[128,512]{1,0:T(8,128)(2,1)}, bf16[128,512]{1,0:T(8,128)(2,1)S(1)}, u32[]{:S(2)}, u32[]{:S(2)}) collective-permute-start(bf16[128,512]{1,0:T(8,128)(2,1)} %bitcast.11), channel_id=1, source_target_pairs={{0,14},{1,15},{2,0},{3,1},{4,2},{5,3},{6,4},{7,5},{8,6},{9,7},{10,... | collective-permute-start | bytes 393224 | tf_op jit(solution)/shard_map/ppermute | solution.py:301
  13.2 17.5 %copy-start.5 = (bf16[128,512]{1,0:T(8,128)(2,1)}, bf16[128,512]{1,0:T(8,128)(2,1)S(1)}, u32[]{:S(2)}) copy-start(bf16[128,512]{1,0:T(8,128)(2,1)S(1)} %collective-permute-done.3.refs_4_) | copy-start | bytes 393220
  13.2 9.1 %collective-permute-start = (bf16[128,512]{1,0:T(8,128)(2,1)}, bf16[128,512]{1,0:T(8,128)(2,1)S(1)}, u32[]{:S(2)}, u32[]{:S(2)}) collective-permute-start(bf16[128,512]{1,0:T(8,128)(2,1)} %bitcast.12), channel_id=1, source_target_pairs={{0,2},{1,3},{2,4},{3,5},{4,6},{5,7},{6,8},{7,9},{8,10},{9,11},{10,... | collective-permute-start | bytes 393224 | tf_op jit(solution)/shard_map/ppermute | solution.py:300
  21.4 9.3 %copy-start.6 = (bf16[128,512]{1,0:T(8,128)(2,1)}, bf16[128,512]{1,0:T(8,128)(2,1)S(1)}, u32[]{:S(2)}) copy-start(bf16[128,512]{1,0:T(8,128)(2,1)S(1)} %collective-permute-done.2.refs_3_) | copy-start | bytes 393220
  21.4 6.6 %collective-permute-start.5 = (bf16[128,512]{1,0:T(8,128)(2,1)S(1)}, bf16[128,512]{1,0:T(8,128)(2,1)S(1)}, u32[]{:S(2)}, u32[]{:S(2)}) collective-permute-start(bf16[128,512]{1,0:T(8,128)(2,1)S(1)} %collective-permute-done.3.refs_4_), channel_id=1, source_target_pairs={{0,14},{1,15},{2,0},{3,1},{4,2},{5,3},{6,4},{7,5},{8,6},{9,7},{10,... | collective-permute-start | bytes 393224 | tf_op jit(solution)/shard_map/ppermute | solution.py:298
  22.2 8.5 %copy-start.7 = (bf16[128,512]{1,0:T(8,128)(2,1)}, bf16[128,512]{1,0:T(8,128)(2,1)S(1)}, u32[]{:S(2)}) copy-start(bf16[128,512]{1,0:T(8,128)(2,1)S(1)} %collective-permute-done.1.refs_2_) | copy-start | bytes 393220
  22.2 7.6 %collective-permute-start.6 = (bf16[128,512]{1,0:T(8,128)(2,1)S(1)}, bf16[128,512]{1,0:T(8,128)(2,1)S(1)}, u32[]{:S(2)}, u32[]{:S(2)}) collective-permute-start(bf16[128,512]{1,0:T(8,128)(2,1)S(1)} %collective-permute-done.2.refs_3_), channel_id=1, source_target_pairs={{0,4},{1,5},{2,6},{3,7},{4,8},{5,9},{6,10},{7,11},{8,12},{9,13},{1... | collective-permute-start | bytes 393224 | tf_op jit(solution)/shard_map/ppermute | solution.py:299
  22.3 8.5 %copy-start.8 = (bf16[128,512]{1,0:T(8,128)(2,1)}, bf16[128,512]{1,0:T(8,128)(2,1)S(1)}, u32[]{:S(2)}) copy-start(bf16[128,512]{1,0:T(8,128)(2,1)S(1)} %collective-permute-done.refs_1_) | copy-start | bytes 393220
  22.3 8.4 %collective-permute-start.4 = (bf16[128,512]{1,0:T(8,128)(2,1)S(1)}, bf16[128,512]{1,0:T(8,128)(2,1)S(1)}, u32[]{:S(2)}, u32[]{:S(2)}) collective-permute-start(bf16[128,512]{1,0:T(8,128)(2,1)S(1)} %collective-permute-done.2.refs_3_), channel_id=1, source_target_pairs={{0,2},{1,3},{2,4},{3,5},{4,6},{5,7},{6,8},{7,9},{8,10},{9,11},{10,... | collective-permute-start | bytes 393224 | tf_op jit(solution)/shard_map/ppermute | solution.py:297
  28.0 2.8 %copy-start.9 = (bf16[128,512]{1,0:T(8,128)(2,1)}, bf16[128,512]{1,0:T(8,128)(2,1)S(1)}, u32[]{:S(2)}) copy-start(bf16[128,512]{1,0:T(8,128)(2,1)S(1)} %collective-permute-done.5.refs_6_) | copy-start | bytes 393220
  29.8 0.9 %copy-start.10 = (bf16[128,512]{1,0:T(8,128)(2,1)}, bf16[128,512]{1,0:T(8,128)(2,1)S(1)}, u32[]{:S(2)}) copy-start(bf16[128,512]{1,0:T(8,128)(2,1)S(1)} %collective-permute-done.6.refs_7_) | copy-start | bytes 393220
  30.7 0.6 copy-start.11
  30.7 0.7 %copy-start.4 = (f32[136,512]{1,0:T(8,128)}, f32[136,512]{1,0:T(8,128)S(1)}, u32[]{:S(2)}) copy-start(f32[136,512]{1,0:T(8,128)S(1)} %collective-permute-done.8.refs_11_) | copy-start | bytes 835588
  30.7 1.0 %copy-start.3 = (bf16[512,512]{1,0:T(8,128)(2,1)}, bf16[512,512]{1,0:T(8,128)(2,1)S(1)}, u32[]{:S(2)}) copy-start(bf16[512,512]{1,0:T(8,128)(2,1)S(1)} %collective-permute-done.7.refs_9_) | copy-start | bytes 1572868
  38.9 5.6 %copy-start = (bf16[1024,1024]{1,0:T(8,128)(2,1)S(1)}, bf16[1024,1024]{1,0:T(8,128)(2,1)}, u32[]{:S(2)}) copy-start(bf16[1024,1024]{1,0:T(8,128)(2,1)} %get-tuple-element.24.low_ref) | copy-start | bytes 6291460
  38.9 31.5 %all-to-all-start = ((bf16[8,128,512]{2,1,0:T(8,128)(2,1)}), bf16[8,128,512]{2,1,0:T(8,128)(2,1)S(1)}, u32[]{:S(2)}, u32[]{:S(2)}) async-start(bf16[8,128,512]{2,1,0:T(8,128)(2,1)} %bitcast.7), calls=%async_computation | async-start | bytes 2097152 | tf_op jit(solution)/shard_map/all_to_all | solution.py:321
  44.5 1.2 %copy-start.1 = (bf16[1024,512]{1,0:T(8,128)(2,1)S(1)}, bf16[1024,512]{1,0:T(8,128)(2,1)}, u32[]{:S(2)}) copy-start(bf16[1024,512]{1,0:T(8,128)(2,1)} %get-tuple-element.25.feats) | copy-start | bytes 3145732
  45.7 0.8 %copy-start.2 = (f32[8,1024]{1,0:T(8,128)S(1)}, f32[8,1024]{1,0:T(8,128)}, u32[]{:S(2)}) copy-start(f32[8,1024]{1,0:T(8,128)} %get-tuple-element.26.bin_ref) | copy-start | bytes 98308
  47.7 2.2 %collective-permute-start.9 = (bf16[544,512]{1,0:T(8,128)(2,1)S(1)}, bf16[544,512]{1,0:T(8,128)(2,1)S(1)}, u32[]{:S(2)}, u32[]{:S(2)}) collective-permute-start(bf16[544,512]{1,0:T(8,128)(2,1)S(1)} %get-tuple-element.28), channel_id=1, source_target_pairs={{0,16},{16,0},{32,48},{48,32},{64,80},{80,64},{96,112},{112,96},{1... | collective-permute-start | bytes 1671176 | tf_op jit(solution)/shard_map/ppermute | solution.py:326
  50.1 7.2 %collective-permute-start.10 = (bf16[144,512]{1,0:T(8,128)(2,1)S(1)}, bf16[144,512]{1,0:T(8,128)(2,1)S(1)}, u32[]{:S(2)}, u32[]{:S(2)}) collective-permute-start(bf16[144,512]{1,0:T(8,128)(2,1)S(1)} %get-tuple-element.30), channel_id=1, source_target_pairs={{0,128},{2,130},{4,132},{6,134},{8,136},{10,138},{12,140},{14,142}... | collective-permute-start | bytes 442376 | tf_op jit(solution)/shard_map/ppermute | solution.py:330
  51.2 10.0 %collective-permute-start.11 = (bf16[144,512]{1,0:T(8,128)(2,1)S(1)}, bf16[144,512]{1,0:T(8,128)(2,1)S(1)}, u32[]{:S(2)}, u32[]{:S(2)}) collective-permute-start(bf16[144,512]{1,0:T(8,128)(2,1)S(1)} %get-tuple-element.31), channel_id=1, source_target_pairs={{0,1},{2,3},{4,5},{6,7},{8,9},{10,11},{12,13},{14,15},{16,17},{18,... | collective-permute-start | bytes 442376 | tf_op jit(solution)/shard_map/ppermute | solution.py:330
  54.3 7.0 %collective-permute-start.12 = (bf16[144,512]{1,0:T(8,128)(2,1)S(1)}, bf16[144,512]{1,0:T(8,128)(2,1)S(1)}, u32[]{:S(2)}, u32[]{:S(2)}) collective-permute-start(bf16[144,512]{1,0:T(8,128)(2,1)S(1)} %get-tuple-element.32), channel_id=1, source_target_pairs={{0,129},{2,131},{4,133},{6,135},{8,137},{10,139},{12,141},{14,143}... | collective-permute-start | bytes 442376 | tf_op jit(solution)/shard_map/ppermute | solution.py:330
  61.4 5.7 %collective-permute-start.13 = (bf16[48,512]{1,0:T(8,128)(2,1)S(1)}, bf16[48,512]{1,0:T(8,128)(2,1)S(1)}, u32[]{:S(2)}, u32[]{:S(2)}) collective-permute-start(bf16[48,512]{1,0:T(8,128)(2,1)S(1)} %get-tuple-element.34), channel_id=1, source_target_pairs={{0,32},{16,48},{32,64},{48,80},{64,96},{80,112},{96,0},{112,16},{1... | collective-permute-start | bytes 147464 | tf_op jit(solution)/shard_map/ppermute | solution.py:338
  62.9 5.6 %collective-permute-start.14 = (bf16[48,512]{1,0:T(8,128)(2,1)S(1)}, bf16[48,512]{1,0:T(8,128)(2,1)S(1)}, u32[]{:S(2)}, u32[]{:S(2)}) collective-permute-start(bf16[48,512]{1,0:T(8,128)(2,1)S(1)} %get-tuple-element.35), channel_id=1, source_target_pairs={{0,64},{16,80},{32,96},{48,112},{64,0},{80,16},{96,32},{112,48},{1... | collective-permute-start | bytes 147464 | tf_op jit(solution)/shard_map/ppermute | solution.py:338
  65.7 4.1 %collective-permute-start.15 = (bf16[48,512]{1,0:T(8,128)(2,1)S(1)}, bf16[48,512]{1,0:T(8,128)(2,1)S(1)}, u32[]{:S(2)}, u32[]{:S(2)}) collective-permute-start(bf16[48,512]{1,0:T(8,128)(2,1)S(1)} %get-tuple-element.36), channel_id=1, source_target_pairs={{0,96},{16,112},{32,0},{48,16},{64,32},{80,48},{96,64},{112,80},{1... | collective-permute-start | bytes 147464 | tf_op jit(solution)/shard_map/ppermute | solution.py:338

commit v4 on v3

--- a/solution.py
+++ b/solution.py
@@ -107,8 +107,8 @@
 
 def grad_kernel(*refs):
     chunks, refs = refs[:8], refs[8:]
-    e0, e1, p0, p1, back_out, low_out, feat_out, bin_ref = refs[:8]
-    feats, embs, events, lows, backs, sems = refs[8:]
+    e0, e1, p0, p1, back_out, low_out = refs[:6]
+    feats, embs, events, lows, backs, sems = refs[6:]
     z, core, _ = place()
 
     def fetch(source, target, slot):
@@ -146,21 +146,21 @@
         base = i * 152
         bias = events[base + 128 : base + 136, :]
         g_bin = jnp.zeros((8, WIDE), jnp.float32)
-        for part in range(4):
+        for part in range(2):
             if i == 0:
-                copies[2 * part].wait()
-                copies[2 * part + 1].wait()
+                for copy in copies[4 * part : 4 * part + 4]:
+                    copy.wait()
             logit = lax.dot_general(
-                feats[part * 256 : (part + 1) * 256, :],
+                feats[part * 512 : (part + 1) * 512, :],
                 emb,
                 (((1,), (1,)), ((), ())),
                 preferred_element_type=jnp.float32,
             )
-            for slot in (2 * part, 2 * part + 1):
+            for slot in range(4 * part, 4 * part + 4):
                 signed = events[pl.ds(pl.multiple_of(base + owners[slot] * 16, 8), 16), :]
                 moment = jnp.abs(signed)[:, None, :]
                 signed = signed[:, None, :]
-                at = (slot % 2) * ROWS
+                at = (slot % 4) * ROWS
                 piece = logit[at : at + ROWS].reshape(16, 8, WIDE) + bias[None]
                 exposure = jnp.clip(moment - lower[None], 0.0, span[None])
                 inside = (signed > lower[None]) & (signed <= upper[None])
@@ -169,14 +169,15 @@
                 lows[slot * ROWS : (slot + 1) * ROWS, out] = dlogit.reshape(ROWS, WIDE).astype(
                     jnp.bfloat16
                 )
-        bin_ref[:, out] = g_bin
+        lows[1024:1040, out] = split_sums(g_bin)
         return carry
 
     stored = []
     for i in range(2):
         step(i, 0)
         if i == 0:
-            stored.append(fetch(feats, feat_out, 14))
+            target = low_out.at[pl.ds(0, 1024), pl.ds(1024, 512)]
+            stored.append(fetch(feats, target, 14))
         half = pl.ds(i * WIDE, WIDE)
         stored.append(fetch(lows.at[:, half], low_out.at[:, half], 12 + i))
     sent = []
@@ -194,12 +195,12 @@
         copy.wait()
 
 
-def emb_kernel(low_ref, feats, bin_ref, keep_ref, send_ref):
+def emb_kernel(low_ref, keep_ref, send_ref):
     _, core, h = place()
     for i in range(4):
         g_emb = lax.dot_general(
-            low_ref[:, i * 256 : (i + 1) * 256],
-            feats[...],
+            low_ref[0:1024, i * 256 : (i + 1) * 256],
+            low_ref[0:1024, 1024:1536],
             (((0,), (0,)), ((), ())),
             preferred_element_type=jnp.float32,
         )
@@ -210,10 +211,11 @@
         keep_ref[spot, :] = jnp.where(core == 0, zero, one)
         send_ref[spot, :] = jnp.where(core == 0, one, zero).astype(jnp.bfloat16)
     for side in range(2):
-        sums = bin_ref[:, side * 512 : (side + 1) * 512]
+        parts = low_ref[1024:1040, side * 512 : (side + 1) * 512]
+        sums = parts.astype(jnp.float32)
         there = h if side == 0 else 1 - h
-        keep_ref[pl.ds(pl.multiple_of(512 + there * 8, 8), 8), :] = sums
-        send_ref[pl.ds(pl.multiple_of(512 + there * 16, 16), 16), :] = split_sums(sums)
+        keep_ref[pl.ds(pl.multiple_of(512 + there * 8, 8), 8), :] = sums[0:8] + sums[8:16]
+        send_ref[pl.ds(pl.multiple_of(512 + there * 16, 16), 16), :] = parts
 
 
 def join_kernel(keep_ref, got_ref, own_ref, *outs):
@@ -301,19 +303,19 @@
     one_back = lax.ppermute(mine, "task", z_shift(-1))
     chunks = (mine, one, one_back, two, two_back, three, three_back, four)
 
-    back, lows, gathered, g_bin = call(
+    back, lows = call(
         grad_kernel,
         "terms",
-        [((1024, 512), low), ((1024, 1024), low), ((1024, 512), low), ((8, 1024), wide)],
+        [((1024, 512), low), ((1040, 1536), low)],
         (*chunks, task_embed, far_emb, p0, p1),
         "h" * 12,
-        "hhh",
+        "hh",
         limit=None,
         scratch=[
             pltpu.VMEM((1024, 512), low),
             pltpu.VMEM((1024, 512), low),
             pltpu.VMEM((288, 512), wide),
-            pltpu.VMEM((1024, 1024), low),
+            pltpu.VMEM((1040, 1024), low),
             pltpu.VMEM((1024, 512), low),
             pltpu.SemaphoreType.DMA((15,)),
         ],
@@ -321,7 +323,7 @@
     returned = lax.all_to_all(back, "task", 0, 0, tiled=True, axis_index_groups=column_groups())
 
     keep, send = call(
-        emb_kernel, "emb_terms", [((528, 512), wide), ((544, 512), low)], (lows, gathered, g_bin)
+        emb_kernel, "emb_terms", [((528, 512), wide), ((544, 512), low)], (lows,)
     )
     got = lax.ppermute(send, "dp", swap)
     own, *parts = call(

time: 72.4 us -> 71.3 us (0.985)
  Pallas kernels: 12.4 us -> 11.5 us
    pallas_call x7, Pallas kernels: 12.4 us -> 11.5 us  [call(): pl.pallas_call(kernel, out_shape=[jax.ShapeDtypeStruct(shape, kind) for s...]
    unnamed x24 -> x20, local copies, waits for them, and re-layouts: 2.9 us -> 2.79 us
where the time goes in v4:
time: 71.3 us; the launch traced here: 70.1 us
  starting transfers between devices  31.1 us (44%)
  waiting for transfers between devices  23.9 us (34%)
  Pallas kernels  11.5 us (16%)
  local copies, waits for them, and re-layouts  2.79 us (4%)
  between operations  0.76 us (1%)
    pallas_call x7, Pallas kernels, call(): pl.pallas_call(kernel, out_shape=[jax.ShapeDtypeStruct(shape, kind) for s...  11.5 us
    ppermute x1, waiting for transfers between devices, per_device(): two = lax.ppermute(mine, BOTH, z_apart(2))  6.39 us
    ppermute x3, starting transfers between devices, per_device(): lax.ppermute(part, 'dp', x_shift(d))  5.74 us
    ppermute x3, starting transfers between devices, per_device(): lax.ppermute(part, BOTH, y_shift(d))  5.63 us
    ppermute x3, waiting for transfers between devices, per_device(): lax.ppermute(part, BOTH, y_shift(d))  5.49 us
    all_to_all x1, starting transfers between devices, per_device(): lax.all_to_all(back, 'task', 0, 0, tiled=True, axis_index_groups=column_g...  5.43 us
    ppermute x1, starting transfers between devices, per_device(): two_back = lax.ppermute(mine, BOTH, z_apart(-2))  5.4 us
    ppermute x1, waiting for transfers between devices, per_device(): three_back = lax.ppermute(two_back, BOTH, z_apart(-1))  4.33 us
  transfers between devices with their start and end apart: 17, of which 10 were waited for; matrix products, arithmetic and copies ran while one was open for 0% of the time, Pallas kernels for 6%

profile of v4, /device:TPU:32, one launch (start us, length us, event | category | flops | bytes accessed | tf_op | source)
XLA Modules:
  0.0 70.1 jit_solution(17216114241604673035)
XLA Ops:
  0.6 3.3 %collective-permute-start.7 = (bf16[512,512]{1,0:T(8,128)(2,1)}, bf16[512,512]{1,0:T(8,128)(2,1)S(1)}, u32[]{:S(2)}, u32[]{:S(2)}) collective-permute-start(bf16[512,512]{1,0:T(8,128)(2,1)} %refs_8_.1), channel_id=1, source_target_pairs={{0,1},{1,0},{2,3},{3,2},{4,5},{5,4},{6,7},{7,6},{8,9},{9,8},{10,11... | collective-permute-start | bytes 1572872 | tf_op jit(solution)/shard_map/ppermute | solution.py:287
  3.9 5.4 %collective-permute-start.3 = (bf16[128,512]{1,0:T(8,128)(2,1)}, bf16[128,512]{1,0:T(8,128)(2,1)S(1)}, u32[]{:S(2)}, u32[]{:S(2)}) collective-permute-start(bf16[128,512]{1,0:T(8,128)(2,1)} %bitcast.9), channel_id=1, source_target_pairs={{0,12},{1,13},{2,14},{3,15},{4,0},{5,1},{6,2},{7,3},{8,4},{9,5},{1... | collective-permute-start | bytes 393224 | tf_op jit(solution)/shard_map/ppermute | solution.py:289
  9.3 2.1 %pack_events.1 = (f32[152,512]{1,0:T(8,128)}, f32[136,512]{1,0:T(8,128)}) custom-call(s32[2,4]{1,0:T(2,128)} %risk_ref.1, s32[9]{0:T(128)} %bounds_ref.1, s32[256,512]{1,0:T(8,128)} %time_ref.1, s32[256,512]{1,0:T(8,128)} %cens_ref.1, f32[8,512]{1,0:T(8,128)} %bitcast.14), custom_call_target="tpu_custom_call" | custom-call | tf_op jit(solution)/shard_map/pack_events/pallas_call | solution.py:69
  11.4 0.3 collective-permute-start.8
  11.8 0.0 collective-permute-start.2
  11.8 1.0 %collective-permute-start.1 = (bf16[128,512]{1,0:T(8,128)(2,1)}, bf16[128,512]{1,0:T(8,128)(2,1)S(1)}, u32[]{:S(2)}, u32[]{:S(2)}) collective-permute-start(bf16[128,512]{1,0:T(8,128)(2,1)} %bitcast.11), channel_id=1, source_target_pairs={{0,14},{1,15},{2,0},{3,1},{4,2},{5,3},{6,4},{7,5},{8,6},{9,7},{10,... | collective-permute-start | bytes 393224 | tf_op jit(solution)/shard_map/ppermute | solution.py:303
  12.8 0.4 collective-permute-done.3.refs_4_
  13.2 0.0 copy-start.3
  13.2 1.8 %collective-permute-start = (bf16[128,512]{1,0:T(8,128)(2,1)}, bf16[128,512]{1,0:T(8,128)(2,1)S(1)}, u32[]{:S(2)}, u32[]{:S(2)}) collective-permute-start(bf16[128,512]{1,0:T(8,128)(2,1)} %bitcast.12), channel_id=1, source_target_pairs={{0,2},{1,3},{2,4},{3,5},{4,6},{5,7},{6,8},{7,9},{8,10},{9,11},{10,... | collective-permute-start | bytes 393224 | tf_op jit(solution)/shard_map/ppermute | solution.py:302
  15.0 6.4 %collective-permute-done.2.refs_3_ = bf16[128,512]{1,0:T(8,128)(2,1)S(1)} collective-permute-done((bf16[128,512]{1,0:T(8,128)(2,1)}, bf16[128,512]{1,0:T(8,128)(2,1)S(1)}, u32[]{:S(2)}, u32[]{:S(2)}) %collective-permute-start.2) | collective-permute-done | bytes 131104 | tf_op jit(solution)/shard_map/ppermute | solution.py:288
  21.4 0.0 copy-start.4
  21.4 0.9 %collective-permute-start.5 = (bf16[128,512]{1,0:T(8,128)(2,1)S(1)}, bf16[128,512]{1,0:T(8,128)(2,1)S(1)}, u32[]{:S(2)}, u32[]{:S(2)}) collective-permute-start(bf16[128,512]{1,0:T(8,128)(2,1)S(1)} %collective-permute-done.3.refs_4_), channel_id=1, source_target_pairs={{0,14},{1,15},{2,0},{3,1},{4,2},{5,3},{6,4},{7,5},{8,6},{9,7},{10,... | collective-permute-start | bytes 393224 | tf_op jit(solution)/shard_map/ppermute | solution.py:300
  22.2 0.0 collective-permute-done.1.refs_2_
  22.2 0.0 copy-start.5
  22.2 0.0 collective-permute-start.6
  22.2 0.0 collective-permute-done.refs_1_
  22.3 0.0 copy-start.6
  22.3 1.4 %collective-permute-start.4 = (bf16[128,512]{1,0:T(8,128)(2,1)S(1)}, bf16[128,512]{1,0:T(8,128)(2,1)S(1)}, u32[]{:S(2)}, u32[]{:S(2)}) collective-permute-start(bf16[128,512]{1,0:T(8,128)(2,1)S(1)} %collective-permute-done.2.refs_3_), channel_id=1, source_target_pairs={{0,2},{1,3},{2,4},{3,5},{4,6},{5,7},{6,8},{7,9},{8,10},{9,11},{10,... | collective-permute-start | bytes 393224 | tf_op jit(solution)/shard_map/ppermute | solution.py:299
  23.6 4.3 %collective-permute-done.5.refs_6_ = bf16[128,512]{1,0:T(8,128)(2,1)S(1)} collective-permute-done((bf16[128,512]{1,0:T(8,128)(2,1)S(1)}, bf16[128,512]{1,0:T(8,128)(2,1)S(1)}, u32[]{:S(2)}, u32[]{:S(2)}) %collective-permute-start.5) | collective-permute-done | bytes 131104 | tf_op jit(solution)/shard_map/ppermute | solution.py:300
  28.0 0.0 copy-start.7
  28.0 1.8 %collective-permute-done.6.refs_7_ = bf16[128,512]{1,0:T(8,128)(2,1)S(1)} collective-permute-done((bf16[128,512]{1,0:T(8,128)(2,1)S(1)}, bf16[128,512]{1,0:T(8,128)(2,1)S(1)}, u32[]{:S(2)}, u32[]{:S(2)}) %collective-permute-start.6) | collective-permute-done | bytes 131104 | tf_op jit(solution)/shard_map/ppermute | solution.py:301
  29.8 0.0 copy-start.8
  29.8 0.8 %collective-permute-done.4.refs_5_ = bf16[128,512]{1,0:T(8,128)(2,1)S(1)} collective-permute-done((bf16[128,512]{1,0:T(8,128)(2,1)S(1)}, bf16[128,512]{1,0:T(8,128)(2,1)S(1)}, u32[]{:S(2)}, u32[]{:S(2)}) %collective-permute-start.4) | collective-permute-done | bytes 131104 | tf_op jit(solution)/shard_map/ppermute | solution.py:299
  30.7 0.0 copy-start.9
  30.7 0.0 collective-permute-done.8.refs_11_
  30.7 0.0 copy-start.2
  30.7 0.0 collective-permute-done.7.refs_9_
  30.7 0.0 copy-start.1
  30.7 0.0 copy-done.3
  30.7 0.0 copy-done.4
  30.7 0.0 copy-done.5
  30.7 0.0 copy-done.6
  30.7 0.0 copy-done.7
  30.7 0.0 copy-done.8
  30.7 0.6 copy-done.9
  31.3 0.1 copy-done.2
  31.4 0.2 copy-done.1
  31.6 6.4 %terms.1 = (bf16[1024,512]{1,0:T(8,128)(2,1)}, bf16[1040,1536]{1,0:T(8,128)(2,1)}) custom-call(bf16[128,512]{1,0:T(8,128)(2,1)} %bitcast.13, bf16[128,512]{1,0:T(8,128)(2,1)} %copy-done.6, bf16[128,512]{1,0:T(8,128)(2,1)} %copy-done.5, bf16[128,512]{1,0:T(8,128)(2,1)} %copy-done.4, bf16[128,512]{1,0:T(8,128)(2,1)} %copy-done.3, bf16[128,512]{1,0:T(8,128)(2,1)} %copy-done.9, ...), custom_call_target="tpu_custom_call" | custom-call | tf_op jit(solution)/shard_map/terms/pallas_call | solution.py:69
  38.1 5.4 %all-to-all-start = ((bf16[8,128,512]{2,1,0:T(8,128)(2,1)}), bf16[8,128,512]{2,1,0:T(8,128)(2,1)S(1)}, u32[]{:S(2)}, u32[]{:S(2)}) async-start(bf16[8,128,512]{2,1,0:T(8,128)(2,1)} %bitcast.7), calls=%async_computation | async-start | bytes 2097152 | tf_op jit(solution)/shard_map/all_to_all | solution.py:323
  43.5 0.0 copy-start
  43.5 1.9 %copy-done = bf16[1040,1536]{1,0:T(8,128)(2,1)S(1)} copy-done((bf16[1040,1536]{1,0:T(8,128)(2,1)S(1)}, bf16[1040,1536]{1,0:T(8,128)(2,1)}, u32[]{:S(2)}) %copy-start) | copy-done | bytes 3194904
  45.4 1.3 %emb_terms.1 = (f32[528,512]{1,0:T(8,128)S(1)}, bf16[544,512]{1,0:T(8,128)(2,1)S(1)}) custom-call(bf16[1040,1536]{1,0:T(8,128)(2,1)S(1)} %copy-done), custom_call_target="tpu_custom_call" | custom-call | tf_op jit(solution)/shard_map/emb_terms/pallas_call | solution.py:69
  46.7 0.3 collective-permute-start.9
  47.0 1.9 %collective-permute-done.9.got_ref = bf16[544,512]{1,0:T(8,128)(2,1)S(1)} collective-permute-done((bf16[544,512]{1,0:T(8,128)(2,1)S(1)}, bf16[544,512]{1,0:T(8,128)(2,1)S(1)}, u32[]{:S(2)}, u32[]{:S(2)}) %collective-permute-start.9) | collective-permute-done | bytes 557088 | tf_op jit(solution)/shard_map/ppermute | solution.py:328
  48.9 0.1 join_cores.1
  49.0 1.1 %collective-permute-start.10 = (bf16[144,512]{1,0:T(8,128)(2,1)S(1)}, bf16[144,512]{1,0:T(8,128)(2,1)S(1)}, u32[]{:S(2)}, u32[]{:S(2)}) collective-permute-start(bf16[144,512]{1,0:T(8,128)(2,1)S(1)} %get-tuple-element.26), channel_id=1, source_target_pairs={{0,128},{2,130},{4,132},{6,134},{8,136},{10,138},{12,140},{14,142}... | collective-permute-start | bytes 442376 | tf_op jit(solution)/shard_map/ppermute | solution.py:332
  50.1 3.0 %collective-permute-start.11 = (bf16[144,512]{1,0:T(8,128)(2,1)S(1)}, bf16[144,512]{1,0:T(8,128)(2,1)S(1)}, u32[]{:S(2)}, u32[]{:S(2)}) collective-permute-start(bf16[144,512]{1,0:T(8,128)(2,1)S(1)} %get-tuple-element.27), channel_id=1, source_target_pairs={{0,1},{2,3},{4,5},{6,7},{8,9},{10,11},{12,13},{14,15},{16,17},{18,... | collective-permute-start | bytes 442376 | tf_op jit(solution)/shard_map/ppermute | solution.py:332
  53.1 1.5 %collective-permute-start.12 = (bf16[144,512]{1,0:T(8,128)(2,1)S(1)}, bf16[144,512]{1,0:T(8,128)(2,1)S(1)}, u32[]{:S(2)}, u32[]{:S(2)}) collective-permute-start(bf16[144,512]{1,0:T(8,128)(2,1)S(1)} %get-tuple-element.28), channel_id=1, source_target_pairs={{0,129},{2,131},{4,133},{6,135},{8,137},{10,139},{12,141},{14,143}... | collective-permute-start | bytes 442376 | tf_op jit(solution)/shard_map/ppermute | solution.py:332
  54.6 1.6 %collective-permute-done.10.refs_1_ = bf16[144,512]{1,0:T(8,128)(2,1)S(1)} collective-permute-done((bf16[144,512]{1,0:T(8,128)(2,1)S(1)}, bf16[144,512]{1,0:T(8,128)(2,1)S(1)}, u32[]{:S(2)}, u32[]{:S(2)}) %collective-permute-start.10) | collective-permute-done | bytes 147488 | tf_op jit(solution)/shard_map/ppermute | solution.py:332
  56.2 3.9 %collective-permute-done.11.refs_2_ = bf16[144,512]{1,0:T(8,128)(2,1)S(1)} collective-permute-done((bf16[144,512]{1,0:T(8,128)(2,1)S(1)}, bf16[144,512]{1,0:T(8,128)(2,1)S(1)}, u32[]{:S(2)}, u32[]{:S(2)}) %collective-permute-start.11) | collective-permute-done | bytes 147488 | tf_op jit(solution)/shard_map/ppermute | solution.py:332
  60.1 0.0 collective-permute-done.12.refs_3_
  60.1 0.1 sum_y.1
  60.2 1.6 %collective-permute-start.13 = (bf16[48,512]{1,0:T(8,128)(2,1)S(1)}, bf16[48,512]{1,0:T(8,128)(2,1)S(1)}, u32[]{:S(2)}, u32[]{:S(2)}) collective-permute-start(bf16[48,512]{1,0:T(8,128)(2,1)S(1)} %get-tuple-element.30), channel_id=1, source_target_pairs={{0,32},{16,48},{32,64},{48,80},{64,96},{80,112},{96,0},{112,16},{1... | collective-permute-start | bytes 147464 | tf_op jit(solution)/shard_map/ppermute | solution.py:340
  61.8 2.7 %collective-permute-start.14 = (bf16[48,512]{1,0:T(8,128)(2,1)S(1)}, bf16[48,512]{1,0:T(8,128)(2,1)S(1)}, u32[]{:S(2)}, u32[]{:S(2)}) collective-permute-start(bf16[48,512]{1,0:T(8,128)(2,1)S(1)} %get-tuple-element.31), channel_id=1, source_target_pairs={{0,64},{16,80},{32,96},{48,112},{64,0},{80,16},{96,32},{112,48},{1... | collective-permute-start | bytes 147464 | tf_op jit(solution)/shard_map/ppermute | solution.py:340
  64.5 1.4 %collective-permute-start.15 = (bf16[48,512]{1,0:T(8,128)(2,1)S(1)}, bf16[48,512]{1,0:T(8,128)(2,1)S(1)}, u32[]{:S(2)}, u32[]{:S(2)}) collective-permute-start(bf16[48,512]{1,0:T(8,128)(2,1)S(1)} %get-tuple-element.32), channel_id=1, source_target_pairs={{0,96},{16,112},{32,0},{48,16},{64,32},{80,48},{96,64},{112,80},{1... | collective-permute-start | bytes 147464 | tf_op jit(solution)/shard_map/ppermute | solution.py:340
  66.0 0.0 collective-permute-done.13.refs_1_
  66.0 1.4 %collective-permute-done.14.refs_2_ = bf16[48,512]{1,0:T(8,128)(2,1)S(1)} collective-permute-done((bf16[48,512]{1,0:T(8,128)(2,1)S(1)}, bf16[48,512]{1,0:T(8,128)(2,1)S(1)}, u32[]{:S(2)}, u32[]{:S(2)}) %collective-permute-start.14) | collective-permute-done | bytes 49184 | tf_op jit(solution)/shard_map/ppermute | solution.py:340
  67.4 1.2 %collective-permute-done.15.refs_3_ = bf16[48,512]{1,0:T(8,128)(2,1)S(1)} collective-permute-done((bf16[48,512]{1,0:T(8,128)(2,1)S(1)}, bf16[48,512]{1,0:T(8,128)(2,1)S(1)}, u32[]{:S(2)}, u32[]{:S(2)}) %collective-permute-start.15) | collective-permute-done | bytes 49184 | tf_op jit(solution)/shard_map/ppermute | solution.py:340
  68.6 0.7 sum_x.1
  69.3 0.0 all-to-all-done
  69.3 0.8 %sum_returned.1 = bf16[128,512]{1,0:T(8,128)(2,1)} custom-call(bf16[1024,512]{1,0:T(8,128)(2,1)S(1)} %bitcast.6), custom_call_target="tpu_custom_call" | custom-call | tf_op jit(solution)/shard_map/sum_returned/pallas_call | solution.py:69
Async XLA Ops:
  0.6 30.0 %collective-permute-start.7 = (bf16[512,512]{1,0:T(8,128)(2,1)}, bf16[512,512]{1,0:T(8,128)(2,1)S(1)}, u32[]{:S(2)}, u32[]{:S(2)}) collective-permute-start(bf16[512,512]{1,0:T(8,128)(2,1)} %refs_8_.1), channel_id=1, source_target_pairs={{0,1},{1,0},{2,3},{3,2},{4,5},{5,4},{6,7},{7,6},{8,9},{9,8},{10,11... | collective-permute-start | bytes 1572872 | tf_op jit(solution)/shard_map/ppermute | solution.py:287
  3.9 9.3 %collective-permute-start.3 = (bf16[128,512]{1,0:T(8,128)(2,1)}, bf16[128,512]{1,0:T(8,128)(2,1)S(1)}, u32[]{:S(2)}, u32[]{:S(2)}) collective-permute-start(bf16[128,512]{1,0:T(8,128)(2,1)} %bitcast.9), channel_id=1, source_target_pairs={{0,12},{1,13},{2,14},{3,15},{4,0},{5,1},{6,2},{7,3},{8,4},{9,5},{1... | collective-permute-start | bytes 393224 | tf_op jit(solution)/shard_map/ppermute | solution.py:289
  11.4 19.2 %collective-permute-start.8 = (f32[136,512]{1,0:T(8,128)}, f32[136,512]{1,0:T(8,128)S(1)}, u32[]{:S(2)}, u32[]{:S(2)}) collective-permute-start(f32[136,512]{1,0:T(8,128)} %get-tuple-element.20), channel_id=1, source_target_pairs={{0,1},{1,0},{2,3},{3,2},{4,5},{5,4},{6,7},{7,6},{8,9},{9,8},{10,11... | collective-permute-start | bytes 835592 | tf_op jit(solution)/shard_map/ppermute | solution.py:298
  11.8 9.6 %collective-permute-start.2 = (bf16[128,512]{1,0:T(8,128)(2,1)}, bf16[128,512]{1,0:T(8,128)(2,1)S(1)}, u32[]{:S(2)}, u32[]{:S(2)}) collective-permute-start(bf16[128,512]{1,0:T(8,128)(2,1)} %bitcast.10), channel_id=1, source_target_pairs={{0,4},{1,5},{2,6},{3,7},{4,8},{5,9},{6,10},{7,11},{8,12},{9,13},{1... | collective-permute-start | bytes 393224 | tf_op jit(solution)/shard_map/ppermute | solution.py:288
  11.8 10.4 %collective-permute-start.1 = (bf16[128,512]{1,0:T(8,128)(2,1)}, bf16[128,512]{1,0:T(8,128)(2,1)S(1)}, u32[]{:S(2)}, u32[]{:S(2)}) collective-permute-start(bf16[128,512]{1,0:T(8,128)(2,1)} %bitcast.11), channel_id=1, source_target_pairs={{0,14},{1,15},{2,0},{3,1},{4,2},{5,3},{6,4},{7,5},{8,6},{9,7},{10,... | collective-permute-start | bytes 393224 | tf_op jit(solution)/shard_map/ppermute | solution.py:303
  13.2 17.5 %copy-start.3 = (bf16[128,512]{1,0:T(8,128)(2,1)}, bf16[128,512]{1,0:T(8,128)(2,1)S(1)}, u32[]{:S(2)}) copy-start(bf16[128,512]{1,0:T(8,128)(2,1)S(1)} %collective-permute-done.3.refs_4_) | copy-start | bytes 393220
  13.2 9.1 %collective-permute-start = (bf16[128,512]{1,0:T(8,128)(2,1)}, bf16[128,512]{1,0:T(8,128)(2,1)S(1)}, u32[]{:S(2)}, u32[]{:S(2)}) collective-permute-start(bf16[128,512]{1,0:T(8,128)(2,1)} %bitcast.12), channel_id=1, source_target_pairs={{0,2},{1,3},{2,4},{3,5},{4,6},{5,7},{6,8},{7,9},{8,10},{9,11},{10,... | collective-permute-start | bytes 393224 | tf_op jit(solution)/shard_map/ppermute | solution.py:302
  21.4 9.3 %copy-start.4 = (bf16[128,512]{1,0:T(8,128)(2,1)}, bf16[128,512]{1,0:T(8,128)(2,1)S(1)}, u32[]{:S(2)}) copy-start(bf16[128,512]{1,0:T(8,128)(2,1)S(1)} %collective-permute-done.2.refs_3_) | copy-start | bytes 393220
  21.4 6.6 %collective-permute-start.5 = (bf16[128,512]{1,0:T(8,128)(2,1)S(1)}, bf16[128,512]{1,0:T(8,128)(2,1)S(1)}, u32[]{:S(2)}, u32[]{:S(2)}) collective-permute-start(bf16[128,512]{1,0:T(8,128)(2,1)S(1)} %collective-permute-done.3.refs_4_), channel_id=1, source_target_pairs={{0,14},{1,15},{2,0},{3,1},{4,2},{5,3},{6,4},{7,5},{8,6},{9,7},{10,... | collective-permute-start | bytes 393224 | tf_op jit(solution)/shard_map/ppermute | solution.py:300
  22.2 8.5 %copy-start.5 = (bf16[128,512]{1,0:T(8,128)(2,1)}, bf16[128,512]{1,0:T(8,128)(2,1)S(1)}, u32[]{:S(2)}) copy-start(bf16[128,512]{1,0:T(8,128)(2,1)S(1)} %collective-permute-done.1.refs_2_) | copy-start | bytes 393220
  22.2 7.6 %collective-permute-start.6 = (bf16[128,512]{1,0:T(8,128)(2,1)S(1)}, bf16[128,512]{1,0:T(8,128)(2,1)S(1)}, u32[]{:S(2)}, u32[]{:S(2)}) collective-permute-start(bf16[128,512]{1,0:T(8,128)(2,1)S(1)} %collective-permute-done.2.refs_3_), channel_id=1, source_target_pairs={{0,4},{1,5},{2,6},{3,7},{4,8},{5,9},{6,10},{7,11},{8,12},{9,13},{1... | collective-permute-start | bytes 393224 | tf_op jit(solution)/shard_map/ppermute | solution.py:301
  22.3 8.5 %copy-start.6 = (bf16[128,512]{1,0:T(8,128)(2,1)}, bf16[128,512]{1,0:T(8,128)(2,1)S(1)}, u32[]{:S(2)}) copy-start(bf16[128,512]{1,0:T(8,128)(2,1)S(1)} %collective-permute-done.refs_1_) | copy-start | bytes 393220
  22.3 8.4 %collective-permute-start.4 = (bf16[128,512]{1,0:T(8,128)(2,1)S(1)}, bf16[128,512]{1,0:T(8,128)(2,1)S(1)}, u32[]{:S(2)}, u32[]{:S(2)}) collective-permute-start(bf16[128,512]{1,0:T(8,128)(2,1)S(1)} %collective-permute-done.2.refs_3_), channel_id=1, source_target_pairs={{0,2},{1,3},{2,4},{3,5},{4,6},{5,7},{6,8},{7,9},{8,10},{9,11},{10,... | collective-permute-start | bytes 393224 | tf_op jit(solution)/shard_map/ppermute | solution.py:299
  28.0 2.8 %copy-start.7 = (bf16[128,512]{1,0:T(8,128)(2,1)}, bf16[128,512]{1,0:T(8,128)(2,1)S(1)}, u32[]{:S(2)}) copy-start(bf16[128,512]{1,0:T(8,128)(2,1)S(1)} %collective-permute-done.5.refs_6_) | copy-start | bytes 393220
  29.8 0.9 %copy-start.8 = (bf16[128,512]{1,0:T(8,128)(2,1)}, bf16[128,512]{1,0:T(8,128)(2,1)S(1)}, u32[]{:S(2)}) copy-start(bf16[128,512]{1,0:T(8,128)(2,1)S(1)} %collective-permute-done.6.refs_7_) | copy-start | bytes 393220
  30.7 0.7 copy-start.9
  30.7 0.7 %copy-start.2 = (f32[136,512]{1,0:T(8,128)}, f32[136,512]{1,0:T(8,128)S(1)}, u32[]{:S(2)}) copy-start(f32[136,512]{1,0:T(8,128)S(1)} %collective-permute-done.8.refs_11_) | copy-start | bytes 835588
  30.7 0.9 %copy-start.1 = (bf16[512,512]{1,0:T(8,128)(2,1)}, bf16[512,512]{1,0:T(8,128)(2,1)S(1)}, u32[]{:S(2)}) copy-start(bf16[512,512]{1,0:T(8,128)(2,1)S(1)} %collective-permute-done.7.refs_9_) | copy-start | bytes 1572868
  38.1 31.3 %all-to-all-start = ((bf16[8,128,512]{2,1,0:T(8,128)(2,1)}), bf16[8,128,512]{2,1,0:T(8,128)(2,1)S(1)}, u32[]{:S(2)}, u32[]{:S(2)}) async-start(bf16[8,128,512]{2,1,0:T(8,128)(2,1)} %bitcast.7), calls=%async_computation | async-start | bytes 2097152 | tf_op jit(solution)/shard_map/all_to_all | solution.py:323
  43.5 1.9 %copy-start = (bf16[1040,1536]{1,0:T(8,128)(2,1)S(1)}, bf16[1040,1536]{1,0:T(8,128)(2,1)}, u32[]{:S(2)}) copy-start(bf16[1040,1536]{1,0:T(8,128)(2,1)} %get-tuple-element.22.low_ref) | copy-start | bytes 9584644
  46.7 2.2 %collective-permute-start.9 = (bf16[544,512]{1,0:T(8,128)(2,1)S(1)}, bf16[544,512]{1,0:T(8,128)(2,1)S(1)}, u32[]{:S(2)}, u32[]{:S(2)}) collective-permute-start(bf16[544,512]{1,0:T(8,128)(2,1)S(1)} %get-tuple-element.24), channel_id=1, source_target_pairs={{0,16},{16,0},{32,48},{48,32},{64,80},{80,64},{96,112},{112,96},{1... | collective-permute-start | bytes 1671176 | tf_op jit(solution)/shard_map/ppermute | solution.py:328
  49.0 7.2 %collective-permute-start.10 = (bf16[144,512]{1,0:T(8,128)(2,1)S(1)}, bf16[144,512]{1,0:T(8,128)(2,1)S(1)}, u32[]{:S(2)}, u32[]{:S(2)}) collective-permute-start(bf16[144,512]{1,0:T(8,128)(2,1)S(1)} %get-tuple-element.26), channel_id=1, source_target_pairs={{0,128},{2,130},{4,132},{6,134},{8,136},{10,138},{12,140},{14,142}... | collective-permute-start | bytes 442376 | tf_op jit(solution)/shard_map/ppermute | solution.py:332
  50.1 10.0 %collective-permute-start.11 = (bf16[144,512]{1,0:T(8,128)(2,1)S(1)}, bf16[144,512]{1,0:T(8,128)(2,1)S(1)}, u32[]{:S(2)}, u32[]{:S(2)}) collective-permute-start(bf16[144,512]{1,0:T(8,128)(2,1)S(1)} %get-tuple-element.27), channel_id=1, source_target_pairs={{0,1},{2,3},{4,5},{6,7},{8,9},{10,11},{12,13},{14,15},{16,17},{18,... | collective-permute-start | bytes 442376 | tf_op jit(solution)/shard_map/ppermute | solution.py:332
  53.1 7.0 %collective-permute-start.12 = (bf16[144,512]{1,0:T(8,128)(2,1)S(1)}, bf16[144,512]{1,0:T(8,128)(2,1)S(1)}, u32[]{:S(2)}, u32[]{:S(2)}) collective-permute-start(bf16[144,512]{1,0:T(8,128)(2,1)S(1)} %get-tuple-element.28), channel_id=1, source_target_pairs={{0,129},{2,131},{4,133},{6,135},{8,137},{10,139},{12,141},{14,143}... | collective-permute-start | bytes 442376 | tf_op jit(solution)/shard_map/ppermute | solution.py:332
  60.2 5.8 %collective-permute-start.13 = (bf16[48,512]{1,0:T(8,128)(2,1)S(1)}, bf16[48,512]{1,0:T(8,128)(2,1)S(1)}, u32[]{:S(2)}, u32[]{:S(2)}) collective-permute-start(bf16[48,512]{1,0:T(8,128)(2,1)S(1)} %get-tuple-element.30), channel_id=1, source_target_pairs={{0,32},{16,48},{32,64},{48,80},{64,96},{80,112},{96,0},{112,16},{1... | collective-permute-start | bytes 147464 | tf_op jit(solution)/shard_map/ppermute | solution.py:340
  61.8 5.6 %collective-permute-start.14 = (bf16[48,512]{1,0:T(8,128)(2,1)S(1)}, bf16[48,512]{1,0:T(8,128)(2,1)S(1)}, u32[]{:S(2)}, u32[]{:S(2)}) collective-permute-start(bf16[48,512]{1,0:T(8,128)(2,1)S(1)} %get-tuple-element.31), channel_id=1, source_target_pairs={{0,64},{16,80},{32,96},{48,112},{64,0},{80,16},{96,32},{112,48},{1... | collective-permute-start | bytes 147464 | tf_op jit(solution)/shard_map/ppermute | solution.py:340
  64.5 4.1 %collective-permute-start.15 = (bf16[48,512]{1,0:T(8,128)(2,1)S(1)}, bf16[48,512]{1,0:T(8,128)(2,1)S(1)}, u32[]{:S(2)}, u32[]{:S(2)}) collective-permute-start(bf16[48,512]{1,0:T(8,128)(2,1)S(1)} %get-tuple-element.32), channel_id=1, source_target_pairs={{0,96},{16,112},{32,0},{48,16},{64,32},{80,48},{96,64},{112,80},{1... | collective-permute-start | bytes 147464 | tf_op jit(solution)/shard_map/ppermute | solution.py:340

commit v5 on v4

--- a/solution.py
+++ b/solution.py
@@ -181,13 +181,12 @@
         half = pl.ds(i * WIDE, WIDE)
         stored.append(fetch(lows.at[:, half], low_out.at[:, half], 12 + i))
     sent = []
-    for slot in range(0, 8, 2):
-        backs[slot * ROWS : (slot + 2) * ROWS, :] = jnp.dot(
-            lows[slot * ROWS : (slot + 2) * ROWS, :],
-            embs[...],
-            preferred_element_type=jnp.float32,
+    for slot in range(0, 8, 4):
+        rows = slice(slot * ROWS, (slot + 4) * ROWS)
+        backs[rows, :] = jnp.dot(
+            lows[rows, :], embs[...], preferred_element_type=jnp.float32
         ).astype(jnp.bfloat16)
-        for one in (slot, slot + 1):
+        for one in range(slot, slot + 4):
             source = backs.at[pl.ds(one * ROWS, ROWS)]
             target = back_out.at[pl.ds(pl.multiple_of(owners[one] * ROWS, ROWS), ROWS)]
             sent.append(fetch(source, target, one))

time: 71.3 us -> 71.4 us (level)
  no operation moved by 1% of the time
where the time goes in v5:
time: 71.4 us; the launch traced here: 70.2 us
  starting transfers between devices  31.1 us (44%)
  waiting for transfers between devices  23.9 us (33%)
  Pallas kernels  11.6 us (16%)
  local copies, waits for them, and re-layouts  2.79 us (4%)
  between operations  0.76 us (1%)
    pallas_call x7, Pallas kernels, call(): pl.pallas_call(kernel, out_shape=[jax.ShapeDtypeStruct(shape, kind) for s...  11.6 us
    ppermute x1, waiting for transfers between devices, per_device(): two = lax.ppermute(mine, BOTH, z_apart(2))  6.39 us
    ppermute x3, starting transfers between devices, per_device(): lax.ppermute(part, 'dp', x_shift(d))  5.73 us
    ppermute x3, starting transfers between devices, per_device(): lax.ppermute(part, BOTH, y_shift(d))  5.63 us
    ppermute x3, waiting for transfers between devices, per_device(): lax.ppermute(part, BOTH, y_shift(d))  5.49 us
    all_to_all x1, starting transfers between devices, per_device(): lax.all_to_all(back, 'task', 0, 0, tiled=True, axis_index_groups=column_g...  5.45 us
    ppermute x1, starting transfers between devices, per_device(): two_back = lax.ppermute(mine, BOTH, z_apart(-2))  5.4 us
    ppermute x1, waiting for transfers between devices, per_device(): three_back = lax.ppermute(two_back, BOTH, z_apart(-1))  4.33 us
  transfers between devices with their start and end apart: 17, of which 10 were waited for; matrix products, arithmetic and copies ran while one was open for 0% of the time, Pallas kernels for 6%

profile of v5, /device:TPU:32, one launch (start us, length us, event | category | flops | bytes accessed | tf_op | source)
XLA Modules:
  0.0 70.2 jit_solution(8271952888583881352)
XLA Ops:
  0.6 3.3 %collective-permute-start.7 = (bf16[512,512]{1,0:T(8,128)(2,1)}, bf16[512,512]{1,0:T(8,128)(2,1)S(1)}, u32[]{:S(2)}, u32[]{:S(2)}) collective-permute-start(bf16[512,512]{1,0:T(8,128)(2,1)} %refs_8_.1), channel_id=1, source_target_pairs={{0,1},{1,0},{2,3},{3,2},{4,5},{5,4},{6,7},{7,6},{8,9},{9,8},{10,11... | collective-permute-start | bytes 1572872 | tf_op jit(solution)/shard_map/ppermute | solution.py:286
  3.9 5.4 %collective-permute-start.3 = (bf16[128,512]{1,0:T(8,128)(2,1)}, bf16[128,512]{1,0:T(8,128)(2,1)S(1)}, u32[]{:S(2)}, u32[]{:S(2)}) collective-permute-start(bf16[128,512]{1,0:T(8,128)(2,1)} %bitcast.9), channel_id=1, source_target_pairs={{0,12},{1,13},{2,14},{3,15},{4,0},{5,1},{6,2},{7,3},{8,4},{9,5},{1... | collective-permute-start | bytes 393224 | tf_op jit(solution)/shard_map/ppermute | solution.py:288
  9.3 2.1 %pack_events.1 = (f32[152,512]{1,0:T(8,128)}, f32[136,512]{1,0:T(8,128)}) custom-call(s32[2,4]{1,0:T(2,128)} %risk_ref.1, s32[9]{0:T(128)} %bounds_ref.1, s32[256,512]{1,0:T(8,128)} %time_ref.1, s32[256,512]{1,0:T(8,128)} %cens_ref.1, f32[8,512]{1,0:T(8,128)} %bitcast.14), custom_call_target="tpu_custom_call" | custom-call | tf_op jit(solution)/shard_map/pack_events/pallas_call | solution.py:69
  11.4 0.3 collective-permute-start.8
  11.8 0.0 collective-permute-start.2
  11.8 1.0 %collective-permute-start.1 = (bf16[128,512]{1,0:T(8,128)(2,1)}, bf16[128,512]{1,0:T(8,128)(2,1)S(1)}, u32[]{:S(2)}, u32[]{:S(2)}) collective-permute-start(bf16[128,512]{1,0:T(8,128)(2,1)} %bitcast.11), channel_id=1, source_target_pairs={{0,14},{1,15},{2,0},{3,1},{4,2},{5,3},{6,4},{7,5},{8,6},{9,7},{10,... | collective-permute-start | bytes 393224 | tf_op jit(solution)/shard_map/ppermute | solution.py:302
  12.8 0.4 collective-permute-done.3.refs_4_
  13.2 0.0 copy-start.3
  13.2 1.8 %collective-permute-start = (bf16[128,512]{1,0:T(8,128)(2,1)}, bf16[128,512]{1,0:T(8,128)(2,1)S(1)}, u32[]{:S(2)}, u32[]{:S(2)}) collective-permute-start(bf16[128,512]{1,0:T(8,128)(2,1)} %bitcast.12), channel_id=1, source_target_pairs={{0,2},{1,3},{2,4},{3,5},{4,6},{5,7},{6,8},{7,9},{8,10},{9,11},{10,... | collective-permute-start | bytes 393224 | tf_op jit(solution)/shard_map/ppermute | solution.py:301
  15.0 6.4 %collective-permute-done.2.refs_3_ = bf16[128,512]{1,0:T(8,128)(2,1)S(1)} collective-permute-done((bf16[128,512]{1,0:T(8,128)(2,1)}, bf16[128,512]{1,0:T(8,128)(2,1)S(1)}, u32[]{:S(2)}, u32[]{:S(2)}) %collective-permute-start.2) | collective-permute-done | bytes 131104 | tf_op jit(solution)/shard_map/ppermute | solution.py:287
  21.4 0.0 copy-start.4
  21.4 0.9 %collective-permute-start.5 = (bf16[128,512]{1,0:T(8,128)(2,1)S(1)}, bf16[128,512]{1,0:T(8,128)(2,1)S(1)}, u32[]{:S(2)}, u32[]{:S(2)}) collective-permute-start(bf16[128,512]{1,0:T(8,128)(2,1)S(1)} %collective-permute-done.3.refs_4_), channel_id=1, source_target_pairs={{0,14},{1,15},{2,0},{3,1},{4,2},{5,3},{6,4},{7,5},{8,6},{9,7},{10,... | collective-permute-start | bytes 393224 | tf_op jit(solution)/shard_map/ppermute | solution.py:299
  22.2 0.0 collective-permute-done.1.refs_2_
  22.2 0.0 copy-start.5
  22.2 0.0 collective-permute-start.6
  22.2 0.0 collective-permute-done.refs_1_
  22.3 0.0 copy-start.6
  22.3 1.4 %collective-permute-start.4 = (bf16[128,512]{1,0:T(8,128)(2,1)S(1)}, bf16[128,512]{1,0:T(8,128)(2,1)S(1)}, u32[]{:S(2)}, u32[]{:S(2)}) collective-permute-start(bf16[128,512]{1,0:T(8,128)(2,1)S(1)} %collective-permute-done.2.refs_3_), channel_id=1, source_target_pairs={{0,2},{1,3},{2,4},{3,5},{4,6},{5,7},{6,8},{7,9},{8,10},{9,11},{10,... | collective-permute-start | bytes 393224 | tf_op jit(solution)/shard_map/ppermute | solution.py:298
  23.6 4.3 %collective-permute-done.5.refs_6_ = bf16[128,512]{1,0:T(8,128)(2,1)S(1)} collective-permute-done((bf16[128,512]{1,0:T(8,128)(2,1)S(1)}, bf16[128,512]{1,0:T(8,128)(2,1)S(1)}, u32[]{:S(2)}, u32[]{:S(2)}) %collective-permute-start.5) | collective-permute-done | bytes 131104 | tf_op jit(solution)/shard_map/ppermute | solution.py:299
  28.0 0.0 copy-start.7
  28.0 1.8 %collective-permute-done.6.refs_7_ = bf16[128,512]{1,0:T(8,128)(2,1)S(1)} collective-permute-done((bf16[128,512]{1,0:T(8,128)(2,1)S(1)}, bf16[128,512]{1,0:T(8,128)(2,1)S(1)}, u32[]{:S(2)}, u32[]{:S(2)}) %collective-permute-start.6) | collective-permute-done | bytes 131104 | tf_op jit(solution)/shard_map/ppermute | solution.py:300
  29.8 0.0 copy-start.8
  29.8 0.8 %collective-permute-done.4.refs_5_ = bf16[128,512]{1,0:T(8,128)(2,1)S(1)} collective-permute-done((bf16[128,512]{1,0:T(8,128)(2,1)S(1)}, bf16[128,512]{1,0:T(8,128)(2,1)S(1)}, u32[]{:S(2)}, u32[]{:S(2)}) %collective-permute-start.4) | collective-permute-done | bytes 131104 | tf_op jit(solution)/shard_map/ppermute | solution.py:298
  30.7 0.0 copy-start.9
  30.7 0.0 collective-permute-done.8.refs_11_
  30.7 0.0 copy-start.2
  30.7 0.0 collective-permute-done.7.refs_9_
  30.7 0.0 copy-start.1
  30.7 0.0 copy-done.3
  30.7 0.0 copy-done.4
  30.7 0.0 copy-done.5
  30.7 0.0 copy-done.6
  30.7 0.0 copy-done.7
  30.7 0.0 copy-done.8
  30.7 0.6 copy-done.9
  31.3 0.1 copy-done.2
  31.4 0.2 copy-done.1
  31.6 6.5 %terms.1 = (bf16[1024,512]{1,0:T(8,128)(2,1)}, bf16[1040,1536]{1,0:T(8,128)(2,1)}) custom-call(bf16[128,512]{1,0:T(8,128)(2,1)} %bitcast.13, bf16[128,512]{1,0:T(8,128)(2,1)} %copy-done.6, bf16[128,512]{1,0:T(8,128)(2,1)} %copy-done.5, bf16[128,512]{1,0:T(8,128)(2,1)} %copy-done.4, bf16[128,512]{1,0:T(8,128)(2,1)} %copy-done.3, bf16[128,512]{1,0:T(8,128)(2,1)} %copy-done.9, ...), custom_call_target="tpu_custom_call" | custom-call | tf_op jit(solution)/shard_map/terms/pallas_call | solution.py:69
  38.1 5.4 %all-to-all-start = ((bf16[8,128,512]{2,1,0:T(8,128)(2,1)}), bf16[8,128,512]{2,1,0:T(8,128)(2,1)S(1)}, u32[]{:S(2)}, u32[]{:S(2)}) async-start(bf16[8,128,512]{2,1,0:T(8,128)(2,1)} %bitcast.7), calls=%async_computation | async-start | bytes 2097152 | tf_op jit(solution)/shard_map/all_to_all | solution.py:322
  43.6 0.0 copy-start
  43.6 1.9 %copy-done = bf16[1040,1536]{1,0:T(8,128)(2,1)S(1)} copy-done((bf16[1040,1536]{1,0:T(8,128)(2,1)S(1)}, bf16[1040,1536]{1,0:T(8,128)(2,1)}, u32[]{:S(2)}) %copy-start) | copy-done | bytes 3194904
  45.5 1.3 %emb_terms.1 = (f32[528,512]{1,0:T(8,128)S(1)}, bf16[544,512]{1,0:T(8,128)(2,1)S(1)}) custom-call(bf16[1040,1536]{1,0:T(8,128)(2,1)S(1)} %copy-done), custom_call_target="tpu_custom_call" | custom-call | tf_op jit(solution)/shard_map/emb_terms/pallas_call | solution.py:69
  46.8 0.3 collective-permute-start.9
  47.1 1.9 %collective-permute-done.9.got_ref = bf16[544,512]{1,0:T(8,128)(2,1)S(1)} collective-permute-done((bf16[544,512]{1,0:T(8,128)(2,1)S(1)}, bf16[544,512]{1,0:T(8,128)(2,1)S(1)}, u32[]{:S(2)}, u32[]{:S(2)}) %collective-permute-start.9) | collective-permute-done | bytes 557088 | tf_op jit(solution)/shard_map/ppermute | solution.py:327
  49.0 0.1 join_cores.1
  49.1 1.1 %collective-permute-start.10 = (bf16[144,512]{1,0:T(8,128)(2,1)S(1)}, bf16[144,512]{1,0:T(8,128)(2,1)S(1)}, u32[]{:S(2)}, u32[]{:S(2)}) collective-permute-start(bf16[144,512]{1,0:T(8,128)(2,1)S(1)} %get-tuple-element.26), channel_id=1, source_target_pairs={{0,128},{2,130},{4,132},{6,134},{8,136},{10,138},{12,140},{14,142}... | collective-permute-start | bytes 442376 | tf_op jit(solution)/shard_map/ppermute | solution.py:331
  50.2 3.0 %collective-permute-start.11 = (bf16[144,512]{1,0:T(8,128)(2,1)S(1)}, bf16[144,512]{1,0:T(8,128)(2,1)S(1)}, u32[]{:S(2)}, u32[]{:S(2)}) collective-permute-start(bf16[144,512]{1,0:T(8,128)(2,1)S(1)} %get-tuple-element.27), channel_id=1, source_target_pairs={{0,1},{2,3},{4,5},{6,7},{8,9},{10,11},{12,13},{14,15},{16,17},{18,... | collective-permute-start | bytes 442376 | tf_op jit(solution)/shard_map/ppermute | solution.py:331
  53.2 1.5 %collective-permute-start.12 = (bf16[144,512]{1,0:T(8,128)(2,1)S(1)}, bf16[144,512]{1,0:T(8,128)(2,1)S(1)}, u32[]{:S(2)}, u32[]{:S(2)}) collective-permute-start(bf16[144,512]{1,0:T(8,128)(2,1)S(1)} %get-tuple-element.28), channel_id=1, source_target_pairs={{0,129},{2,131},{4,133},{6,135},{8,137},{10,139},{12,141},{14,143}... | collective-permute-start | bytes 442376 | tf_op jit(solution)/shard_map/ppermute | solution.py:331
  54.8 1.6 %collective-permute-done.10.refs_1_ = bf16[144,512]{1,0:T(8,128)(2,1)S(1)} collective-permute-done((bf16[144,512]{1,0:T(8,128)(2,1)S(1)}, bf16[144,512]{1,0:T(8,128)(2,1)S(1)}, u32[]{:S(2)}, u32[]{:S(2)}) %collective-permute-start.10) | collective-permute-done | bytes 147488 | tf_op jit(solution)/shard_map/ppermute | solution.py:331
  56.3 3.9 %collective-permute-done.11.refs_2_ = bf16[144,512]{1,0:T(8,128)(2,1)S(1)} collective-permute-done((bf16[144,512]{1,0:T(8,128)(2,1)S(1)}, bf16[144,512]{1,0:T(8,128)(2,1)S(1)}, u32[]{:S(2)}, u32[]{:S(2)}) %collective-permute-start.11) | collective-permute-done | bytes 147488 | tf_op jit(solution)/shard_map/ppermute | solution.py:331
  60.2 0.0 collective-permute-done.12.refs_3_
  60.2 0.1 sum_y.1
  60.3 1.6 %collective-permute-start.13 = (bf16[48,512]{1,0:T(8,128)(2,1)S(1)}, bf16[48,512]{1,0:T(8,128)(2,1)S(1)}, u32[]{:S(2)}, u32[]{:S(2)}) collective-permute-start(bf16[48,512]{1,0:T(8,128)(2,1)S(1)} %get-tuple-element.30), channel_id=1, source_target_pairs={{0,32},{16,48},{32,64},{48,80},{64,96},{80,112},{96,0},{112,16},{1... | collective-permute-start | bytes 147464 | tf_op jit(solution)/shard_map/ppermute | solution.py:339
  61.9 2.8 %collective-permute-start.14 = (bf16[48,512]{1,0:T(8,128)(2,1)S(1)}, bf16[48,512]{1,0:T(8,128)(2,1)S(1)}, u32[]{:S(2)}, u32[]{:S(2)}) collective-permute-start(bf16[48,512]{1,0:T(8,128)(2,1)S(1)} %get-tuple-element.31), channel_id=1, source_target_pairs={{0,64},{16,80},{32,96},{48,112},{64,0},{80,16},{96,32},{112,48},{1... | collective-permute-start | bytes 147464 | tf_op jit(solution)/shard_map/ppermute | solution.py:339
  64.6 1.4 %collective-permute-start.15 = (bf16[48,512]{1,0:T(8,128)(2,1)S(1)}, bf16[48,512]{1,0:T(8,128)(2,1)S(1)}, u32[]{:S(2)}, u32[]{:S(2)}) collective-permute-start(bf16[48,512]{1,0:T(8,128)(2,1)S(1)} %get-tuple-element.32), channel_id=1, source_target_pairs={{0,96},{16,112},{32,0},{48,16},{64,32},{80,48},{96,64},{112,80},{1... | collective-permute-start | bytes 147464 | tf_op jit(solution)/shard_map/ppermute | solution.py:339
  66.1 0.0 collective-permute-done.13.refs_1_
  66.1 1.4 %collective-permute-done.14.refs_2_ = bf16[48,512]{1,0:T(8,128)(2,1)S(1)} collective-permute-done((bf16[48,512]{1,0:T(8,128)(2,1)S(1)}, bf16[48,512]{1,0:T(8,128)(2,1)S(1)}, u32[]{:S(2)}, u32[]{:S(2)}) %collective-permute-start.14) | collective-permute-done | bytes 49184 | tf_op jit(solution)/shard_map/ppermute | solution.py:339
  67.5 1.2 %collective-permute-done.15.refs_3_ = bf16[48,512]{1,0:T(8,128)(2,1)S(1)} collective-permute-done((bf16[48,512]{1,0:T(8,128)(2,1)S(1)}, bf16[48,512]{1,0:T(8,128)(2,1)S(1)}, u32[]{:S(2)}, u32[]{:S(2)}) %collective-permute-start.15) | collective-permute-done | bytes 49184 | tf_op jit(solution)/shard_map/ppermute | solution.py:339
  68.7 0.7 sum_x.1
  69.4 0.0 all-to-all-done
  69.4 0.8 %sum_returned.1 = bf16[128,512]{1,0:T(8,128)(2,1)} custom-call(bf16[1024,512]{1,0:T(8,128)(2,1)S(1)} %bitcast.6), custom_call_target="tpu_custom_call" | custom-call | tf_op jit(solution)/shard_map/sum_returned/pallas_call | solution.py:69
Async XLA Ops:
  0.6 30.0 %collective-permute-start.7 = (bf16[512,512]{1,0:T(8,128)(2,1)}, bf16[512,512]{1,0:T(8,128)(2,1)S(1)}, u32[]{:S(2)}, u32[]{:S(2)}) collective-permute-start(bf16[512,512]{1,0:T(8,128)(2,1)} %refs_8_.1), channel_id=1, source_target_pairs={{0,1},{1,0},{2,3},{3,2},{4,5},{5,4},{6,7},{7,6},{8,9},{9,8},{10,11... | collective-permute-start | bytes 1572872 | tf_op jit(solution)/shard_map/ppermute | solution.py:286
  3.9 9.3 %collective-permute-start.3 = (bf16[128,512]{1,0:T(8,128)(2,1)}, bf16[128,512]{1,0:T(8,128)(2,1)S(1)}, u32[]{:S(2)}, u32[]{:S(2)}) collective-permute-start(bf16[128,512]{1,0:T(8,128)(2,1)} %bitcast.9), channel_id=1, source_target_pairs={{0,12},{1,13},{2,14},{3,15},{4,0},{5,1},{6,2},{7,3},{8,4},{9,5},{1... | collective-permute-start | bytes 393224 | tf_op jit(solution)/shard_map/ppermute | solution.py:288
  11.4 19.2 %collective-permute-start.8 = (f32[136,512]{1,0:T(8,128)}, f32[136,512]{1,0:T(8,128)S(1)}, u32[]{:S(2)}, u32[]{:S(2)}) collective-permute-start(f32[136,512]{1,0:T(8,128)} %get-tuple-element.20), channel_id=1, source_target_pairs={{0,1},{1,0},{2,3},{3,2},{4,5},{5,4},{6,7},{7,6},{8,9},{9,8},{10,11... | collective-permute-start | bytes 835592 | tf_op jit(solution)/shard_map/ppermute | solution.py:297
  11.8 9.6 %collective-permute-start.2 = (bf16[128,512]{1,0:T(8,128)(2,1)}, bf16[128,512]{1,0:T(8,128)(2,1)S(1)}, u32[]{:S(2)}, u32[]{:S(2)}) collective-permute-start(bf16[128,512]{1,0:T(8,128)(2,1)} %bitcast.10), channel_id=1, source_target_pairs={{0,4},{1,5},{2,6},{3,7},{4,8},{5,9},{6,10},{7,11},{8,12},{9,13},{1... | collective-permute-start | bytes 393224 | tf_op jit(solution)/shard_map/ppermute | solution.py:287
  11.8 10.4 %collective-permute-start.1 = (bf16[128,512]{1,0:T(8,128)(2,1)}, bf16[128,512]{1,0:T(8,128)(2,1)S(1)}, u32[]{:S(2)}, u32[]{:S(2)}) collective-permute-start(bf16[128,512]{1,0:T(8,128)(2,1)} %bitcast.11), channel_id=1, source_target_pairs={{0,14},{1,15},{2,0},{3,1},{4,2},{5,3},{6,4},{7,5},{8,6},{9,7},{10,... | collective-permute-start | bytes 393224 | tf_op jit(solution)/shard_map/ppermute | solution.py:302
  13.2 17.5 %copy-start.3 = (bf16[128,512]{1,0:T(8,128)(2,1)}, bf16[128,512]{1,0:T(8,128)(2,1)S(1)}, u32[]{:S(2)}) copy-start(bf16[128,512]{1,0:T(8,128)(2,1)S(1)} %collective-permute-done.3.refs_4_) | copy-start | bytes 393220
  13.2 9.1 %collective-permute-start = (bf16[128,512]{1,0:T(8,128)(2,1)}, bf16[128,512]{1,0:T(8,128)(2,1)S(1)}, u32[]{:S(2)}, u32[]{:S(2)}) collective-permute-start(bf16[128,512]{1,0:T(8,128)(2,1)} %bitcast.12), channel_id=1, source_target_pairs={{0,2},{1,3},{2,4},{3,5},{4,6},{5,7},{6,8},{7,9},{8,10},{9,11},{10,... | collective-permute-start | bytes 393224 | tf_op jit(solution)/shard_map/ppermute | solution.py:301
  21.4 9.3 %copy-start.4 = (bf16[128,512]{1,0:T(8,128)(2,1)}, bf16[128,512]{1,0:T(8,128)(2,1)S(1)}, u32[]{:S(2)}) copy-start(bf16[128,512]{1,0:T(8,128)(2,1)S(1)} %collective-permute-done.2.refs_3_) | copy-start | bytes 393220
  21.4 6.6 %collective-permute-start.5 = (bf16[128,512]{1,0:T(8,128)(2,1)S(1)}, bf16[128,512]{1,0:T(8,128)(2,1)S(1)}, u32[]{:S(2)}, u32[]{:S(2)}) collective-permute-start(bf16[128,512]{1,0:T(8,128)(2,1)S(1)} %collective-permute-done.3.refs_4_), channel_id=1, source_target_pairs={{0,14},{1,15},{2,0},{3,1},{4,2},{5,3},{6,4},{7,5},{8,6},{9,7},{10,... | collective-permute-start | bytes 393224 | tf_op jit(solution)/shard_map/ppermute | solution.py:299
  22.2 8.5 %copy-start.5 = (bf16[128,512]{1,0:T(8,128)(2,1)}, bf16[128,512]{1,0:T(8,128)(2,1)S(1)}, u32[]{:S(2)}) copy-start(bf16[128,512]{1,0:T(8,128)(2,1)S(1)} %collective-permute-done.1.refs_2_) | copy-start | bytes 393220
  22.2 7.6 %collective-permute-start.6 = (bf16[128,512]{1,0:T(8,128)(2,1)S(1)}, bf16[128,512]{1,0:T(8,128)(2,1)S(1)}, u32[]{:S(2)}, u32[]{:S(2)}) collective-permute-start(bf16[128,512]{1,0:T(8,128)(2,1)S(1)} %collective-permute-done.2.refs_3_), channel_id=1, source_target_pairs={{0,4},{1,5},{2,6},{3,7},{4,8},{5,9},{6,10},{7,11},{8,12},{9,13},{1... | collective-permute-start | bytes 393224 | tf_op jit(solution)/shard_map/ppermute | solution.py:300
  22.3 8.5 %copy-start.6 = (bf16[128,512]{1,0:T(8,128)(2,1)}, bf16[128,512]{1,0:T(8,128)(2,1)S(1)}, u32[]{:S(2)}) copy-start(bf16[128,512]{1,0:T(8,128)(2,1)S(1)} %collective-permute-done.refs_1_) | copy-start | bytes 393220
  22.3 8.4 %collective-permute-start.4 = (bf16[128,512]{1,0:T(8,128)(2,1)S(1)}, bf16[128,512]{1,0:T(8,128)(2,1)S(1)}, u32[]{:S(2)}, u32[]{:S(2)}) collective-permute-start(bf16[128,512]{1,0:T(8,128)(2,1)S(1)} %collective-permute-done.2.refs_3_), channel_id=1, source_target_pairs={{0,2},{1,3},{2,4},{3,5},{4,6},{5,7},{6,8},{7,9},{8,10},{9,11},{10,... | collective-permute-start | bytes 393224 | tf_op jit(solution)/shard_map/ppermute | solution.py:298
  28.0 2.8 %copy-start.7 = (bf16[128,512]{1,0:T(8,128)(2,1)}, bf16[128,512]{1,0:T(8,128)(2,1)S(1)}, u32[]{:S(2)}) copy-start(bf16[128,512]{1,0:T(8,128)(2,1)S(1)} %collective-permute-done.5.refs_6_) | copy-start | bytes 393220
  29.8 0.9 %copy-start.8 = (bf16[128,512]{1,0:T(8,128)(2,1)}, bf16[128,512]{1,0:T(8,128)(2,1)S(1)}, u32[]{:S(2)}) copy-start(bf16[128,512]{1,0:T(8,128)(2,1)S(1)} %collective-permute-done.6.refs_7_) | copy-start | bytes 393220
  30.7 0.7 copy-start.9
  30.7 0.7 %copy-start.2 = (f32[136,512]{1,0:T(8,128)}, f32[136,512]{1,0:T(8,128)S(1)}, u32[]{:S(2)}) copy-start(f32[136,512]{1,0:T(8,128)S(1)} %collective-permute-done.8.refs_11_) | copy-start | bytes 835588
  30.7 0.9 %copy-start.1 = (bf16[512,512]{1,0:T(8,128)(2,1)}, bf16[512,512]{1,0:T(8,128)(2,1)S(1)}, u32[]{:S(2)}) copy-start(bf16[512,512]{1,0:T(8,128)(2,1)S(1)} %collective-permute-done.7.refs_9_) | copy-start | bytes 1572868
  38.1 31.3 %all-to-all-start = ((bf16[8,128,512]{2,1,0:T(8,128)(2,1)}), bf16[8,128,512]{2,1,0:T(8,128)(2,1)S(1)}, u32[]{:S(2)}, u32[]{:S(2)}) async-start(bf16[8,128,512]{2,1,0:T(8,128)(2,1)} %bitcast.7), calls=%async_computation | async-start | bytes 2097152 | tf_op jit(solution)/shard_map/all_to_all | solution.py:322
  43.6 1.9 %copy-start = (bf16[1040,1536]{1,0:T(8,128)(2,1)S(1)}, bf16[1040,1536]{1,0:T(8,128)(2,1)}, u32[]{:S(2)}) copy-start(bf16[1040,1536]{1,0:T(8,128)(2,1)} %get-tuple-element.22.low_ref) | copy-start | bytes 9584644
  46.8 2.2 %collective-permute-start.9 = (bf16[544,512]{1,0:T(8,128)(2,1)S(1)}, bf16[544,512]{1,0:T(8,128)(2,1)S(1)}, u32[]{:S(2)}, u32[]{:S(2)}) collective-permute-start(bf16[544,512]{1,0:T(8,128)(2,1)S(1)} %get-tuple-element.24), channel_id=1, source_target_pairs={{0,16},{16,0},{32,48},{48,32},{64,80},{80,64},{96,112},{112,96},{1... | collective-permute-start | bytes 1671176 | tf_op jit(solution)/shard_map/ppermute | solution.py:327
  49.1 7.2 %collective-permute-start.10 = (bf16[144,512]{1,0:T(8,128)(2,1)S(1)}, bf16[144,512]{1,0:T(8,128)(2,1)S(1)}, u32[]{:S(2)}, u32[]{:S(2)}) collective-permute-start(bf16[144,512]{1,0:T(8,128)(2,1)S(1)} %get-tuple-element.26), channel_id=1, source_target_pairs={{0,128},{2,130},{4,132},{6,134},{8,136},{10,138},{12,140},{14,142}... | collective-permute-start | bytes 442376 | tf_op jit(solution)/shard_map/ppermute | solution.py:331
  50.2 10.0 %collective-permute-start.11 = (bf16[144,512]{1,0:T(8,128)(2,1)S(1)}, bf16[144,512]{1,0:T(8,128)(2,1)S(1)}, u32[]{:S(2)}, u32[]{:S(2)}) collective-permute-start(bf16[144,512]{1,0:T(8,128)(2,1)S(1)} %get-tuple-element.27), channel_id=1, source_target_pairs={{0,1},{2,3},{4,5},{6,7},{8,9},{10,11},{12,13},{14,15},{16,17},{18,... | collective-permute-start | bytes 442376 | tf_op jit(solution)/shard_map/ppermute | solution.py:331
  53.2 7.0 %collective-permute-start.12 = (bf16[144,512]{1,0:T(8,128)(2,1)S(1)}, bf16[144,512]{1,0:T(8,128)(2,1)S(1)}, u32[]{:S(2)}, u32[]{:S(2)}) collective-permute-start(bf16[144,512]{1,0:T(8,128)(2,1)S(1)} %get-tuple-element.28), channel_id=1, source_target_pairs={{0,129},{2,131},{4,133},{6,135},{8,137},{10,139},{12,141},{14,143}... | collective-permute-start | bytes 442376 | tf_op jit(solution)/shard_map/ppermute | solution.py:331
  60.3 5.8 %collective-permute-start.13 = (bf16[48,512]{1,0:T(8,128)(2,1)S(1)}, bf16[48,512]{1,0:T(8,128)(2,1)S(1)}, u32[]{:S(2)}, u32[]{:S(2)}) collective-permute-start(bf16[48,512]{1,0:T(8,128)(2,1)S(1)} %get-tuple-element.30), channel_id=1, source_target_pairs={{0,32},{16,48},{32,64},{48,80},{64,96},{80,112},{96,0},{112,16},{1... | collective-permute-start | bytes 147464 | tf_op jit(solution)/shard_map/ppermute | solution.py:339
  61.9 5.6 %collective-permute-start.14 = (bf16[48,512]{1,0:T(8,128)(2,1)S(1)}, bf16[48,512]{1,0:T(8,128)(2,1)S(1)}, u32[]{:S(2)}, u32[]{:S(2)}) collective-permute-start(bf16[48,512]{1,0:T(8,128)(2,1)S(1)} %get-tuple-element.31), channel_id=1, source_target_pairs={{0,64},{16,80},{32,96},{48,112},{64,0},{80,16},{96,32},{112,48},{1... | collective-permute-start | bytes 147464 | tf_op jit(solution)/shard_map/ppermute | solution.py:339
  64.6 4.1 %collective-permute-start.15 = (bf16[48,512]{1,0:T(8,128)(2,1)S(1)}, bf16[48,512]{1,0:T(8,128)(2,1)S(1)}, u32[]{:S(2)}, u32[]{:S(2)}) collective-permute-start(bf16[48,512]{1,0:T(8,128)(2,1)S(1)} %get-tuple-element.32), channel_id=1, source_target_pairs={{0,96},{16,112},{32,0},{48,16},{64,32},{80,48},{96,64},{112,80},{1... | collective-permute-start | bytes 147464 | tf_op jit(solution)/shard_map/ppermute | solution.py:339
